TPU v7x, 256 devices: a whole 4x4x8 slice. The times are simulated.
256 devices in a mesh: patch: 8 (over x, core), chan: 32 (over y, z).
Axes of the slice: x: 4, y: 4, z: 8, core: 2. Of those that a mesh axis runs over, the one named last changes fastest.
Arguments:
- alpha: float32 [4096, 150], P(('patch', 'chan')), parts along dimension 0, may hold values from -0.6 to 0.6
- images: float32 [4096, 2, 128, 128], P(('patch', 'chan')), parts along dimension 0, may hold values from -6 to 6
- modes: float32 [150, 4096], replicated, may hold values from -4.8 to 4.8
- diversity: float32 [4096], replicated, may hold values from -6 to 6
- chan_of_frame: int32 [512, 1], P('chan'), may hold values from 0 to 31
Outputs:
- gradient: float32 [4096, 150], P(('patch', 'chan')), parts along dimension 0
- nb_objects: float32 [256, 2, 128, 128], P(('patch', 'chan')), parts along dimension 0
- wb_object: float32 [16, 128, 128], P('patch'), parts along dimension 0
There are 8 independent parts, one for each index of `patch`. A program takes and returns all parts, laid end to end along the dimension named above; an argument that names none is the same for every part. Nothing has to cross between parts.
Inputs may be any that keep to these rules, and one draw needn't show every extreme that they name: `chan_of_frame`: every channel is observed in at least one frame.
All inputs are finite; a program needn't handle non-finite values.
Results may differ from a plain program's by a relative error of at most 0.0003.
Values sent between devices are 32-bit elements; how exact they have to be, the bound alone decides.
No kernel may reach another device: no remote copies, remote signals or barrier semaphores. Data moves between devices by JAX's collectives and lax.ppermute only.
A program may use at most 128 MiB of HBM per device.

v0:
```python
import math

import jax
import jax.numpy as jnp
from jax import lax
from jax.sharding import PartitionSpec as P

PUP = 64
CH_DEV = 1


PRECISE = lax.Precision.HIGHEST
PRIOR_WEIGHT = 0.1


def dft_table(length, columns):
    row_index = jnp.arange(length, dtype=jnp.int32)[:, None]
    col_index = jnp.arange(columns, dtype=jnp.int32)[None, :]
    angles = (row_index * col_index % length).astype(jnp.float32) * (2.0 * math.pi / length)
    return (jnp.cos(angles), -jnp.sin(angles))


def aperture(width):
    coords = jnp.arange(width, dtype=jnp.float32) - (width - 1) / 2.0
    radius = coords[:, None] ** 2 + coords[None, :] ** 2
    return (radius <= (width / 2.0) ** 2).astype(jnp.float32)


def apply_left(matrix, block):
    return jnp.einsum("ux,fxy->fuy", matrix, block, precision=PRECISE)


def apply_right(block, matrix):
    return jnp.einsum("fxy,vy->fxv", block, matrix, precision=PRECISE)


def transform(table, real_part, imag_part):
    cosine, sine = table
    if imag_part is None:
        left_real = apply_left(cosine, real_part)
        left_imag = apply_left(sine, real_part)
    else:
        left_real = apply_left(cosine, real_part) - apply_left(sine, imag_part)
        left_imag = apply_left(cosine, imag_part) + apply_left(sine, real_part)
    out_real = apply_right(left_real, cosine) - apply_right(left_imag, sine)
    out_imag = apply_right(left_imag, cosine) + apply_right(left_real, sine)
    return (out_real, out_imag)


def frame_terms(data_pair, spec_pair):
    data_real, data_imag = data_pair
    spec_real, spec_imag = spec_pair
    return jnp.stack(
        [
            data_real * spec_real + data_imag * spec_imag,
            data_imag * spec_real - data_real * spec_imag,
            spec_real * spec_real + spec_imag * spec_imag,
        ],
        axis=1,
    )


def estimate(sums):
    return sums[..., 0:2, :, :] / (PRIOR_WEIGHT + sums[..., 2:3, :, :])


def cotangent(data_pair, obj_real, obj_imag, spec_pair, factor):
    rest_real = data_pair[0] - (obj_real * spec_pair[0] - obj_imag * spec_pair[1])
    rest_imag = data_pair[1] - (obj_real * spec_pair[1] + obj_imag * spec_pair[0])
    return (
        -factor * (rest_real * obj_real + rest_imag * obj_imag),
        factor * (rest_real * obj_imag - rest_imag * obj_real),
    )


def shards(alpha, images, modes, diversity, chan_of_frame):
    length = images.shape[-1]
    width = PUP
    full_table = dft_table(length, length)
    pupil_table = dft_table(length, width)
    pupil = aperture(width)
    nch = CH_DEV * lax.axis_size("chan")

    def forward(coeffs):
        phase = jnp.dot(coeffs, modes, precision=PRECISE).reshape(coeffs.shape[0], width, width)
        results = []
        for offset in (jnp.zeros((width, width), jnp.float32), diversity.reshape(width, width)):
            total = phase + offset
            field_real, field_imag = transform(
                pupil_table, pupil * jnp.cos(total), pupil * jnp.sin(total)
            )
            power = field_real * field_real + field_imag * field_imag
            power = power / jnp.sum(power, axis=(1, 2), keepdims=True)
            results.append(transform(full_table, power, None))
        return tuple(results)

    (wide_spec, narrow_spec), pullback = jax.vjp(forward, alpha)
    wide_real, wide_imag = transform(full_table, images[:, 0], None)
    narrow_real, narrow_imag = transform(full_table, images[:, 1], None)
    wide_data = (wide_real / length, wide_imag / length)
    narrow_data = (narrow_real / length, narrow_imag / length)
    wide_local = jnp.sum(frame_terms(wide_data, wide_spec), axis=0)
    onehot = (chan_of_frame[:, 0][None, :] == jnp.arange(nch, dtype=jnp.int32)[:, None]).astype(
        jnp.float32
    )
    grid_local = jnp.einsum(
        "kf,fcuv->kcuv", onehot, frame_terms(narrow_data, narrow_spec), precision=PRECISE
    )
    wide_sums = lax.psum(wide_local, "chan")
    own_sums = lax.psum_scatter(grid_local, "chan", scatter_dimension=0, tiled=True)
    wide_object = estimate(wide_sums)
    own_objects = estimate(own_sums)
    narrow_objects = lax.all_gather(own_objects, "chan", axis=0, tiled=True)
    frame_objects = jnp.einsum("kf,kcuv->fcuv", onehot, narrow_objects, precision=PRECISE)
    factor = 2.0 / (length * length)
    wide_cot = cotangent(wide_data, wide_object[0], wide_object[1], wide_spec, factor)
    narrow_cot = cotangent(
        narrow_data, frame_objects[:, 0], frame_objects[:, 1], narrow_spec, factor
    )
    (gradient,) = pullback((wide_cot, narrow_cot))
    return (gradient, own_objects, wide_object)


def solution(mesh):
    placed = (
        P(("patch", "chan"), None),
        P(("patch", "chan"), None, None, None),
        P(),
        P(),
        P("chan", None),
    )
    return jax.shard_map(
        shards,
        mesh=mesh,
        in_specs=placed,
        out_specs=(
            P(("patch", "chan"), None),
            P(("patch", "chan"), None, None, None),
            P("patch", None, None),
        ),
        check_vma=False,
    )
```

profile of v0, /device:TPU:2, one launch (start us, length us, event | category | flops | bytes accessed | tf_op | source)
XLA Modules:
  0.0 566.7 jit_solution(9865842252962421154)
XLA Ops:
  8.9 2.0 fusion.507
  12.4 2.3 fusion.59
  14.8 2.4 fusion.63
  17.1 3.5 convolution_bitcast_fusion.6
  20.6 2.3 convolution_bitcast_fusion.7
  22.9 2.4 fusion.35
  25.2 2.2 fusion.176
  27.4 2.3 fusion.36
  33.5 3.3 fusion.504
  36.7 2.5 copy.59
  39.3 2.6 convolution_bitcast_fusion.4
  47.1 1.9 fusion.126
  51.0 1.9 convolution_add_fusion.8
  54.2 2.2 convolution_subtract_fusion.2
  58.0 4.4 fusion.2
  62.4 6.3 %copy.65 = f32[32,3,128,128]{3,2,1,0:T(8,128)} copy(f32[32,3,128,128]{3,0,2,1:T(8,128)S(1)} %fusion.2) | data formatting | bytes 12582912 | tf_op jit(solution)/shard_map/kf,fcuv->kcuv/dot_general | solution.py:106
  68.8 2.3 fusion.506
  81.0 3.2 fusion.503
  84.2 2.5 copy.76
  86.7 2.6 convolution_bitcast_fusion.3
  89.3 2.7 convolution_bitcast_fusion.2
  102.1 2.4 convolution_add_fusion.3
  104.4 1.9 convolution_subtract_fusion
  109.6 186.8 %reduce-scatter.2.cloned.1.call-done = f32[1,3,128,128]{3,2,1,0:T(8,128)} async-done(((f32[32,3,128,128]{3,2,1,0:T(8,128)}), f32[1,3,128,128]{3,2,1,0:T(8,128)}) %reduce-scatter.2.cloned.1.call-update) | async-done | bytes 196624 | tf_op jit(solution)/shard_map/reduce_scatter | solution.py:110
  299.3 141.7 %all-reduce.2.cloned.1.call-done = f32[3,128,128]{2,1,0:T(8,128)} async-done(((f32[3,128,128]{2,1,0:T(8,128)}), f32[3,128,128]{2,1,0:T(8,128)}) %all-reduce.2.cloned.1.call-update) | async-done | bytes 196624 | tf_op jit(solution)/shard_map/psum | solution.py:109
  443.5 2.5 subtract_subtract_fusion
  462.0 2.4 fusion.12
  464.4 59.1 %all-gather.2.cloned.1.call-done = f32[32,2,128,128]{3,2,1,0:T(8,128)} async-done(((f32[1,2,128,128]{3,2,1,0:T(8,128)}), f32[32,2,128,128]{3,2,1,0:T(8,128)}) %all-gather.2.cloned.1.call-update) | async-done | bytes 4194320 | tf_op jit(solution)/shard_map/all_gather | solution.py:113
  523.5 6.0 %fusion = f32[16,2,128,128]{3,0,2,1:T(8,128)S(1)} fusion(f32[32,2,128,128]{3,2,1,0:T(8,128)} %all-gather.2.cloned.1.call-done, s32[16]{0:T(128)S(1)} %bitcast.343), kind=kOutput, calls=%fused_computation | convolution fusion | flops 201327104 | bytes 6291520 | tf_op jit(solution)/shard_map/kf,kcuv->fcuv/dot_general | solution.py:114
  548.6 2.5 fusion.34
  551.1 2.3 fusion.31
  557.1 2.6 fusion.508
  (157 shorter events, 83.5 us)
Async XLA Ops:
  7.2 4.1 copy-start.37
  7.2 289.2 %reduce-scatter.2.cloned.1.call-start = ((), (), s32[]{:S(2)}) async-start(), calls=%async_computation.1 | async-start | bytes 6488064 | tf_op jit(solution)/shard_map/reduce_scatter | solution.py:110
  11.5 15.9 %copy-start.30 = (f32[64,64]{0,1:T(8,128)}, f32[64,64]{0,1:T(8,128)S(1)}, u32[]{:S(2)}) copy-start(f32[64,64]{0,1:T(8,128)S(1)} %copy.56) | copy-start | bytes 49156
  11.5 9.1 %copy-start.19 = (f32[16,2,128,128]{3,2,1,0:T(8,128)S(1)}, f32[16,2,128,128]{3,2,1,0:T(8,128)}, u32[]{:S(2)}) copy-start(f32[16,2,128,128]{3,2,1,0:T(8,128)} %param.6) | copy-start | bytes 6291460
  12.4 15.0 %copy-start.20 = (f32[64,64]{0,1:T(8,128)}, f32[64,64]{0,1:T(8,128)S(1)}, u32[]{:S(2)}) copy-start(f32[64,64]{0,1:T(8,128)S(1)} %fusion.204) | copy-start | bytes 49156
  33.4 3.3 copy-start.23
  39.3 2.6 copy-start.35
  39.3 4.0 copy-start.7
  41.9 2.7 copy-start.8
  47.1 9.3 %copy-start.9 = (f32[16,128,128]{2,1,0:T(8,128)}, f32[16,128,128]{2,1,0:T(8,128)S(1)}, u32[]{:S(2)}) copy-start(f32[16,128,128]{2,1,0:T(8,128)S(1)} %fusion.10) | copy-start | bytes 3145732
  52.9 3.5 copy-start.11
  54.2 2.9 copy-start.13
  68.7 372.3 %all-reduce.2.cloned.1.call-start = ((), (), s32[]{:S(2)}) async-start(), calls=%async_computation.3 | async-start | bytes 393216 | tf_op jit(solution)/shard_map/psum | solution.py:109
  68.8 5.2 copy-start.21
  71.1 6.2 %copy-start.17 = (f32[16,64,64]{1,2,0:T(8,128)}, f32[16,64,64]{1,2,0:T(8,128)S(1)}, u32[]{:S(2)}) copy-start(f32[16,64,64]{1,2,0:T(8,128)S(1)} %get-tuple-element.26) | copy-start | bytes 786436
  81.0 3.2 copy-start.25
  86.7 6.5 %copy-start.34 = (f32[16,128,128]{1,2,0:T(8,128)S(1)}, f32[16,128,128]{1,2,0:T(8,128)}, u32[]{:S(2)}) copy-start(f32[16,128,128]{1,2,0:T(8,128)} %copy.76) | copy-start | bytes 3145732
  102.0 5.6 copy-start.1
  104.4 3.3 copy-start.2
  106.4 2.0 copy-start.3
  109.5 414.0 %all-gather.2.cloned.1.call-start = ((), (), s32[]{:S(2)}) async-start(), calls=%async_computation.2 | async-start | bytes 4325376 | tf_op jit(solution)/shard_map/all_gather | solution.py:113
  449.9 2.5 copy-start.6
  449.9 2.5 copy-start.39
  529.6 2.1 copy-start.16
  536.4 2.8 copy-start.5
  537.9 2.8 copy-start.32
  545.5 3.0 copy-start.22
  545.5 3.0 copy-start.31
  548.5 4.9 copy-start.18
  548.6 4.9 copy-start.28
  548.6 4.9 copy-start.29
  551.1 3.1 copy-start.27
  (11 other events, 14.3 us)
Sparse Core Ops, SparseCore 0:
  68.9 227.4 reduce-scatter.1
  300.2 140.8 all-reduce.1
  444.2 79.2 all-gather.1
where the time goes:
time: 576 us; the launch traced here: 567 us
  waiting for transfers between devices  388 us (67%)
  matrix products  131 us (23%)
  local copies, waits for them, and re-layouts  20.5 us (4%)
  between operations  15.2 us (3%)
  other arithmetic  12.1 us (2%)
    reduce_scatter x1, waiting for transfers between devices, shards(): lax.psum_scatter(grid_local, 'chan', scatter_dimension=0, tiled=True)  187 us
    psum x1, waiting for transfers between devices, shards(): wide_sums = lax.psum(wide_local, 'chan')  142 us
    dot_general x40, matrix products, apply_right(): return jnp.einsum('fxy,vy->fxv', block, matrix, precision=PRECISE)  67.3 us
    all_gather x1, waiting for transfers between devices, shards(): narrow_objects = lax.all_gather(own_objects, 'chan', axis=0, tiled=True)  59.1 us
    dot_general x28, matrix products, apply_left(): return jnp.einsum('ux,fxy->fuy', matrix, block, precision=PRECISE)  48.7 us
  transfers between devices with their start and end apart: 3, of which 3 were waited for; matrix products, arithmetic and copies ran while one was open for 12% of the time, Pallas kernels for 0%

commit v1 on v0

v1 whole, which is shorter than its diff:
```python
import functools
import math

import jax
import jax.numpy as jnp
import numpy as np
from jax import lax
from jax.experimental import pallas as pl
from jax.experimental.pallas import tpu as pltpu
from jax.sharding import PartitionSpec as P

PUP = 64
SIZE = 128
HALF = SIZE // 2 + 1
ROWS = 72
NY, NZ = 4, 8
GROUP = 64 // NY
OWN = 32 // NZ
FRAMES = 16
STEP = 4
PRIOR_WEIGHT = 0.1
F32 = jnp.float32
BF16 = jnp.bfloat16
VMEM_LIMIT = 56 * 1024 * 1024
Y_ROWS = FRAMES * 3 * GROUP + FRAMES * 3
W_ROWS = 56
Z_ROWS = 216
F_ROWS = 144
R_ROWS = (FRAMES + 2) * 2 * GROUP


def dft(length, columns):
    angle = np.outer(np.arange(length), np.arange(columns)) % SIZE * (2.0 * math.pi / SIZE)
    return np.cos(angle), -np.sin(angle)


def halves(table):
    table = np.asarray(table, np.float32)
    high = table.astype(jnp.bfloat16)
    low = (table - high.astype(np.float32)).astype(jnp.bfloat16)
    return high, low


def left_short(table):
    high, low = halves(table)
    return [np.concatenate([high, high], 1), low]


def right_short(table):
    high, low = halves(table)
    return [np.concatenate([high, high], 0), low]


def make_tables():
    c, s = dft(SIZE, SIZE)
    cp, sp = dft(SIZE, PUP)
    ch, sh = np.zeros((ROWS, SIZE)), np.zeros((ROWS, SIZE))
    ch[:HALF], sh[:HALF] = c[:HALF], s[:HALF]
    weight = np.zeros((ROWS, 1))
    weight[:HALF] = 2.0
    weight[0] = weight[HALF - 1] = 1.0
    forward = (
        right_short(np.block([[cp.T, sp.T], [-sp.T, cp.T]]))
        + left_short(np.block([[cp, -sp], [sp, cp]]))
        + left_short(np.concatenate([ch, sh], 0))
        + list(halves(np.block([[c.T, s.T], [-s.T, c.T]])))
    )
    backward = (
        list(halves(np.block([[c, -s], [s, c]])))
        + list(halves(np.concatenate([(weight * ch).T, (weight * sh).T], 1)))
        + list(halves(np.block([[cp.T, sp.T], [-sp.T, cp.T]])))
        + list(halves(np.block([[cp, -sp], [sp, cp]])))
    )
    return forward, backward


def mm(a, b):
    return jnp.dot(a, b, preferred_element_type=F32)


def cut(x):
    high = x.astype(BF16)
    return high, (x - high.astype(F32)).astype(BF16)


def right_mul_short(x, twice, low):
    h, r = cut(x)
    return mm(jnp.concatenate([h, r], 1), twice[...]) + mm(h, low[...])


def left_mul_short(twice, low, x):
    h, r = cut(x)
    return mm(twice[...], jnp.concatenate([h, r], 0)) + mm(low[...], h)


def right_mul(x, high, low):
    h, r = cut(x)
    return mm(h, high[...]) + (mm(r, high[...]) + mm(h, low[...]))


def left_mul(high, low, x):
    h, r = cut(x)
    return mm(high[...], h) + (mm(high[...], r) + mm(low[...], h))


def pair_spectra(blocks, left, right):
    out = []
    for a, b in zip(blocks[::2], blocks[1::2], strict=True):
        t = left_mul_short(*left, jnp.concatenate([a, b], 1))
        for k in range(2):
            lanes = slice(k * SIZE, (k + 1) * SIZE)
            out.append(jnp.concatenate([t[:ROWS, lanes], t[ROWS:, lanes]], 1))
    full = right_mul(jnp.concatenate(out, 0), *right)
    return [full[k * ROWS : (k + 1) * ROWS] for k in range(len(blocks))]


def forward_kernel(wide, place, q_ref, im_ref, r1, r2, l1, l2, h1, h2, f1, f2, *rest):
    s_ref, d_ref, g_ref = rest[:3]
    outs, scr = rest[3 : 3 + NY], rest[3 + NY]
    step = pl.program_id(0)
    y = place[0]
    t = right_mul_short(q_ref[...].reshape(STEP * PUP, 2 * PUP), r1, r2)
    powers = []
    for a in range(0, STEP, 2):
        cols = []
        for k in (a, a + 1):
            tk = t[k * PUP : (k + 1) * PUP]
            cols.append(jnp.concatenate([tk[:, :SIZE], tk[:, SIZE:]], 0))
        g = left_mul_short(l1, l2, jnp.concatenate(cols, 1))
        for k in (a, a + 1):
            lanes = slice((k - a) * SIZE, (k - a + 1) * SIZE)
            gr, gi = g[:SIZE, lanes], g[SIZE:, lanes]
            g_ref[k, 0], g_ref[k, 1] = gr, gi
            power = gr * gr + gi * gi
            powers.append(power / jnp.sum(power, keepdims=True))
    images = [im_ref[k, 0] for k in range(STEP)]
    spectra = pair_spectra(powers + images, (h1, h2), (f1, f2))

    if wide:

        @pl.when(step == 0)
        def _():
            scr[...] = jnp.zeros_like(scr)

    for k in range(STEP):
        sk, dk = spectra[k], spectra[STEP + k] * (1.0 / SIZE)
        s_ref[k], d_ref[k] = sk, dk
        sr, si, dr, di = sk[:, :SIZE], sk[:, SIZE:], dk[:, :SIZE], dk[:, SIZE:]
        terms = (dr * sr + di * si, di * sr - dr * si, sr * sr + si * si)
        for c in range(3):
            if wide:
                scr[c] += terms[c]
            else:
                scr[c] = terms[c]
        if not wide:
            frame = step * STEP + k
            for shift in range(NY):
                row = pl.multiple_of(GROUP * lax.rem(y + shift, NY), GROUP)
                for c in range(3):
                    at = pl.multiple_of(frame * 3 * GROUP + c * GROUP, GROUP)
                    outs[shift][pl.ds(at, GROUP), :] = scr[c, pl.ds(row, GROUP), :]
                    outs[shift][pl.ds(FRAMES * 3 * GROUP + 3 * frame + c, 1), :] = scr[c, 64:65, :]

    if wide:

        @pl.when(step == FRAMES // STEP - 1)
        def _():
            for shift in range(NY):
                row = pl.multiple_of(GROUP * lax.rem(y + shift, NY), GROUP)
                for c in range(3):
                    outs[shift][c * GROUP : (c + 1) * GROUP, :] = scr[c, pl.ds(row, GROUP), :]
                    outs[shift][3 * GROUP + c : 3 * GROUP + c + 1, :] = scr[c, 64:65, :]
                outs[shift][3 * GROUP + 3 :, :] = jnp.zeros((W_ROWS - 3 * GROUP - 3, SIZE), F32)


def smem():
    return pl.BlockSpec(memory_space=pltpu.SMEM)


def whole(a):
    return pl.BlockSpec(a.shape, lambda i: (0,) * a.ndim)


def shape(*dims):
    return jax.ShapeDtypeStruct(dims, F32)


def forward(wide, place, q, images, tables):
    camera = 0 if wide else 1
    rows = W_ROWS if wide else Y_ROWS
    outs = [shape(FRAMES, ROWS, 2 * SIZE)] * 2 + [shape(FRAMES, 2, SIZE, SIZE)] + [shape(rows, SIZE)] * NY
    return pl.pallas_call(
        functools.partial(forward_kernel, wide),
        grid=(FRAMES // STEP,),
        in_specs=[
            smem(),
            pl.BlockSpec((STEP, PUP, 2 * PUP), lambda i: (i, 0, 0)),
            pl.BlockSpec((STEP, 1, SIZE, SIZE), lambda i: (i, camera, 0, 0)),
        ]
        + [whole(t) for t in tables],
        out_specs=[pl.BlockSpec((STEP, ROWS, 2 * SIZE), lambda i: (i, 0, 0))] * 2
        + [pl.BlockSpec((STEP, 2, SIZE, SIZE), lambda i: (i, 0, 0, 0))]
        + [pl.BlockSpec((rows, SIZE), lambda i: (0, 0))] * NY,
        out_shape=outs,
        scratch_shapes=[pltpu.VMEM((3, ROWS, SIZE), F32)],
        compiler_params=pltpu.CompilerParams(vmem_limit_bytes=VMEM_LIMIT),
        cost_estimate=pl.CostEstimate(flops=20_000_000_000, bytes_accessed=8_000_000, transcendentals=0),
        name="forward_wide" if wide else "forward_narrow",
    )(place, q, images, *tables)


def sum_kernel(place, ids, *refs):
    narrow, wides = refs[:NY], refs[NY : 2 * NY]
    outs = refs[2 * NY : 2 * NY + NZ]
    acc, edge, total = refs[2 * NY + NZ :]
    z = place[1]
    acc[...] = jnp.zeros_like(acc)
    edge[...] = jnp.zeros_like(edge)
    total[...] = (wides[0][...] + wides[1][...]) + (wides[2][...] + wides[3][...])
    for shift in range(NY):
        source = (NY - shift) % NY
        for f in range(FRAMES):
            k = ids[source * FRAMES + f]
            acc[k] += narrow[shift][f * 3 * GROUP : (f + 1) * 3 * GROUP, :]
            at = FRAMES * 3 * GROUP + 3 * f
            edge[k, 0:3, :] += narrow[shift][at : at + 3, :]
    for shift in range(NZ):
        to = lax.rem(z + shift, NZ)
        out = outs[shift]
        for k in range(OWN):
            out[k * 3 * GROUP : (k + 1) * 3 * GROUP, :] = acc[OWN * to + k]
            at = OWN * 3 * GROUP + 3 * k
            out[at : at + 3, :] = edge[OWN * to + k, 0:3, :]
        at = OWN * (3 * GROUP + 3)
        for c in range(3):
            for j in range(2):
                out[at + 2 * c + j : at + 2 * c + j + 1, :] = total[pl.ds(c * GROUP + 2 * to + j, 1), :]
        out[at + 6 : at + 9, :] = total[3 * GROUP : 3 * GROUP + 3, :]
        out[at + 9 :, :] = jnp.zeros((Z_ROWS - at - 9, SIZE), F32)


def quotient(num_re, num_im, den):
    den = PRIOR_WEIGHT + den
    return num_re / den, num_im / den


def object_kernel(*refs):
    parts, out = refs[:NZ], refs[NZ]
    sums = parts[0][...]
    for part in parts[1:]:
        sums = sums + part[...]
    for k in range(OWN):
        base = k * 3 * GROUP
        re, im = quotient(*(sums[base + c * GROUP : base + (c + 1) * GROUP] for c in range(3)))
        out[k * 2 * GROUP : k * 2 * GROUP + GROUP, :] = re
        out[k * 2 * GROUP + GROUP : (k + 1) * 2 * GROUP, :] = im
        base = OWN * 3 * GROUP + 3 * k
        re, im = quotient(*(sums[base + c : base + c + 1] for c in range(3)))
        at = OWN * 2 * GROUP + 2 * k
        out[at : at + 1, :] = re
        out[at + 1 : at + 2, :] = im
    base = OWN * (3 * GROUP + 3)
    at = OWN * (2 * GROUP + 2)
    re, im = quotient(*(sums[base + 2 * c : base + 2 * c + 2] for c in range(3)))
    out[at : at + 2, :] = re
    out[at + 2 : at + 4, :] = im
    re, im = quotient(*(sums[base + 6 + c : base + 7 + c] for c in range(3)))
    out[at + 4 : at + 5, :] = re
    out[at + 5 : at + 6, :] = im
    out[at + 6 :, :] = jnp.zeros((F_ROWS - at - 6, SIZE), F32)


def select_kernel(place, ids, *refs):
    parts, outs = refs[:NZ], refs[NZ : NZ + NY]
    near, objects, edge, total = refs[NZ + NY :]
    y, z = place[0], place[1]
    for shift in range(NZ):
        source = lax.rem(z + NZ - shift, NZ)
        part = parts[shift]
        for k in range(OWN):
            objects[OWN * source + k] = part[k * 2 * GROUP : (k + 1) * 2 * GROUP, :]
            at = OWN * 2 * GROUP + 2 * k
            edge[OWN * source + k, 0:2, :] = part[at : at + 2, :]
        at = OWN * (2 * GROUP + 2)
        for j in range(2):
            total[pl.ds(2 * source + j, 1), :] = part[at + j : at + j + 1, :]
            total[pl.ds(GROUP + 2 * source + j, 1), :] = part[at + 2 + j : at + 3 + j, :]
    at = OWN * (2 * GROUP + 2) + 4
    for shift in range(NY):
        out = outs[shift]
        for f in range(FRAMES):
            out[f * 2 * GROUP : (f + 1) * 2 * GROUP, :] = objects[ids[shift * FRAMES + f]]
        own = lax.rem(y + shift, NY) * NZ + z
        out[FRAMES * 2 * GROUP : (FRAMES + 1) * 2 * GROUP, :] = objects[own]
        out[(FRAMES + 1) * 2 * GROUP :, :] = total[...]
    for f in range(FRAMES):
        near[2 * f : 2 * f + 2, :] = edge[ids[f], 0:2, :]
    near[2 * FRAMES : 2 * FRAMES + 2, :] = edge[y * NZ + z, 0:2, :]
    near[2 * FRAMES + 2 : 2 * FRAMES + 4, :] = parts[0][at : at + 2, :]
    near[2 * FRAMES + 4 :, :] = jnp.zeros((4, SIZE), F32)


def plain(kernel, name, smems, arrays, outs, scratch):
    return pl.pallas_call(
        kernel,
        in_specs=[smem()] * len(smems) + [pl.BlockSpec(memory_space=pltpu.VMEM)] * len(arrays),
        out_specs=[pl.BlockSpec(memory_space=pltpu.VMEM)] * len(outs),
        out_shape=outs,
        scratch_shapes=scratch,
        compiler_params=pltpu.CompilerParams(vmem_limit_bytes=VMEM_LIMIT),
        name=name,
    )(*smems, *arrays)


def backward_kernel(wide, place, q_ref, s_ref, d_ref, g_ref, *refs):
    parts, refs = refs[:NY], refs[NY:]
    own, refs = (refs[:NY], refs[NY:]) if not wide else (None, refs)
    near, a1, a2, b1, b2, e1, e2, f1, f2, out, obj, scr = refs
    step = pl.program_id(0)
    y = place[0]

    def gather(sources, at):
        for shift in range(NY):
            row = pl.multiple_of(GROUP * lax.rem(y + NY - shift, NY), GROUP)
            for c in range(2):
                scr[c, pl.ds(row, GROUP), :] = sources[shift][at + c * GROUP : at + (c + 1) * GROUP, :]

    @pl.when(step == 0)
    def _():
        scr[...] = jnp.zeros_like(scr)
        gather(parts if wide else own, 0)
        at = 2 * FRAMES + (2 if wide else 0)
        for c in range(2):
            scr[c, 64:65, :] = near[at + c : at + c + 1, :]
        obj[...] = scr[...]

    cots = []
    for k in range(STEP):
        if not wide:
            gather(parts, k * 2 * GROUP)
            for c in range(2):
                scr[c, 64:65, :] = near[pl.ds(2 * (step * STEP + k) + c, 1), :]
        fr, fi = scr[0], scr[1]
        sk, dk = s_ref[k], d_ref[k]
        sr, si, dr, di = sk[:, :SIZE], sk[:, SIZE:], dk[:, :SIZE], dk[:, SIZE:]
        rest_r = dr - (fr * sr - fi * si)
        rest_i = di - (fr * si + fi * sr)
        cots.append(jnp.concatenate([-(rest_r * fr + rest_i * fi), rest_r * fi - rest_i * fr], 1))
    t = right_mul(jnp.concatenate(cots, 0), a1, a2)
    steps = []
    for a in range(0, STEP, 2):
        cols = []
        for k in (a, a + 1):
            tk = t[k * ROWS : (k + 1) * ROWS]
            cols.append(jnp.concatenate([tk[:, :SIZE], tk[:, SIZE:]], 0))
        dp = left_mul(b1, b2, jnp.concatenate(cols, 1))
        fields = []
        for k in (a, a + 1):
            gr, gi = g_ref[k, 0], g_ref[k, 1]
            power = gr * gr + gi * gi
            scale = 1.0 / jnp.sum(power, keepdims=True)
            dk = dp[:, (k - a) * SIZE : (k - a + 1) * SIZE]
            mean = jnp.sum(dk * power, keepdims=True) * scale
            dk = (dk - mean) * (scale * (4.0 / (SIZE * SIZE)))
            fields.append(jnp.concatenate([gr * dk, gi * dk], 0))
        h = left_mul(e1, e2, jnp.concatenate(fields, 1))
        for k in (a, a + 1):
            lanes = slice((k - a) * SIZE, (k - a + 1) * SIZE)
            steps.append(jnp.concatenate([h[:PUP, lanes], h[PUP:, lanes]], 1))
    dq = right_mul(jnp.concatenate(steps, 0), f1, f2)
    q = q_ref[...].reshape(STEP * PUP, 2 * PUP)
    dphase = q[:, :PUP] * dq[:, PUP:] - q[:, PUP:] * dq[:, :PUP]
    out[...] = dphase.reshape(STEP, PUP, PUP)


def backward(wide, place, q, s, d, g, parts, near, tables):
    item = FRAMES + 1 if wide else FRAMES
    block = 2 * GROUP
    if wide:
        sources, specs = list(parts), [pl.BlockSpec((block, SIZE), lambda i: (item, 0))] * NY
    else:
        sources = list(parts) * 2
        specs = [pl.BlockSpec((STEP * block, SIZE), lambda i: (i, 0))] * NY
        specs += [pl.BlockSpec((block, SIZE), lambda i: (item, 0))] * NY
    return pl.pallas_call(
        functools.partial(backward_kernel, wide),
        grid=(FRAMES // STEP,),
        in_specs=[
            smem(),
            pl.BlockSpec((STEP, PUP, 2 * PUP), lambda i: (i, 0, 0)),
            pl.BlockSpec((STEP, ROWS, 2 * SIZE), lambda i: (i, 0, 0)),
            pl.BlockSpec((STEP, ROWS, 2 * SIZE), lambda i: (i, 0, 0)),
            pl.BlockSpec((STEP, 2, SIZE, SIZE), lambda i: (i, 0, 0, 0)),
        ]
        + specs
        + [whole(near)]
        + [whole(t) for t in tables],
        out_specs=[
            pl.BlockSpec((STEP, PUP, PUP), lambda i: (i, 0, 0)),
            pl.BlockSpec((2, ROWS, SIZE), lambda i: (0, 0, 0)),
        ],
        out_shape=[shape(FRAMES, PUP, PUP), shape(2, ROWS, SIZE)],
        scratch_shapes=[pltpu.VMEM((2, ROWS, SIZE), F32)],
        compiler_params=pltpu.CompilerParams(vmem_limit_bytes=VMEM_LIMIT),
        cost_estimate=pl.CostEstimate(flops=20_000_000_000, bytes_accessed=8_000_000, transcendentals=0),
        name="backward_wide" if wide else "backward_narrow",
    )(place, q, s, d, g, *sources, near, *tables)


def mirrored(half):
    high = jnp.roll(jnp.flip(half[:, 1 : HALF - 1], (1, 2)), 1, 2)
    return jnp.concatenate([half[:, :HALF], high * jnp.array([1.0, -1.0], F32)[:, None, None]], 1)


def along(axis, shift):
    pairs = []
    for y in range(NY):
        for z in range(NZ):
            to = ((y + shift) % NY, z) if axis == "y" else (y, (z + shift) % NZ)
            pairs.append((y * NZ + z, to[0] * NZ + to[1]))
    return pairs


def send(x, axis, shift):
    return lax.ppermute(x, "chan", along(axis, shift))


def shards(alpha, images, modes, diversity, chan_of_frame):
    tables_f, tables_b = ([jnp.asarray(t) for t in group] for group in make_tables())
    here = lax.axis_index("chan")
    place = jnp.stack([here // NZ, here % NZ]).astype(jnp.int32)
    own_ids = chan_of_frame[:, 0]
    ids = jnp.concatenate([own_ids] + [send(own_ids, "y", -shift) for shift in range(1, NY)])

    phase = jnp.dot(alpha, modes, precision=lax.Precision.HIGHEST)
    axis = np.arange(PUP, dtype=np.float32) - (PUP - 1) / 2.0
    pupil = (axis[:, None] ** 2 + axis[None, :] ** 2 <= (PUP / 2.0) ** 2).astype(np.float32)

    def field(total):
        parts = [(jnp.asarray(pupil.reshape(-1)) * f(total)).reshape(FRAMES, PUP, PUP) for f in (jnp.cos, jnp.sin)]
        return jnp.concatenate(parts, 2)

    q_narrow = field(phase + diversity)
    q_wide = field(phase)

    narrow_s, narrow_d, narrow_g, *narrow_out = forward(False, place, q_narrow, images, tables_f)
    narrow_in = [narrow_out[0]] + [send(narrow_out[k], "y", k) for k in range(1, NY)]
    wide_s, wide_d, wide_g, *wide_out = forward(True, place, q_wide, images, tables_f)
    wide_in = [wide_out[0]] + [send(wide_out[k], "y", k) for k in range(1, NY)]

    sums = plain(
        sum_kernel,
        "sum_channels",
        [place, ids],
        narrow_in + wide_in,
        [shape(Z_ROWS, SIZE)] * NZ,
        [pltpu.VMEM((32, 3 * GROUP, SIZE), F32), pltpu.VMEM((32, 8, SIZE), F32), pltpu.VMEM((W_ROWS, SIZE), F32)],
    )
    sums = [sums[0]] + [send(sums[k], "z", k) for k in range(1, NZ)]
    (own,) = plain(object_kernel, "objects", [], sums, [shape(F_ROWS, SIZE)], [])
    every = [own] + [send(own, "z", k) for k in range(1, NZ)]
    *back, near = plain(
        select_kernel,
        "select_objects",
        [place, ids],
        every,
        [shape(R_ROWS, SIZE)] * NY + [shape(2 * FRAMES + 8, SIZE)],
        [pltpu.VMEM((32, 2 * GROUP, SIZE), F32), pltpu.VMEM((32, 8, SIZE), F32), pltpu.VMEM((2 * GROUP, SIZE), F32)],
    )
    back = [back[0]] + [send(back[k], "y", k) for k in range(1, NY)]

    wide_dphase, wide_half = backward(True, place, q_wide, wide_s, wide_d, wide_g, back, near, tables_b)
    narrow_dphase, narrow_half = backward(False, place, q_narrow, narrow_s, narrow_d, narrow_g, back, near, tables_b)
    dphase = (wide_dphase + narrow_dphase).reshape(FRAMES, PUP * PUP)
    gradient = lax.dot_general(dphase, modes, (((1,), (1,)), ((), ())), precision=lax.Precision.HIGHEST)
    return gradient, mirrored(narrow_half)[None], mirrored(wide_half)


def solution(mesh):
    placed = (
        P(("patch", "chan"), None),
        P(("patch", "chan"), None, None, None),
        P(),
        P(),
        P("chan", None),
    )
    return jax.shard_map(
        shards,
        mesh=mesh,
        in_specs=placed,
        out_specs=(
            P(("patch", "chan"), None),
            P(("patch", "chan"), None, None, None),
            P("patch", None, None),
        ),
        check_vma=False,
    )
```

time: 576 us -> 165 us (0.29); the launches traced: 567 us -> 164 us
  waiting for transfers between devices: 388 us -> 48.9 us
  matrix products: 131 us -> 7.63 us
  starting transfers between devices: 0.12 us -> 45.3 us
  Pallas kernels: 0 us -> 43.2 us
  between operations: 15.2 us -> 0.96 us
  local copies, waits for them, and re-layouts: 20.5 us -> 12.7 us
  other arithmetic: 12.1 us -> 5.77 us
    reduce_scatter x1 -> x0, waiting for transfers between devices: 187 us -> none  [shards(): lax.psum_scatter(grid_local, 'chan', scatter_dimension=0, tiled=True)]
    psum x1 -> x0, waiting for transfers between devices: 142 us -> none  [shards(): wide_sums = lax.psum(wide_local, 'chan')]
    dot_general x72 -> x2, matrix products: 131 us -> 7.63 us  [the longest x1 4.98 us: shards(): phase = jnp.dot(alpha, modes, precision=lax.Precision.HIGHEST)]
    all_gather x1 -> x0, waiting for transfers between devices: 59.1 us -> none  [shards(): narrow_objects = lax.all_gather(own_objects, 'chan', axis=0, tiled=True)]
    ppermute x0 -> x26, waiting for transfers between devices: none -> 48.9 us  [send(): return lax.ppermute(x, 'chan', along(axis, shift))]
    ppermute x0 -> x26, starting transfers between devices: none -> 45.3 us  [send(): return lax.ppermute(x, 'chan', along(axis, shift))]
    pallas_call x0 -> x7, Pallas kernels: none -> 43.2 us  [the longest x2 19.5 us: backward(): pl.pallas_call(functools.partial(backward_kernel, wide), grid=(FRAMES //...]
    dot_general x1 -> x0, local copies, waits for them, and re-layouts: 6.28 us -> none  [shards(): jnp.einsum('kf,fcuv->kcuv', onehot, frame_terms(narrow_data, narrow_spec)...]
  transfers between devices with their start and end apart: 3 -> 26, of which waited for: 3 -> 16; matrix products, arithmetic and copies ran while one was open for 12% -> 2% of each run, Pallas kernels for 0% -> 5%
where the time goes in v1:
time: 165 us; the launch traced here: 164 us
  waiting for transfers between devices  48.9 us (30%)
  starting transfers between devices  45.3 us (27%)
  Pallas kernels  43.2 us (26%)
  local copies, waits for them, and re-layouts  12.7 us (8%)
  matrix products  7.63 us (5%)
  other arithmetic  5.77 us (3%)
    ppermute x26, waiting for transfers between devices, send(): return lax.ppermute(x, 'chan', along(axis, shift))  48.9 us
    ppermute x26, starting transfers between devices, send(): return lax.ppermute(x, 'chan', along(axis, shift))  45.3 us
    pallas_call x2, Pallas kernels, backward(): pl.pallas_call(functools.partial(backward_kernel, wide), grid=(FRAMES //...  19.5 us
    pallas_call x2, Pallas kernels, forward(): pl.pallas_call(functools.partial(forward_kernel, wide), grid=(FRAMES // S...  16.8 us
    pallas_call x3, Pallas kernels, plain(): pl.pallas_call(kernel, in_specs=[smem()] * len(smems) + [pl.BlockSpec(mem...  6.91 us
    slice x8, local copies, waits for them, and re-layouts, mirrored(): high = jnp.roll(jnp.flip(half[:, 1:HALF - 1], (1, 2)), 1, 2)  5.45 us
    dot_general x1, matrix products, shards(): phase = jnp.dot(alpha, modes, precision=lax.Precision.HIGHEST)  4.98 us
    unnamed x58, local copies, waits for them, and re-layouts  4.3 us
  transfers between devices with their start and end apart: 26, of which 16 were waited for; matrix products, arithmetic and copies ran while one was open for 2% of the time, Pallas kernels for 5%

profile of v1, /device:TPU:2, one launch (start us, length us, event | category | flops | bytes accessed | tf_op | source)
XLA Modules:
  0.0 164.4 jit_solution(543532626652276096)
XLA Ops:
  2.3 5.0 %cosine_multiply_fusion = (f32[16,4096]{1,0:T(8,128)S(1)}, f32[16,4096]{1,0:T(8,128)}, f32[16,4096]{1,0:T(8,128)}, f32[16,4096]{1,0:T(8,128)}) fusion(f32[4096]{0:T(1024)} %param.30, f32[4096]{0:T(1024)} %constant.76.clone, f32[16,150]{1,0:T(8,128)} %param.27, f32[150,4096]{1,0:T(8,128)S(1)} %copy-done), kind=kOutput, calls=%fused_computation.3 | convolution fusion | flops 118292480 | bytes 3548544 | tf_op jit(solution)/shard_map/dot_general | solution.py:435
  10.3 8.5 %forward_narrow.1 = (f32[16,72,256]{2,1,0:T(8,128)}, f32[16,72,256]{2,1,0:T(8,128)}, f32[16,2,128,128]{3,2,1,0:T(8,128)}, f32[816,128]{1,0:T(8,128)}, f32[816,12...) custom-call(s32[2]{0:T(128)} %pad_add_fusion.place, f32[16,64,128]{2,1,0:T(8,128)} %pad_maximum_fusion.1.q_ref, ...), custom_call_target="tpu_custom_call" | custom-call | flops 20000000000 | bytes 8000000 | tf_op jit(solution)/shard_map/forward_narrow/pallas_call | solution.py:192
  20.5 2.9 %collective-permute-start.4 = (f32[816,128]{1,0:T(8,128)}, f32[816,128]{1,0:T(8,128)}, u32[]{:S(2)}, u32[]{:S(2)}) collective-permute-start(f32[816,128]{1,0:T(8,128)} %get-tuple-element.39), channel_id=1, source_target_pairs={{0,16},{1,17},{2,18},{3,19},{4,20},{5,21},{6,22},{7,23},{8,24},{9,... | collective-permute-start | bytes 1253384 | tf_op jit(solution)/shard_map/ppermute | solution.py:425
  27.2 8.3 %forward_wide.1 = (f32[16,72,256]{2,1,0:T(8,128)}, f32[16,72,256]{2,1,0:T(8,128)}, f32[16,2,128,128]{3,2,1,0:T(8,128)}, f32[56,128]{1,0:T(8,128)}, f32[56,128]{1...) custom-call(s32[2]{0:T(128)} %pad_add_fusion.place, f32[16,64,128]{2,1,0:T(8,128)} %pad_maximum_fusion.q_ref, ...), custom_call_target="tpu_custom_call" | custom-call | flops 20000000000 | bytes 8000000 | tf_op jit(solution)/shard_map/forward_wide/pallas_call | solution.py:192
  36.3 6.3 %collective-permute-done.2 = s32[16]{0:T(128)S(1)} collective-permute-done((s32[16]{0:T(128)S(1)}, s32[16]{0:T(128)S(1)}, u32[]{:S(2)}, u32[]{:S(2)}) %collective-permute-start.2) | collective-permute-done | bytes 96 | tf_op jit(solution)/shard_map/ppermute | solution.py:425
  43.3 4.4 %collective-permute-done.1 = s32[16]{0:T(128)S(1)} collective-permute-done((s32[16]{0:T(128)S(1)}, s32[16]{0:T(128)S(1)}, u32[]{:S(2)}, u32[]{:S(2)}) %collective-permute-start.1) | collective-permute-done | bytes 96 | tf_op jit(solution)/shard_map/ppermute | solution.py:425
  48.3 2.9 %collective-permute-done = s32[16]{0:T(128)S(1)} collective-permute-done((s32[16]{0:T(128)S(1)}, s32[16]{0:T(128)S(1)}, u32[]{:S(2)}, u32[]{:S(2)}) %collective-permute-start) | collective-permute-done | bytes 96 | tf_op jit(solution)/shard_map/ppermute | solution.py:425
  54.3 2.5 %collective-permute-done.7.refs_6_ = f32[56,128]{1,0:T(8,128)S(1)} collective-permute-done((f32[56,128]{1,0:T(8,128)}, f32[56,128]{1,0:T(8,128)S(1)}, u32[]{:S(2)}, u32[]{:S(2)}) %collective-permute-start.7) | collective-permute-done | bytes 28704 | tf_op jit(solution)/shard_map/ppermute | solution.py:425
  57.4 2.8 %sum_channels.1 = (f32[216,128]{1,0:T(8,128)}, f32[216,128]{1,0:T(8,128)}, f32[216,128]{1,0:T(8,128)}, f32[216,128]{1,0:T(8,128)}, f32[216,128]{1,0:T(8,128)}, /...) custom-call(s32[2]{0:T(128)} %pad_add_fusion.place, s32[64]{0:T(128)} %pad_add_fusion.1.ids, ...), custom_call_target="tpu_custom_call" | custom-call | tf_op jit(solution)/shard_map/sum_channels/pallas_call | solution.py:304
  60.2 1.9 %collective-permute-start.9 = (f32[216,128]{1,0:T(8,128)}, f32[216,128]{1,0:T(8,128)S(1)}, u32[]{:S(2)}, u32[]{:S(2)}) collective-permute-start(f32[216,128]{1,0:T(8,128)} %get-tuple-element.46), channel_id=1, source_target_pairs={{0,1},{1,2},{2,3},{3,4},{4,5},{5,6},{6,7},{7,0},{8,9},{9,10},{10,1... | collective-permute-start | bytes 331784 | tf_op jit(solution)/shard_map/ppermute | solution.py:425
  62.1 3.3 %collective-permute-start.10 = (f32[216,128]{1,0:T(8,128)}, f32[216,128]{1,0:T(8,128)S(1)}, u32[]{:S(2)}, u32[]{:S(2)}) collective-permute-start(f32[216,128]{1,0:T(8,128)} %get-tuple-element.47), channel_id=1, source_target_pairs={{0,2},{1,3},{2,4},{3,5},{4,6},{5,7},{6,0},{7,1},{8,10},{9,11},{10,... | collective-permute-start | bytes 331784 | tf_op jit(solution)/shard_map/ppermute | solution.py:425
  65.4 4.0 %collective-permute-start.11 = (f32[216,128]{1,0:T(8,128)}, f32[216,128]{1,0:T(8,128)S(1)}, u32[]{:S(2)}, u32[]{:S(2)}) collective-permute-start(f32[216,128]{1,0:T(8,128)} %get-tuple-element.48), channel_id=1, source_target_pairs={{0,3},{1,4},{2,5},{3,6},{4,7},{5,0},{6,1},{7,2},{8,11},{9,12},{10,... | collective-permute-start | bytes 331784 | tf_op jit(solution)/shard_map/ppermute | solution.py:425
  70.0 4.9 %collective-permute-start.13 = (f32[216,128]{1,0:T(8,128)}, f32[216,128]{1,0:T(8,128)S(1)}, u32[]{:S(2)}, u32[]{:S(2)}) collective-permute-start(f32[216,128]{1,0:T(8,128)} %get-tuple-element.50), channel_id=1, source_target_pairs={{0,5},{1,6},{2,7},{3,0},{4,1},{5,2},{6,3},{7,4},{8,13},{9,14},{10,... | collective-permute-start | bytes 331784 | tf_op jit(solution)/shard_map/ppermute | solution.py:425
  74.9 2.7 %collective-permute-start.14 = (f32[216,128]{1,0:T(8,128)}, f32[216,128]{1,0:T(8,128)S(1)}, u32[]{:S(2)}, u32[]{:S(2)}) collective-permute-start(f32[216,128]{1,0:T(8,128)} %get-tuple-element.51), channel_id=1, source_target_pairs={{0,6},{1,7},{2,0},{3,1},{4,2},{5,3},{6,4},{7,5},{8,14},{9,15},{10,... | collective-permute-start | bytes 331784 | tf_op jit(solution)/shard_map/ppermute | solution.py:425
  77.6 2.3 %collective-permute-done.10.refs_2_ = f32[216,128]{1,0:T(8,128)S(1)} collective-permute-done((f32[216,128]{1,0:T(8,128)}, f32[216,128]{1,0:T(8,128)S(1)}, u32[]{:S(2)}, u32[]{:S(2)}) %collective-permute-start.10) | collective-permute-done | bytes 110624 | tf_op jit(solution)/shard_map/ppermute | solution.py:425
  79.9 2.8 %collective-permute-done.11.refs_3_ = f32[216,128]{1,0:T(8,128)S(1)} collective-permute-done((f32[216,128]{1,0:T(8,128)}, f32[216,128]{1,0:T(8,128)S(1)}, u32[]{:S(2)}, u32[]{:S(2)}) %collective-permute-start.11) | collective-permute-done | bytes 110624 | tf_op jit(solution)/shard_map/ppermute | solution.py:425
  82.7 4.0 %collective-permute-done.13.refs_5_ = f32[216,128]{1,0:T(8,128)S(1)} collective-permute-done((f32[216,128]{1,0:T(8,128)}, f32[216,128]{1,0:T(8,128)S(1)}, u32[]{:S(2)}, u32[]{:S(2)}) %collective-permute-start.13) | collective-permute-done | bytes 110624 | tf_op jit(solution)/shard_map/ppermute | solution.py:425
  86.8 1.8 %collective-permute-done.14.refs_6_ = f32[216,128]{1,0:T(8,128)S(1)} collective-permute-done((f32[216,128]{1,0:T(8,128)}, f32[216,128]{1,0:T(8,128)S(1)}, u32[]{:S(2)}, u32[]{:S(2)}) %collective-permute-start.14) | collective-permute-done | bytes 110624 | tf_op jit(solution)/shard_map/ppermute | solution.py:425
  89.8 1.9 %objects.1.refs_0_ = f32[144,128]{1,0:T(8,128)} custom-call(f32[216,128]{1,0:T(8,128)} %get-tuple-element.45.refs_0_, f32[216,128]{1,0:T(8,128)} %copy-done.7, f32[216,128]{1,0:T(8,128)} %copy-done.8, f32[216,128]{1,0:T(8,128)} %copy-done.9, f32[216,128]{1,0:T(8,128)} %copy-done.10, f32[216,128]{1,0:T(8,128)} %copy-done.11, f32[216,128]{1,0:T(8,128)} %copy-done.12, ...), custom_call_target="tpu_custom_call" | custom-call | tf_op jit(solution)/shard_map/objects/pallas_call | solution.py:304
  91.7 2.7 %collective-permute-start.22 = (f32[144,128]{1,0:T(8,128)}, f32[144,128]{1,0:T(8,128)S(1)}, u32[]{:S(2)}, u32[]{:S(2)}) collective-permute-start(f32[144,128]{1,0:T(8,128)} %objects.1.refs_0_), channel_id=1, source_target_pairs={{0,7},{1,0},{2,1},{3,2},{4,3},{5,4},{6,5},{7,6},{8,15},{9,8},{10,9... | collective-permute-start | bytes 221192 | tf_op jit(solution)/shard_map/ppermute | solution.py:425
  94.4 3.2 %collective-permute-start.20 = (f32[144,128]{1,0:T(8,128)}, f32[144,128]{1,0:T(8,128)S(1)}, u32[]{:S(2)}, u32[]{:S(2)}) collective-permute-start(f32[144,128]{1,0:T(8,128)} %objects.1.refs_0_), channel_id=1, source_target_pairs={{0,5},{1,6},{2,7},{3,0},{4,1},{5,2},{6,3},{7,4},{8,13},{9,14},{10,... | collective-permute-start | bytes 221192 | tf_op jit(solution)/shard_map/ppermute | solution.py:425
  97.6 3.0 %collective-permute-start.19 = (f32[144,128]{1,0:T(8,128)}, f32[144,128]{1,0:T(8,128)S(1)}, u32[]{:S(2)}, u32[]{:S(2)}) collective-permute-start(f32[144,128]{1,0:T(8,128)} %objects.1.refs_0_), channel_id=1, source_target_pairs={{0,4},{1,5},{2,6},{3,7},{4,0},{5,1},{6,2},{7,3},{8,12},{9,13},{10,... | collective-permute-start | bytes 221192 | tf_op jit(solution)/shard_map/ppermute | solution.py:425
  102.3 2.4 %collective-permute-start.17 = (f32[144,128]{1,0:T(8,128)}, f32[144,128]{1,0:T(8,128)S(1)}, u32[]{:S(2)}, u32[]{:S(2)}) collective-permute-start(f32[144,128]{1,0:T(8,128)} %objects.1.refs_0_), channel_id=1, source_target_pairs={{0,2},{1,3},{2,4},{3,5},{4,6},{5,7},{6,0},{7,1},{8,10},{9,11},{10,... | collective-permute-start | bytes 221192 | tf_op jit(solution)/shard_map/ppermute | solution.py:425
  104.7 2.2 %collective-permute-done.19.refs_4_ = f32[144,128]{1,0:T(8,128)S(1)} collective-permute-done((f32[144,128]{1,0:T(8,128)}, f32[144,128]{1,0:T(8,128)S(1)}, u32[]{:S(2)}, u32[]{:S(2)}) %collective-permute-start.19) | collective-permute-done | bytes 73760 | tf_op jit(solution)/shard_map/ppermute | solution.py:425
  106.9 4.7 %collective-permute-done.18.refs_3_ = f32[144,128]{1,0:T(8,128)S(1)} collective-permute-done((f32[144,128]{1,0:T(8,128)}, f32[144,128]{1,0:T(8,128)S(1)}, u32[]{:S(2)}, u32[]{:S(2)}) %collective-permute-start.18) | collective-permute-done | bytes 73760 | tf_op jit(solution)/shard_map/ppermute | solution.py:425
  114.7 2.2 %select_objects.1 = (f32[576,128]{1,0:T(8,128)}, f32[576,128]{1,0:T(8,128)}, f32[576,128]{1,0:T(8,128)}, f32[576,128]{1,0:T(8,128)}, f32[40,128]{1,0:T(8,128)}) custom-call(s32[2]{0:T(128)} %pad_add_fusion.place, s32[64]{0:T(128)} %pad_add_fusion.1.ids, f32[144,128]{1,0:T(8,128)} %objects.1.refs_0_, f32[144,128]{1,0:T(8,128)} %copy-done.20, ...), custom_call_target="tpu_custom_call" | custom-call | tf_op jit(solution)/shard_map/select_objects/pallas_call | solution.py:304
  117.4 3.2 %collective-permute-start.24 = (f32[576,128]{1,0:T(8,128)}, f32[576,128]{1,0:T(8,128)S(1)}, u32[]{:S(2)}, u32[]{:S(2)}) collective-permute-start(f32[576,128]{1,0:T(8,128)} %get-tuple-element.55), channel_id=1, source_target_pairs={{0,16},{1,17},{2,18},{3,19},{4,20},{5,21},{6,22},{7,23},{8,24},{9,... | collective-permute-start | bytes 884744 | tf_op jit(solution)/shard_map/ppermute | solution.py:425
  121.3 6.6 %collective-permute-done.23.refs_1_.refs_5_ = f32[576,128]{1,0:T(8,128)S(1)} collective-permute-done((f32[576,128]{1,0:T(8,128)}, f32[576,128]{1,0:T(8,128)S(1)}, u32[]{:S(2)}, u32[]{:S(2)}) %collective-permute-start.23) | collective-permute-done | bytes 294944 | tf_op jit(solution)/shard_map/ppermute | solution.py:425
  127.9 5.1 %collective-permute-done.24.refs_2_.refs_6_ = f32[576,128]{1,0:T(8,128)S(1)} collective-permute-done((f32[576,128]{1,0:T(8,128)}, f32[576,128]{1,0:T(8,128)S(1)}, u32[]{:S(2)}, u32[]{:S(2)}) %collective-permute-start.24) | collective-permute-done | bytes 294944 | tf_op jit(solution)/shard_map/ppermute | solution.py:425
  133.9 9.8 %backward_narrow.1 = (f32[16,64,64]{2,1,0:T(8,128)}, f32[2,72,128]{2,1,0:T(8,128)}) custom-call(s32[2]{0:T(128)} %pad_add_fusion.place, f32[16,64,128]{2,1,0:T(8,128)} %pad_maximum_fusion.1.q_ref, f32[16,72,256]{2,1,0:T(8,128)} %get-tuple-element.59.s_ref, f32[16,72,256]{2,1,0:T(8,128)} %get-tuple-element.60.d_ref, ...), custom_call_target="tpu_custom_call" | custom-call | flops 20000000000 | bytes 8000000 | tf_op jit(solution)/shard_map/backward_narrow/pallas_call | solution.py:385
  145.6 9.7 %backward_wide.1 = (f32[16,64,64]{2,1,0:T(8,128)}, f32[2,72,128]{2,1,0:T(8,128)}) custom-call(s32[2]{0:T(128)} %pad_add_fusion.place, f32[16,64,128]{2,1,0:T(8,128)} %pad_maximum_fusion.q_ref, f32[16,72,256]{2,1,0:T(8,128)} %get-tuple-element.34.s_ref, f32[16,72,256]{2,1,0:T(8,128)} %get-tuple-element.35.d_ref, f32[16,2,128,128]{3,2,1,0:T(8,128)} %get-tuple-element.36.g_ref, ...), custom_call_target="tpu_custom_call" | custom-call | flops 20000000000 | bytes 8000000 | tf_op jit(solution)/shard_map/backward_wide/pallas_call | solution.py:385
  159.8 2.6 %fusion = f32[16,150]{1,0:T(8,128)} fusion(f32[16,4096]{1,0:T(8,128)S(1)} %reshape.32, f32[150,4096]{1,0:T(8,128)S(1)} %copy-done), kind=kOutput, calls=%fused_computation.12 | convolution fusion | flops 117964800 | bytes 2729344 | tf_op jit(solution)/shard_map/dot_general | solution.py:475
  (108 shorter events, 32.7 us)
Async XLA Ops:
  10.3 14.4 %copy-start.1 = (f32[16,4096]{1,0:T(8,128)S(1)}, f32[16,4096]{1,0:T(8,128)}, u32[]{:S(2)}) copy-start(f32[16,4096]{1,0:T(8,128)} %get-tuple-element.67) | copy-start | bytes 786436
  18.9 37.9 %collective-permute-start.3 = (f32[816,128]{1,0:T(8,128)}, f32[816,128]{1,0:T(8,128)}, u32[]{:S(2)}, u32[]{:S(2)}) collective-permute-start(f32[816,128]{1,0:T(8,128)} %get-tuple-element.38), channel_id=1, source_target_pairs={{0,8},{1,9},{2,10},{3,11},{4,12},{5,13},{6,14},{7,15},{8,16},{9,17... | collective-permute-start | bytes 1253384 | tf_op jit(solution)/shard_map/ppermute | solution.py:425
  20.5 36.3 %collective-permute-start.4 = (f32[816,128]{1,0:T(8,128)}, f32[816,128]{1,0:T(8,128)}, u32[]{:S(2)}, u32[]{:S(2)}) collective-permute-start(f32[816,128]{1,0:T(8,128)} %get-tuple-element.39), channel_id=1, source_target_pairs={{0,16},{1,17},{2,18},{3,19},{4,20},{5,21},{6,22},{7,23},{8,24},{9,... | collective-permute-start | bytes 1253384 | tf_op jit(solution)/shard_map/ppermute | solution.py:425
  23.4 33.4 %collective-permute-start.5 = (f32[816,128]{1,0:T(8,128)}, f32[816,128]{1,0:T(8,128)}, u32[]{:S(2)}, u32[]{:S(2)}) collective-permute-start(f32[816,128]{1,0:T(8,128)} %get-tuple-element.40), channel_id=1, source_target_pairs={{0,24},{1,25},{2,26},{3,27},{4,28},{5,29},{6,30},{7,31},{8,0},{9,1... | collective-permute-start | bytes 1253384 | tf_op jit(solution)/shard_map/ppermute | solution.py:425
  35.4 16.5 %collective-permute-start.6 = (f32[56,128]{1,0:T(8,128)}, f32[56,128]{1,0:T(8,128)S(1)}, u32[]{:S(2)}, u32[]{:S(2)}) collective-permute-start(f32[56,128]{1,0:T(8,128)} %get-tuple-element.42), channel_id=1, source_target_pairs={{0,8},{1,9},{2,10},{3,11},{4,12},{5,13},{6,14},{7,15},{8,16},{9,17... | collective-permute-start | bytes 86024 | tf_op jit(solution)/shard_map/ppermute | solution.py:425
  36.2 6.4 %collective-permute-start.2 = (s32[16]{0:T(128)S(1)}, s32[16]{0:T(128)S(1)}, u32[]{:S(2)}, u32[]{:S(2)}) collective-permute-start(s32[16]{0:T(128)S(1)} %bitcast.13), channel_id=1, source_target_pairs={{0,8},{1,9},{2,10},{3,11},{4,12},{5,13},{6,14},{7,15},{8,16},{9,17... | collective-permute-start | bytes 200 | tf_op jit(solution)/shard_map/ppermute | solution.py:425
  42.6 5.0 %collective-permute-start.1 = (s32[16]{0:T(128)S(1)}, s32[16]{0:T(128)S(1)}, u32[]{:S(2)}, u32[]{:S(2)}) collective-permute-start(s32[16]{0:T(128)S(1)} %bitcast.14), channel_id=1, source_target_pairs={{0,16},{1,17},{2,18},{3,19},{4,20},{5,21},{6,22},{7,23},{8,24},{9,... | collective-permute-start | bytes 200 | tf_op jit(solution)/shard_map/ppermute | solution.py:425
  47.7 3.5 %collective-permute-start = (s32[16]{0:T(128)S(1)}, s32[16]{0:T(128)S(1)}, u32[]{:S(2)}, u32[]{:S(2)}) collective-permute-start(s32[16]{0:T(128)S(1)} %bitcast.15), channel_id=1, source_target_pairs={{0,24},{1,25},{2,26},{3,27},{4,28},{5,29},{6,30},{7,31},{8,0},{9,1... | collective-permute-start | bytes 200 | tf_op jit(solution)/shard_map/ppermute | solution.py:425
  51.2 5.6 %collective-permute-start.7 = (f32[56,128]{1,0:T(8,128)}, f32[56,128]{1,0:T(8,128)S(1)}, u32[]{:S(2)}, u32[]{:S(2)}) collective-permute-start(f32[56,128]{1,0:T(8,128)} %get-tuple-element.43), channel_id=1, source_target_pairs={{0,16},{1,17},{2,18},{3,19},{4,20},{5,21},{6,22},{7,23},{8,24},{9,... | collective-permute-start | bytes 86024 | tf_op jit(solution)/shard_map/ppermute | solution.py:425
  51.9 4.9 %collective-permute-start.8 = (f32[56,128]{1,0:T(8,128)}, f32[56,128]{1,0:T(8,128)S(1)}, u32[]{:S(2)}, u32[]{:S(2)}) collective-permute-start(f32[56,128]{1,0:T(8,128)} %get-tuple-element.44), channel_id=1, source_target_pairs={{0,24},{1,25},{2,26},{3,27},{4,28},{5,29},{6,30},{7,31},{8,0},{9,1... | collective-permute-start | bytes 86024 | tf_op jit(solution)/shard_map/ppermute | solution.py:425
  60.2 14.7 %collective-permute-start.9 = (f32[216,128]{1,0:T(8,128)}, f32[216,128]{1,0:T(8,128)S(1)}, u32[]{:S(2)}, u32[]{:S(2)}) collective-permute-start(f32[216,128]{1,0:T(8,128)} %get-tuple-element.46), channel_id=1, source_target_pairs={{0,1},{1,2},{2,3},{3,4},{4,5},{5,6},{6,7},{7,0},{8,9},{9,10},{10,1... | collective-permute-start | bytes 331784 | tf_op jit(solution)/shard_map/ppermute | solution.py:425
  62.1 17.7 %collective-permute-start.10 = (f32[216,128]{1,0:T(8,128)}, f32[216,128]{1,0:T(8,128)S(1)}, u32[]{:S(2)}, u32[]{:S(2)}) collective-permute-start(f32[216,128]{1,0:T(8,128)} %get-tuple-element.47), channel_id=1, source_target_pairs={{0,2},{1,3},{2,4},{3,5},{4,6},{5,7},{6,0},{7,1},{8,10},{9,11},{10,... | collective-permute-start | bytes 331784 | tf_op jit(solution)/shard_map/ppermute | solution.py:425
  65.4 17.3 %collective-permute-start.11 = (f32[216,128]{1,0:T(8,128)}, f32[216,128]{1,0:T(8,128)S(1)}, u32[]{:S(2)}, u32[]{:S(2)}) collective-permute-start(f32[216,128]{1,0:T(8,128)} %get-tuple-element.48), channel_id=1, source_target_pairs={{0,3},{1,4},{2,5},{3,6},{4,7},{5,0},{6,1},{7,2},{8,11},{9,12},{10,... | collective-permute-start | bytes 331784 | tf_op jit(solution)/shard_map/ppermute | solution.py:425
  69.4 13.3 %collective-permute-start.12 = (f32[216,128]{1,0:T(8,128)}, f32[216,128]{1,0:T(8,128)S(1)}, u32[]{:S(2)}, u32[]{:S(2)}) collective-permute-start(f32[216,128]{1,0:T(8,128)} %get-tuple-element.49), channel_id=1, source_target_pairs={{0,4},{1,5},{2,6},{3,7},{4,0},{5,1},{6,2},{7,3},{8,12},{9,13},{10,... | collective-permute-start | bytes 331784 | tf_op jit(solution)/shard_map/ppermute | solution.py:425
  70.0 16.8 %collective-permute-start.13 = (f32[216,128]{1,0:T(8,128)}, f32[216,128]{1,0:T(8,128)S(1)}, u32[]{:S(2)}, u32[]{:S(2)}) collective-permute-start(f32[216,128]{1,0:T(8,128)} %get-tuple-element.50), channel_id=1, source_target_pairs={{0,5},{1,6},{2,7},{3,0},{4,1},{5,2},{6,3},{7,4},{8,13},{9,14},{10,... | collective-permute-start | bytes 331784 | tf_op jit(solution)/shard_map/ppermute | solution.py:425
  74.9 14.2 %copy-start.7 = (f32[216,128]{1,0:T(8,128)}, f32[216,128]{1,0:T(8,128)S(1)}, u32[]{:S(2)}) copy-start(f32[216,128]{1,0:T(8,128)S(1)} %collective-permute-done.9.refs_1_) | copy-start | bytes 331780
  74.9 13.6 %collective-permute-start.14 = (f32[216,128]{1,0:T(8,128)}, f32[216,128]{1,0:T(8,128)S(1)}, u32[]{:S(2)}, u32[]{:S(2)}) collective-permute-start(f32[216,128]{1,0:T(8,128)} %get-tuple-element.51), channel_id=1, source_target_pairs={{0,6},{1,7},{2,0},{3,1},{4,2},{5,3},{6,4},{7,5},{8,14},{9,15},{10,... | collective-permute-start | bytes 331784 | tf_op jit(solution)/shard_map/ppermute | solution.py:425
  79.9 9.3 %collective-permute-start.15 = (f32[216,128]{1,0:T(8,128)}, f32[216,128]{1,0:T(8,128)S(1)}, u32[]{:S(2)}, u32[]{:S(2)}) collective-permute-start(f32[216,128]{1,0:T(8,128)} %get-tuple-element.52), channel_id=1, source_target_pairs={{0,7},{1,0},{2,1},{3,2},{4,3},{5,4},{6,5},{7,6},{8,15},{9,8},{10,9... | collective-permute-start | bytes 331784 | tf_op jit(solution)/shard_map/ppermute | solution.py:425
  91.7 10.7 %collective-permute-start.22 = (f32[144,128]{1,0:T(8,128)}, f32[144,128]{1,0:T(8,128)S(1)}, u32[]{:S(2)}, u32[]{:S(2)}) collective-permute-start(f32[144,128]{1,0:T(8,128)} %objects.1.refs_0_), channel_id=1, source_target_pairs={{0,7},{1,0},{2,1},{3,2},{4,3},{5,4},{6,5},{7,6},{8,15},{9,8},{10,9... | collective-permute-start | bytes 221192 | tf_op jit(solution)/shard_map/ppermute | solution.py:425
  94.4 10.3 %collective-permute-start.21 = (f32[144,128]{1,0:T(8,128)}, f32[144,128]{1,0:T(8,128)S(1)}, u32[]{:S(2)}, u32[]{:S(2)}) collective-permute-start(f32[144,128]{1,0:T(8,128)} %objects.1.refs_0_), channel_id=1, source_target_pairs={{0,6},{1,7},{2,0},{3,1},{4,2},{5,3},{6,4},{7,5},{8,14},{9,15},{10,... | collective-permute-start | bytes 221192 | tf_op jit(solution)/shard_map/ppermute | solution.py:425
  94.4 10.4 %collective-permute-start.20 = (f32[144,128]{1,0:T(8,128)}, f32[144,128]{1,0:T(8,128)S(1)}, u32[]{:S(2)}, u32[]{:S(2)}) collective-permute-start(f32[144,128]{1,0:T(8,128)} %objects.1.refs_0_), channel_id=1, source_target_pairs={{0,5},{1,6},{2,7},{3,0},{4,1},{5,2},{6,3},{7,4},{8,13},{9,14},{10,... | collective-permute-start | bytes 221192 | tf_op jit(solution)/shard_map/ppermute | solution.py:425
  97.6 9.4 %collective-permute-start.19 = (f32[144,128]{1,0:T(8,128)}, f32[144,128]{1,0:T(8,128)S(1)}, u32[]{:S(2)}, u32[]{:S(2)}) collective-permute-start(f32[144,128]{1,0:T(8,128)} %objects.1.refs_0_), channel_id=1, source_target_pairs={{0,4},{1,5},{2,6},{3,7},{4,0},{5,1},{6,2},{7,3},{8,12},{9,13},{10,... | collective-permute-start | bytes 221192 | tf_op jit(solution)/shard_map/ppermute | solution.py:425
  100.6 11.0 %collective-permute-start.18 = (f32[144,128]{1,0:T(8,128)}, f32[144,128]{1,0:T(8,128)S(1)}, u32[]{:S(2)}, u32[]{:S(2)}) collective-permute-start(f32[144,128]{1,0:T(8,128)} %objects.1.refs_0_), channel_id=1, source_target_pairs={{0,3},{1,4},{2,5},{3,6},{4,7},{5,0},{6,1},{7,2},{8,11},{9,12},{10,... | collective-permute-start | bytes 221192 | tf_op jit(solution)/shard_map/ppermute | solution.py:425
  102.3 11.7 %copy-start.14 = (f32[144,128]{1,0:T(8,128)}, f32[144,128]{1,0:T(8,128)S(1)}, u32[]{:S(2)}) copy-start(f32[144,128]{1,0:T(8,128)S(1)} %collective-permute-done.22.refs_7_) | copy-start | bytes 221188
  102.3 10.2 %collective-permute-start.17 = (f32[144,128]{1,0:T(8,128)}, f32[144,128]{1,0:T(8,128)S(1)}, u32[]{:S(2)}, u32[]{:S(2)}) collective-permute-start(f32[144,128]{1,0:T(8,128)} %objects.1.refs_0_), channel_id=1, source_target_pairs={{0,2},{1,3},{2,4},{3,5},{4,6},{5,7},{6,0},{7,1},{8,10},{9,11},{10,... | collective-permute-start | bytes 221192 | tf_op jit(solution)/shard_map/ppermute | solution.py:425
  104.7 9.3 %copy-start.15 = (f32[144,128]{1,0:T(8,128)}, f32[144,128]{1,0:T(8,128)S(1)}, u32[]{:S(2)}) copy-start(f32[144,128]{1,0:T(8,128)S(1)} %collective-permute-done.21.refs_6_) | copy-start | bytes 221188
  104.7 9.3 %collective-permute-start.16 = (f32[144,128]{1,0:T(8,128)}, f32[144,128]{1,0:T(8,128)S(1)}, u32[]{:S(2)}, u32[]{:S(2)}) collective-permute-start(f32[144,128]{1,0:T(8,128)} %objects.1.refs_0_), channel_id=1, source_target_pairs={{0,1},{1,2},{2,3},{3,4},{4,5},{5,6},{6,7},{7,0},{8,9},{9,10},{10,1... | collective-permute-start | bytes 221192 | tf_op jit(solution)/shard_map/ppermute | solution.py:425
  104.7 9.3 %copy-start.16 = (f32[144,128]{1,0:T(8,128)}, f32[144,128]{1,0:T(8,128)S(1)}, u32[]{:S(2)}) copy-start(f32[144,128]{1,0:T(8,128)S(1)} %collective-permute-done.20.refs_5_) | copy-start | bytes 221188
  116.9 11.0 %collective-permute-start.23 = (f32[576,128]{1,0:T(8,128)}, f32[576,128]{1,0:T(8,128)S(1)}, u32[]{:S(2)}, u32[]{:S(2)}) collective-permute-start(f32[576,128]{1,0:T(8,128)} %get-tuple-element.54), channel_id=1, source_target_pairs={{0,8},{1,9},{2,10},{3,11},{4,12},{5,13},{6,14},{7,15},{8,16},{9,17... | collective-permute-start | bytes 884744 | tf_op jit(solution)/shard_map/ppermute | solution.py:425
  117.4 15.6 %collective-permute-start.24 = (f32[576,128]{1,0:T(8,128)}, f32[576,128]{1,0:T(8,128)S(1)}, u32[]{:S(2)}, u32[]{:S(2)}) collective-permute-start(f32[576,128]{1,0:T(8,128)} %get-tuple-element.55), channel_id=1, source_target_pairs={{0,16},{1,17},{2,18},{3,19},{4,20},{5,21},{6,22},{7,23},{8,24},{9,... | collective-permute-start | bytes 884744 | tf_op jit(solution)/shard_map/ppermute | solution.py:425
  120.6 12.6 %collective-permute-start.25 = (f32[576,128]{1,0:T(8,128)}, f32[576,128]{1,0:T(8,128)S(1)}, u32[]{:S(2)}, u32[]{:S(2)}) collective-permute-start(f32[576,128]{1,0:T(8,128)} %get-tuple-element.56), channel_id=1, source_target_pairs={{0,24},{1,25},{2,26},{3,27},{4,28},{5,29},{6,30},{7,31},{8,0},{9,1... | collective-permute-start | bytes 884744 | tf_op jit(solution)/shard_map/ppermute | solution.py:425
  145.6 12.8 %copy-start.4 = (f32[16,64,64]{2,1,0:T(8,128)S(1)}, f32[16,64,64]{2,1,0:T(8,128)}, u32[]{:S(2)}) copy-start(f32[16,64,64]{2,1,0:T(8,128)} %get-tuple-element.62) | copy-start | bytes 786436
  (23 other events, 77.9 us)

commit v2 on v1

v2 whole, which is shorter than its diff:
```python
import functools
import math

import jax
import jax.numpy as jnp
import numpy as np
from jax import lax
from jax.experimental import pallas as pl
from jax.experimental.pallas import tpu as pltpu
from jax.sharding import PartitionSpec as P

PUP = 64
SIZE = 128
HALF = SIZE // 2 + 1
ROWS = 72
NY, NZ = 4, 8
GROUP = 64 // NY
OWN = 32 // NZ
FRAMES = 16
STEP = 16
PRIOR_WEIGHT = 0.1
F32 = jnp.float32
BF16 = jnp.bfloat16
VMEM_LIMIT = 12 * 1024 * 1024
VMEM_SMALL = 6 * 1024 * 1024
EDGES = FRAMES * 3 * GROUP
IDS = EDGES + FRAMES * 3
Y_ROWS = IDS + 8
W_ROWS = 56
ORDER = (0, 2, 1, 3)
Z_ROWS = 216
F_ROWS = 144
R_ROWS = (FRAMES + 1) * 2 * GROUP


def dft(length, columns):
    angle = np.outer(np.arange(length), np.arange(columns)) % SIZE * (2.0 * math.pi / SIZE)
    return np.cos(angle), -np.sin(angle)


def halves(table):
    table = np.asarray(table, np.float32)
    high = table.astype(jnp.bfloat16)
    low = (table - high.astype(np.float32)).astype(jnp.bfloat16)
    return high, low


def left_short(table):
    high, low = halves(table)
    return [np.concatenate([high, high], 1), low]


def right_short(table):
    high, low = halves(table)
    return [np.concatenate([high, high], 0), low]


def mirrors():
    rows, lanes = np.zeros((SIZE, SIZE)), np.zeros((SIZE, SIZE))
    for j in range(1, 64):
        rows[j, 64 - j] = 1.0
        rows[64 + j, 128 - j] = -1.0
    for v in range(SIZE):
        lanes[-v % SIZE, v] = 1.0
    return [rows.astype(jnp.bfloat16), lanes.astype(jnp.bfloat16)]


def make_tables():
    c, s = dft(SIZE, SIZE)
    cp, sp = dft(SIZE, PUP)
    order = np.r_[0:PUP:2, 1:PUP:2]
    cx, sx = cp[:, order], sp[:, order]
    ch, sh = np.zeros((ROWS, SIZE)), np.zeros((ROWS, SIZE))
    ch[:HALF], sh[:HALF] = c[:HALF], s[:HALF]
    weight = np.zeros((ROWS, 1))
    weight[:HALF] = 2.0
    weight[0] = weight[HALF - 1] = 1.0
    forward = (
        right_short(np.block([[cp.T, sp.T], [-sp.T, cp.T]]))
        + left_short(np.block([[cx, -sx], [sx, cx]]))
        + left_short(np.concatenate([ch, sh], 0))
        + list(halves(np.block([[c.T, s.T], [-s.T, c.T]])))
    )
    backward = (
        list(halves(np.block([[c, -s], [s, c]])))
        + list(halves(np.concatenate([(weight * ch).T, (weight * sh).T], 1)))
        + list(halves(np.block([[cx.T, sx.T], [-sx.T, cx.T]])))
        + list(halves(np.block([[cp, -sp], [sp, cp]])))
        + mirrors()
    )
    return forward, backward


def mm(a, b):
    return jnp.dot(a, b, preferred_element_type=F32)


def cut(x):
    high = x.astype(BF16)
    return high, (x - high.astype(F32)).astype(BF16)


def right_mul_short(x, twice, low):
    h, r = cut(x)
    return mm(jnp.concatenate([h, r], 1), twice[...]) + mm(h, low[...])


def left_mul_short(twice, low, x):
    h, r = cut(x)
    return mm(twice[...], jnp.concatenate([h, r], 0)) + mm(low[...], h)


def right_mul(x, high, low):
    h, r = cut(x)
    return mm(h, high[...]) + (mm(r, high[...]) + mm(h, low[...]))


def left_mul(high, low, x):
    h, r = cut(x)
    return mm(high[...], h) + (mm(high[...], r) + mm(low[...], h))


def pair_spectra(blocks, left, right):
    out = []
    for a, b in zip(blocks[::2], blocks[1::2], strict=True):
        t = left_mul_short(*left, jnp.concatenate([a, b], 1))
        for k in range(2):
            lanes = slice(k * SIZE, (k + 1) * SIZE)
            out.append(jnp.concatenate([t[:ROWS, lanes], t[ROWS:, lanes]], 1))
    full = right_mul(jnp.concatenate(out, 0), *right)
    return [full[k * ROWS : (k + 1) * ROWS] for k in range(len(blocks))]


def cos_sin(x):
    turns = jnp.floor(x * (2.0 / math.pi) + 0.5)
    r = ((x - turns * 1.5703125) - turns * 4.837512969970703125e-4) - turns * 7.54978995489188216e-8
    z = r * r
    sine = r + r * z * ((-1.9515295891e-4 * z + 8.3321608736e-3) * z - 1.6666654611e-1)
    cosine = 1.0 - 0.5 * z + z * z * ((2.443315711809948e-5 * z - 1.388731625493765e-3) * z + 4.166664568298827e-2)
    quarter = turns.astype(jnp.int32)
    odd = (quarter & 1) != 0
    c, s = jnp.where(odd, sine, cosine), jnp.where(odd, cosine, sine)
    return jnp.where(((quarter + 1) & 2) != 0, -c, c), jnp.where((quarter & 2) != 0, -s, s)


def low_lanes(rows):
    return lax.broadcasted_iota(jnp.int32, (rows, SIZE), 1) < PUP


def forward_kernel(wide, place, phase_ref, pupil_ref, *rest):
    if not wide:
        diversity_ref, ids_ref, *rest = rest
    im_ref, r1, r2, l1, l2, h1, h2, f1, f2, q_ref, s_ref, d_ref, g_ref, *rest = rest
    outs, scr = rest[:-1], rest[-1]
    step = pl.program_id(0)
    y = place[0]
    low = low_lanes(PUP // 2)
    for k in range(STEP):
        total = phase_ref[k]
        if not wide:
            total = total + diversity_ref[...]
        re, im = (pupil_ref[...] * part for part in cos_sin(total))
        q_ref[k, : PUP // 2, :] = jnp.where(low, re, pltpu.roll(im, PUP, 1))
        q_ref[k, PUP // 2 :, :] = jnp.where(low, pltpu.roll(re, PUP, 1), im)
    t = right_mul_short(q_ref[...].reshape(STEP * PUP, 2 * PUP), r1, r2)
    powers = []
    for a in range(0, STEP, 2):
        cols = []
        for k in (a, a + 1):
            tk = t[k * PUP : (k + 1) * PUP]
            cols.append(jnp.concatenate([tk[:, :SIZE], tk[:, SIZE:]], 0))
        g = left_mul_short(l1, l2, jnp.concatenate(cols, 1))
        for k in (a, a + 1):
            lanes = slice((k - a) * SIZE, (k - a + 1) * SIZE)
            gr, gi = g[:SIZE, lanes], g[SIZE:, lanes]
            g_ref[k, 0], g_ref[k, 1] = gr, gi
            power = gr * gr + gi * gi
            powers.append(power / jnp.sum(power, keepdims=True))
    images = [im_ref[k, 0] for k in range(STEP)]
    spectra = pair_spectra(powers + images, (h1, h2), (f1, f2))

    if wide:

        @pl.when(step == 0)
        def _():
            scr[...] = jnp.zeros_like(scr)

    for k in range(STEP):
        sk, dk = spectra[k], spectra[STEP + k] * (1.0 / SIZE)
        s_ref[k], d_ref[k] = sk, dk
        sr, si, dr, di = sk[:, :SIZE], sk[:, SIZE:], dk[:, :SIZE], dk[:, SIZE:]
        terms = (dr * sr + di * si, di * sr - dr * si, sr * sr + si * si)
        for c in range(3):
            if wide:
                scr[c] += terms[c]
            else:
                scr[c] = terms[c]
        if not wide:
            frame = step * STEP + k
            for shift in range(NY):
                row = pl.multiple_of(GROUP * lax.rem(y + shift, NY), GROUP)
                for c in range(3):
                    at = pl.multiple_of(frame * 3 * GROUP + c * GROUP, GROUP)
                    outs[shift][pl.ds(at, GROUP), :] = scr[c, pl.ds(row, GROUP), :]
                    outs[shift][pl.ds(EDGES + 3 * frame + c, 1), :] = scr[c, 64:65, :]

    @pl.when(step == 0)
    def _():
        if not wide:
            for shift in range(NY):
                outs[shift][IDS:, :] = ids_ref[...]

    if wide:

        @pl.when(step == FRAMES // STEP - 1)
        def _():
            for shift in range(NY):
                out = outs[shift // 2]
                row = pl.multiple_of(GROUP * lax.rem(y + shift, NY), GROUP)
                for c in range(3):
                    out[shift % 2, c * GROUP : (c + 1) * GROUP, :] = scr[c, pl.ds(row, GROUP), :]
                    out[shift % 2, 3 * GROUP + c : 3 * GROUP + c + 1, :] = scr[c, 64:65, :]
                out[shift % 2, 3 * GROUP + 3 :, :] = jnp.zeros((W_ROWS - 3 * GROUP - 3, SIZE), F32)


def smem():
    return pl.BlockSpec(memory_space=pltpu.SMEM)


def whole(a):
    return pl.BlockSpec(a.shape, lambda i: (0,) * a.ndim)


def shape(*dims):
    return jax.ShapeDtypeStruct(dims, F32)


def forward(wide, place, phase, pupil, extra, images, tables):
    camera = 0 if wide else 1
    outs = [shape(FRAMES, PUP, 2 * PUP)] + [shape(FRAMES, ROWS, 2 * SIZE)] * 2 + [shape(FRAMES, 2, SIZE, SIZE)]
    terms = [shape(2, W_ROWS, SIZE)] * 2 if wide else [shape(Y_ROWS, SIZE)] * NY
    return pl.pallas_call(
        functools.partial(forward_kernel, wide),
        grid=(FRAMES // STEP,),
        in_specs=[smem(), pl.BlockSpec((STEP, PUP // 2, SIZE), lambda i: (i, 0, 0)), whole(pupil)]
        + [whole(e) for e in extra]
        + [pl.BlockSpec((STEP, 1, SIZE, SIZE), lambda i: (i, camera, 0, 0))]
        + [whole(t) for t in tables],
        out_specs=[pl.BlockSpec((STEP, PUP, 2 * PUP), lambda i: (i, 0, 0))]
        + [pl.BlockSpec((STEP, ROWS, 2 * SIZE), lambda i: (i, 0, 0))] * 2
        + [pl.BlockSpec((STEP, 2, SIZE, SIZE), lambda i: (i, 0, 0, 0))]
        + [whole(t) for t in terms],
        out_shape=outs + terms,
        scratch_shapes=[pltpu.VMEM((3, ROWS, SIZE), F32)],
        compiler_params=pltpu.CompilerParams(vmem_limit_bytes=VMEM_LIMIT),
        cost_estimate=pl.CostEstimate(flops=200_000_000_000, bytes_accessed=8_000_000, transcendentals=0),
        name="forward_wide" if wide else "forward_narrow",
    )(place, phase, pupil, *extra, images, *tables)


UP, DOWN, KEEP = (1, 4, 6), (7, 2), (0, 3, 5)


def sum_kernel(place, ids, *refs):
    narrow, (w1, w2, *outs, acc, edge) = refs[:NY], refs[NY:]
    z = place[1]
    acc[...] = jnp.zeros_like(acc)
    edge[...] = jnp.zeros_like(edge)
    for source in range(NY):
        for f in range(FRAMES):
            k = ids[source * FRAMES + f]
            acc[k] += narrow[source][f * 3 * GROUP : (f + 1) * 3 * GROUP, :]
            at = EDGES + 3 * f
            edge[k, 0:3, :] += narrow[source][at : at + 3, :]
    for out, group in zip(outs, (KEEP, UP, DOWN), strict=True):
        for n, shift in enumerate(group):
            to = lax.rem(z + shift, NZ)
            start = n * Z_ROWS
            for k in range(OWN):
                at = start + k * 3 * GROUP
                out[at : at + 3 * GROUP, :] = acc[OWN * to + k]
                at = start + OWN * 3 * GROUP + 3 * k
                out[at : at + 3, :] = edge[OWN * to + k, 0:3, :]
            at = start + OWN * (3 * GROUP + 3)
            for c in range(3):
                for j in range(2):
                    row = pl.ds(GROUP * c + 2 * to + j, 1)
                    out[at + 2 * c + j : at + 2 * c + j + 1, :] = w1[row, :] + w2[row, :]
            row = slice(3 * GROUP, 3 * GROUP + 3)
            out[at + 6 : at + 9, :] = w1[row, :] + w2[row, :]
            out[at + 9 : start + Z_ROWS, :] = jnp.zeros((Z_ROWS - OWN * (3 * GROUP + 3) - 9, SIZE), F32)


def relay_kernel(keep, up, down, far, back):
    one, two = slice(Z_ROWS, 2 * Z_ROWS), slice(2 * Z_ROWS, 3 * Z_ROWS)
    far[...] = keep[one, :] + (up[one, :] + down[one, :])
    back[...] = keep[two, :] + up[two, :]


def quotient(num_re, num_im, den):
    den = PRIOR_WEIGHT + den
    return num_re / den, num_im / den


def object_kernel(keep, up, down, far, back, out):
    own = slice(0, Z_ROWS)
    sums = (keep[own, :] + (up[own, :] + down[own, :])) + (far[...] + back[...])
    for k in range(OWN):
        base = k * 3 * GROUP
        re, im = quotient(*(sums[base + c * GROUP : base + (c + 1) * GROUP] for c in range(3)))
        out[k * 2 * GROUP : k * 2 * GROUP + GROUP, :] = re
        out[k * 2 * GROUP + GROUP : (k + 1) * 2 * GROUP, :] = im
        base = OWN * 3 * GROUP + 3 * k
        re, im = quotient(*(sums[base + c : base + c + 1] for c in range(3)))
        at = OWN * 2 * GROUP + 2 * k
        out[at : at + 1, :] = re
        out[at + 1 : at + 2, :] = im
    base = OWN * (3 * GROUP + 3)
    at = OWN * (2 * GROUP + 2)
    re, im = quotient(*(sums[base + 2 * c : base + 2 * c + 2] for c in range(3)))
    out[at : at + 2, :] = re
    out[at + 2 : at + 4, :] = im
    re, im = quotient(*(sums[base + 6 + c : base + 7 + c] for c in range(3)))
    out[at + 4 : at + 5, :] = re
    out[at + 5 : at + 6, :] = im
    out[at + 6 :, :] = jnp.zeros((F_ROWS - at - 6, SIZE), F32)


def select_kernel(place, ids, own, ahead, behind, up, down, *refs):
    outs, (wide, near, objects, edge, total) = refs[:NY], refs[NY:]
    y, z = place[0], place[1]
    parts = ((0, own, 0), (3, ahead, 0), (5, behind, 0), (7, up, 0), (2, up, 1), (4, up, 2), (1, down, 0), (6, down, 1))
    for shift, part, n in parts:
        source = lax.rem(z + shift, NZ)
        start = n * F_ROWS
        for k in range(OWN):
            at = start + k * 2 * GROUP
            objects[OWN * source + k] = part[at : at + 2 * GROUP, :]
            at = start + OWN * 2 * GROUP + 2 * k
            edge[OWN * source + k, 0:2, :] = part[at : at + 2, :]
        at = start + OWN * (2 * GROUP + 2)
        for j in range(2):
            total[pl.ds(2 * source + j, 1), :] = part[at + j : at + j + 1, :]
            total[pl.ds(GROUP + 2 * source + j, 1), :] = part[at + 2 + j : at + 3 + j, :]
    wide[...] = total[...]
    for shift in range(NY):
        out = outs[shift]
        source = ORDER.index((NY - shift) % NY)
        for f in range(FRAMES):
            out[f * 2 * GROUP : (f + 1) * 2 * GROUP, :] = objects[ids[source * FRAMES + f]]
        out[FRAMES * 2 * GROUP :, :] = objects[lax.rem(y + shift, NY) * NZ + z]
    for f in range(FRAMES):
        near[2 * f : 2 * f + 2, :] = edge[ids[f], 0:2, :]
    near[2 * FRAMES : 2 * FRAMES + 2, :] = edge[y * NZ + z, 0:2, :]
    at = OWN * (2 * GROUP + 2) + 4
    near[2 * FRAMES + 2 : 2 * FRAMES + 4, :] = own[at : at + 2, :]
    near[2 * FRAMES + 4 :, :] = jnp.zeros((4, SIZE), F32)


def plain(kernel, name, smems, arrays, outs, scratch):
    return pl.pallas_call(
        kernel,
        in_specs=[smem()] * len(smems) + [pl.BlockSpec(memory_space=pltpu.VMEM)] * len(arrays),
        out_specs=[pl.BlockSpec(memory_space=pltpu.VMEM)] * len(outs),
        out_shape=outs,
        scratch_shapes=scratch,
        compiler_params=pltpu.CompilerParams(vmem_limit_bytes=VMEM_SMALL),
        name=name,
    )(*smems, *arrays)


def backward_kernel(wide, place, q_ref, s_ref, d_ref, g_ref, *refs):
    parts, refs = refs[:NY], refs[NY:]
    if not wide:
        own, (other, *refs) = refs[:NY], refs[NY:]
    near, a1, a2, b1, b2, e1, e2, f1, f2, m1, m2, out, obj, scr = refs
    step = pl.program_id(0)
    y = place[0]

    def gather(sources, at):
        for shift in range(NY):
            row = pl.multiple_of(GROUP * lax.rem(y + NY - shift, NY), GROUP)
            for c in range(2):
                scr[c, pl.ds(row, GROUP), :] = sources[shift][at + c * GROUP : at + (c + 1) * GROUP, :]

    @pl.when(step == 0)
    def _():
        scr[...] = jnp.zeros_like(scr)
        gather(parts if wide else own, 0)
        at = 2 * FRAMES + (2 if wide else 0)
        for c in range(2):
            scr[c, 64:65, :] = near[at + c : at + c + 1, :]
        half = jnp.concatenate([scr[0, :64, :], scr[1, :64, :]], 0)
        high = half.astype(BF16)
        middle, low = cut(half - high.astype(F32))
        turned = jnp.zeros((SIZE, SIZE), F32)
        for part in (high, middle, low):
            turned = turned + mm(m1[...], mm(part, m2[...]).astype(BF16))
        for c in range(2):
            obj[c, :64, :] = scr[c, :64, :]
            obj[c, 64:, :] = turned[64 * c : 64 * (c + 1)]
            obj[c, 64:65, :] = scr[c, 64:65, :]

    cots = []
    for k in range(STEP):
        if not wide:
            gather(parts, k * 2 * GROUP)
            for c in range(2):
                scr[c, 64:65, :] = near[pl.ds(2 * (step * STEP + k) + c, 1), :]
        fr, fi = scr[0], scr[1]
        sk, dk = s_ref[k], d_ref[k]
        sr, si, dr, di = sk[:, :SIZE], sk[:, SIZE:], dk[:, :SIZE], dk[:, SIZE:]
        rest_r = dr - (fr * sr - fi * si)
        rest_i = di - (fr * si + fi * sr)
        cots.append(jnp.concatenate([-(rest_r * fr + rest_i * fi), rest_r * fi - rest_i * fr], 1))
    t = right_mul(jnp.concatenate(cots, 0), a1, a2)
    steps = []
    for a in range(0, STEP, 2):
        cols = []
        for k in (a, a + 1):
            tk = t[k * ROWS : (k + 1) * ROWS]
            cols.append(jnp.concatenate([tk[:, :SIZE], tk[:, SIZE:]], 0))
        dp = left_mul(b1, b2, jnp.concatenate(cols, 1))
        fields = []
        for k in (a, a + 1):
            gr, gi = g_ref[k, 0], g_ref[k, 1]
            power = gr * gr + gi * gi
            scale = 1.0 / jnp.sum(power, keepdims=True)
            dk = dp[:, (k - a) * SIZE : (k - a + 1) * SIZE]
            mean = jnp.sum(dk * power, keepdims=True) * scale
            dk = (dk - mean) * (scale * (4.0 / (SIZE * SIZE)))
            fields.append(jnp.concatenate([gr * dk, gi * dk], 0))
        h = left_mul(e1, e2, jnp.concatenate(fields, 1))
        for k in (a, a + 1):
            lanes = slice((k - a) * SIZE, (k - a + 1) * SIZE)
            steps.append(jnp.concatenate([h[:PUP, lanes], h[PUP:, lanes]], 1))
    dq = right_mul(jnp.concatenate(steps, 0), f1, f2)
    low = low_lanes(PUP // 2)
    flat = []
    for k in range(STEP):
        m = q_ref[k] * pltpu.roll(dq[k * PUP : (k + 1) * PUP], PUP, 1)
        m = m - pltpu.roll(m, PUP, 1)
        dphase = jnp.where(low, m[: PUP // 2], -m[PUP // 2 :])
        if wide:
            out[k] = dphase
        else:
            flat.append(dphase + other[k])
    for at in range(0, FRAMES if flat else 0, STEP):

        @pl.when(step * STEP == at)
        def _(at=at):
            for k, dphase in enumerate(flat):
                for r in range(PUP // 2):
                    out[at + k : at + k + 1, r * SIZE : (r + 1) * SIZE] = dphase[r : r + 1]


def backward(wide, place, q, s, d, g, parts, near, other, tables):
    block = 2 * GROUP
    pairs = pl.BlockSpec((STEP, PUP // 2, SIZE), lambda i: (i, 0, 0))
    if wide:
        sources, specs = list(parts), [whole(p) for p in parts]
        dphase, dphase_spec = shape(FRAMES, PUP // 2, SIZE), pairs
    else:
        sources = list(parts) * 2 + [other]
        specs = [pl.BlockSpec((STEP * block, SIZE), lambda i: (i, 0))] * NY
        specs += [pl.BlockSpec((block, SIZE), lambda i: (FRAMES, 0))] * NY + [pairs]
        dphase = shape(FRAMES, PUP * PUP)
        dphase_spec = pl.BlockSpec(dphase.shape, lambda i: (0, 0))
    return pl.pallas_call(
        functools.partial(backward_kernel, wide),
        grid=(FRAMES // STEP,),
        in_specs=[
            smem(),
            pl.BlockSpec((STEP, PUP, 2 * PUP), lambda i: (i, 0, 0)),
            pl.BlockSpec((STEP, ROWS, 2 * SIZE), lambda i: (i, 0, 0)),
            pl.BlockSpec((STEP, ROWS, 2 * SIZE), lambda i: (i, 0, 0)),
            pl.BlockSpec((STEP, 2, SIZE, SIZE), lambda i: (i, 0, 0, 0)),
        ]
        + specs
        + [whole(near)]
        + [whole(t) for t in tables],
        out_specs=[dphase_spec, pl.BlockSpec((2, SIZE, SIZE), lambda i: (0, 0, 0))],
        out_shape=[dphase, shape(2, SIZE, SIZE)],
        scratch_shapes=[pltpu.VMEM((2, ROWS, SIZE), F32)],
        compiler_params=pltpu.CompilerParams(vmem_limit_bytes=VMEM_LIMIT),
        cost_estimate=pl.CostEstimate(flops=200_000_000_000, bytes_accessed=8_000_000, transcendentals=0),
        name="backward_wide" if wide else "backward_narrow",
    )(place, q, s, d, g, *sources, near, *tables)


def along(axis, shift):
    pairs = []
    for y in range(NY):
        for z in range(NZ):
            to = ((y + shift) % NY, z) if axis == "y" else (y, (z + shift) % NZ)
            pairs.append((y * NZ + z, to[0] * NZ + to[1]))
    return pairs


def send(x, axis, shift):
    return lax.ppermute(x, "chan", along(axis, shift))


def shards(alpha, images, modes, diversity, chan_of_frame):
    tables_f, tables_b = ([jnp.asarray(t) for t in group] for group in make_tables())
    here = lax.axis_index("chan")
    place = jnp.stack([here // NZ, here % NZ]).astype(jnp.int32)
    own_ids = jnp.zeros((8, SIZE), F32).at[0, :FRAMES].set(chan_of_frame[:, 0].astype(F32))

    phase = jnp.dot(alpha, modes, precision=lax.Precision.HIGH).reshape(FRAMES, PUP // 2, SIZE)
    axis = np.arange(PUP, dtype=np.float32) - (PUP - 1) / 2.0
    pupil = (axis[:, None] ** 2 + axis[None, :] ** 2 <= (PUP / 2.0) ** 2).astype(np.float32)
    pupil = jnp.asarray(pupil.reshape(PUP // 2, SIZE))
    extra = [diversity.reshape(PUP // 2, SIZE), own_ids]

    *narrow_kept, n0, n1, n2, n3 = forward(False, place, phase, pupil, extra, images, tables_f)
    narrow_in = [n0] + [send((n0, n1, n2, n3)[k], "y", k) for k in ORDER[1:]]
    *wide_kept, near, far = forward(True, place, phase, pupil, [], images, tables_f)
    near = near + send(far, "y", 2)
    wide_in = [near[0], send(near[1], "y", 1)]
    ids = jnp.concatenate([part[IDS, :FRAMES] for part in narrow_in]).astype(jnp.int32)

    keep, up, down = plain(
        sum_kernel,
        "sum_channels",
        [place, ids],
        narrow_in + wide_in,
        [shape(len(group) * Z_ROWS, SIZE) for group in (KEEP, UP, DOWN)],
        [pltpu.VMEM((32, 3 * GROUP, SIZE), F32), pltpu.VMEM((32, 8, SIZE), F32)],
    )
    up, down = send(up, "z", 1), send(down, "z", -1)
    far, back = plain(relay_kernel, "relay", [], [keep, up, down], [shape(Z_ROWS, SIZE)] * 2, [])
    far, back = send(far, "z", 3), send(back, "z", -3)
    (own,) = plain(object_kernel, "objects", [], [keep, up, down, far, back], [shape(F_ROWS, SIZE)], [])
    ahead, behind = send(own, "z", -3), send(own, "z", 3)
    up = send(jnp.concatenate([own, ahead, behind]), "z", 1)
    down = send(jnp.concatenate([own, behind]), "z", -1)
    *back, wide_own, near = plain(
        select_kernel,
        "select_objects",
        [place, ids],
        [own, ahead, behind, up, down],
        [shape(R_ROWS, SIZE)] * NY + [shape(2 * GROUP, SIZE), shape(2 * FRAMES + 8, SIZE)],
        [pltpu.VMEM((32, 2 * GROUP, SIZE), F32), pltpu.VMEM((32, 8, SIZE), F32), pltpu.VMEM((2 * GROUP, SIZE), F32)],
    )
    wide_back = [wide_own] + [send(wide_own, "y", k) for k in range(1, NY)]
    back = [back[0]] + [send(back[k], "y", k) for k in range(1, NY)]

    wide_dphase, wide_object = backward(True, place, *wide_kept, wide_back, near, None, tables_b)
    dphase, narrow_object = backward(False, place, *narrow_kept, back, near, wide_dphase, tables_b)
    gradient = lax.dot_general(dphase, modes, (((1,), (1,)), ((), ())), precision=lax.Precision.HIGH)
    return gradient, narrow_object[None], wide_object


def solution(mesh):
    placed = (
        P(("patch", "chan"), None),
        P(("patch", "chan"), None, None, None),
        P(),
        P(),
        P("chan", None),
    )
    return jax.shard_map(
        shards,
        mesh=mesh,
        in_specs=placed,
        out_specs=(
            P(("patch", "chan"), None),
            P(("patch", "chan"), None, None, None),
            P("patch", None, None),
        ),
        check_vma=False,
    )
```

time: 165 us -> 112 us (0.68)
  Pallas kernels: 43.2 us -> 22.5 us
  local copies, waits for them, and re-layouts: 12.7 us -> 3.36 us
  starting transfers between devices: 45.3 us -> 37.1 us
  waiting for transfers between devices: 48.9 us -> 42.5 us
  other arithmetic: 5.77 us -> 1.01 us
  matrix products: 7.63 us -> 3.13 us
    pallas_call x2, Pallas kernels: 16.8 us -> 8.57 us  [forward(): pl.pallas_call(functools.partial(forward_kernel, wide), grid=(FRAMES // S...]
    pallas_call x2, Pallas kernels: 19.5 us -> 11.3 us  [backward(): pl.pallas_call(functools.partial(backward_kernel, wide), grid=(FRAMES //...]
    ppermute x26 -> x19, starting transfers between devices: 45.3 us -> 37.1 us  [send(): return lax.ppermute(x, 'chan', along(axis, shift))]
    ppermute x26 -> x19, waiting for transfers between devices: 48.9 us -> 42.5 us  [send(): return lax.ppermute(x, 'chan', along(axis, shift))]
    slice x8 -> x0, local copies, waits for them, and re-layouts: 5.45 us -> none  [mirrored(): high = jnp.roll(jnp.flip(half[:, 1:HALF - 1], (1, 2)), 1, 2)]
    pallas_call x3 -> x4, Pallas kernels: 6.91 us -> 2.62 us  [plain(): pl.pallas_call(kernel, in_specs=[smem()] * len(smems) + [pl.BlockSpec(mem...]
    dot_general x1, matrix products: 4.98 us -> 1.43 us  [shards(): jnp.dot(alpha, modes, precision=lax.Precision.HIGH)]
    concatenate x4 -> x2, other arithmetic: 3.29 us -> 0.03 us  [the longest x1 0.02 us: shards(): up = send(jnp.concatenate([own, ahead, behind]), 'z', 1)]
  transfers between devices with their start and end apart: 26 -> 19, of which waited for: 16 -> 10; matrix products, arithmetic and copies ran while one was open for 2% -> 1% of each run, Pallas kernels for 5% -> 9%
where the time goes in v2:
time: 112 us; the launch traced here: 111 us
  waiting for transfers between devices  42.5 us (38%)
  starting transfers between devices  37.1 us (33%)
  Pallas kernels  22.5 us (20%)
  local copies, waits for them, and re-layouts  3.36 us (3%)
  matrix products  3.13 us (3%)
    ppermute x19, waiting for transfers between devices, send(): return lax.ppermute(x, 'chan', along(axis, shift))  42.5 us
    ppermute x19, starting transfers between devices, send(): return lax.ppermute(x, 'chan', along(axis, shift))  37.1 us
    pallas_call x2, Pallas kernels, backward(): pl.pallas_call(functools.partial(backward_kernel, wide), grid=(FRAMES //...  11.3 us
    pallas_call x2, Pallas kernels, forward(): pl.pallas_call(functools.partial(forward_kernel, wide), grid=(FRAMES // S...  8.57 us
    unnamed x49, local copies, waits for them, and re-layouts  3.34 us
    pallas_call x4, Pallas kernels, plain(): pl.pallas_call(kernel, in_specs=[smem()] * len(smems) + [pl.BlockSpec(mem...  2.62 us
  transfers between devices with their start and end apart: 19, of which 10 were waited for; matrix products, arithmetic and copies ran while one was open for 1% of the time, Pallas kernels for 9%

profile of v2, /device:TPU:2, one launch (start us, length us, event | category | flops | bytes accessed | tf_op | source)
XLA Modules:
  0.0 110.6 jit_solution(3862583103606665880)
XLA Ops:
  0.8 1.6 %copy-done = f32[150,4096]{1,0:T(8,128)S(1)} copy-done((f32[150,4096]{1,0:T(8,128)S(1)}, f32[150,4096]{1,0:T(8,128)}, u32[]{:S(2)}) %copy-start) | copy-done | bytes 2457624
  2.3 1.4 %convolution_bitcast_fusion = f32[2,8,32,128]{3,1,2,0:T(8,128)S(1)} fusion(f32[16,150]{1,0:T(8,128)} %param.26, f32[150,4096]{1,0:T(8,128)S(1)} %copy-done), kind=kOutput, calls=%fused_computation | convolution fusion | flops 58982400 | bytes 2729344 | tf_op jit(solution)/shard_map/dot_general | solution.py:510
  4.0 1.6 %copy-done.1 = f32[16,2,128,128]{3,2,1,0:T(8,128)S(1)} copy-done((f32[16,2,128,128]{3,2,1,0:T(8,128)S(1)}, f32[16,2,128,128]{3,2,1,0:T(8,128)}, u32[]{:S(2)}) %copy-start.1) | copy-done | bytes 2097176
  5.6 4.5 %forward_wide.1 = (f32[16,64,128]{2,1,0:T(8,128)S(1)}, f32[16,72,256]{2,1,0:T(8,128)S(1)}, f32[16,72,256]{2,1,0:T(8,128)S(1)}, f32[16,2,128,128]{3,2,1,0:T(8,128...) custom-call(s32[2]{0:T(128)S(1)} %pad_add_fusion.place, f32[16,32,128]{2,1,0:T(8,128)S(1)} %bitcast.25, ...), custom_call_target="tpu_custom_call" | custom-call | flops 199999995904 | bytes 8000000 | tf_op jit(solution)/shard_map/forward_wide/pallas_call | solution.py:242
  10.0 3.2 %collective-permute-start.3 = (f32[2,56,128]{2,1,0:T(8,128)}, f32[2,56,128]{2,1,0:T(8,128)}, u32[]{:S(2)}, u32[]{:S(2)}) collective-permute-start(f32[2,56,128]{2,1,0:T(8,128)} %get-tuple-element.53), channel_id=1, source_target_pairs={{0,16},{1,17},{2,18},{3,19},{4,20},{5,21},{6,22},{7,23},{8,24},{9,... | collective-permute-start | bytes 172040 | tf_op jit(solution)/shard_map/ppermute | solution.py:501
  13.3 4.1 %forward_narrow.1 = (f32[16,64,128]{2,1,0:T(8,128)S(1)}, f32[16,72,256]{2,1,0:T(8,128)S(1)}, f32[16,72,256]{2,1,0:T(8,128)S(1)}, f32[16,2,128,128]{3,2,1,0:T(8,1...) custom-call(s32[2]{0:T(128)S(1)} %pad_add_fusion.place, ...), custom_call_target="tpu_custom_call" | custom-call | flops 199999995904 | bytes 8000000 | tf_op jit(solution)/shard_map/forward_narrow/pallas_call | solution.py:242
  17.8 1.6 %collective-permute-start.1 = (f32[824,128]{1,0:T(8,128)S(1)}, f32[824,128]{1,0:T(8,128)S(1)}, u32[]{:S(2)}, u32[]{:S(2)}) collective-permute-start(f32[824,128]{1,0:T(8,128)S(1)} %get-tuple-element.50), channel_id=1, source_target_pairs={{0,8},{1,9},{2,10},{3,11},{4,12},{5,13},{6,14},{7,15},{8,16},{9,17... | collective-permute-start | bytes 1265672 | tf_op jit(solution)/shard_map/ppermute | solution.py:501
  19.4 1.7 %collective-permute-start.2 = (f32[824,128]{1,0:T(8,128)S(1)}, f32[824,128]{1,0:T(8,128)S(1)}, u32[]{:S(2)}, u32[]{:S(2)}) collective-permute-start(f32[824,128]{1,0:T(8,128)S(1)} %get-tuple-element.51), channel_id=1, source_target_pairs={{0,24},{1,25},{2,26},{3,27},{4,28},{5,29},{6,30},{7,31},{8,0},{9,1... | collective-permute-start | bytes 1265672 | tf_op jit(solution)/shard_map/ppermute | solution.py:501
  22.3 9.3 %collective-permute-done.refs_1_ = f32[824,128]{1,0:T(8,128)S(1)} collective-permute-done((f32[824,128]{1,0:T(8,128)S(1)}, f32[824,128]{1,0:T(8,128)S(1)}, u32[]{:S(2)}, u32[]{:S(2)}) %collective-permute-start) | collective-permute-done | bytes 421920 | tf_op jit(solution)/shard_map/ppermute | solution.py:501
  31.6 7.7 %collective-permute-done.1.refs_2_ = f32[824,128]{1,0:T(8,128)S(1)} collective-permute-done((f32[824,128]{1,0:T(8,128)S(1)}, f32[824,128]{1,0:T(8,128)S(1)}, u32[]{:S(2)}, u32[]{:S(2)}) %collective-permute-start.1) | collective-permute-done | bytes 421920 | tf_op jit(solution)/shard_map/ppermute | solution.py:501
  39.7 1.0 sum_channels.1
  40.8 2.2 %collective-permute-start.5 = (f32[648,128]{1,0:T(8,128)S(1)}, f32[648,128]{1,0:T(8,128)S(1)}, u32[]{:S(2)}, u32[]{:S(2)}) collective-permute-start(f32[648,128]{1,0:T(8,128)S(1)} %get-tuple-element.55), channel_id=1, source_target_pairs={{0,1},{1,2},{2,3},{3,4},{4,5},{5,6},{6,7},{7,0},{8,9},{9,10},{10,1... | collective-permute-start | bytes 995336 | tf_op jit(solution)/shard_map/ppermute | solution.py:501
  42.9 4.0 %collective-permute-start.6 = (f32[432,128]{1,0:T(8,128)S(1)}, f32[432,128]{1,0:T(8,128)S(1)}, u32[]{:S(2)}, u32[]{:S(2)}) collective-permute-start(f32[432,128]{1,0:T(8,128)S(1)} %get-tuple-element.56), channel_id=1, source_target_pairs={{0,7},{1,0},{2,1},{3,2},{4,3},{5,4},{6,5},{7,6},{8,15},{9,8},{10,9... | collective-permute-start | bytes 663560 | tf_op jit(solution)/shard_map/ppermute | solution.py:501
  47.0 4.7 %collective-permute-done.6.down = f32[432,128]{1,0:T(8,128)S(1)} collective-permute-done((f32[432,128]{1,0:T(8,128)S(1)}, f32[432,128]{1,0:T(8,128)S(1)}, u32[]{:S(2)}, u32[]{:S(2)}) %collective-permute-start.6) | collective-permute-done | bytes 221216 | tf_op jit(solution)/shard_map/ppermute | solution.py:501
  51.7 3.0 %collective-permute-done.5.up = f32[648,128]{1,0:T(8,128)S(1)} collective-permute-done((f32[648,128]{1,0:T(8,128)S(1)}, f32[648,128]{1,0:T(8,128)S(1)}, u32[]{:S(2)}, u32[]{:S(2)}) %collective-permute-start.5) | collective-permute-done | bytes 331808 | tf_op jit(solution)/shard_map/ppermute | solution.py:501
  54.7 2.3 %collective-permute-start.7 = (f32[216,128]{1,0:T(8,128)S(1)}, f32[216,128]{1,0:T(8,128)S(1)}, u32[]{:S(2)}, u32[]{:S(2)}) collective-permute-start(f32[216,128]{1,0:T(8,128)S(1)} %get-tuple-element.57), channel_id=1, source_target_pairs={{0,3},{1,4},{2,5},{3,6},{4,7},{5,0},{6,1},{7,2},{8,11},{9,12},{10,... | collective-permute-start | bytes 331784 | tf_op jit(solution)/shard_map/ppermute | solution.py:501
  57.0 2.8 %collective-permute-start.8 = (f32[216,128]{1,0:T(8,128)S(1)}, f32[216,128]{1,0:T(8,128)S(1)}, u32[]{:S(2)}, u32[]{:S(2)}) collective-permute-start(f32[216,128]{1,0:T(8,128)S(1)} %get-tuple-element.58), channel_id=1, source_target_pairs={{0,5},{1,6},{2,7},{3,0},{4,1},{5,2},{6,3},{7,4},{8,13},{9,14},{10,... | collective-permute-start | bytes 331784 | tf_op jit(solution)/shard_map/ppermute | solution.py:501
  59.8 5.4 %collective-permute-done.7.far = f32[216,128]{1,0:T(8,128)S(1)} collective-permute-done((f32[216,128]{1,0:T(8,128)S(1)}, f32[216,128]{1,0:T(8,128)S(1)}, u32[]{:S(2)}, u32[]{:S(2)}) %collective-permute-start.7) | collective-permute-done | bytes 110624 | tf_op jit(solution)/shard_map/ppermute | solution.py:501
  65.2 4.9 %collective-permute-start.10 = (f32[144,128]{1,0:T(8,128)S(1)}, f32[144,128]{1,0:T(8,128)S(1)}, u32[]{:S(2)}, u32[]{:S(2)}) collective-permute-start(f32[144,128]{1,0:T(8,128)S(1)} %objects.1.own), channel_id=1, source_target_pairs={{0,3},{1,4},{2,5},{3,6},{4,7},{5,0},{6,1},{7,2},{8,11},{9,12},{10,... | collective-permute-start | bytes 221192 | tf_op jit(solution)/shard_map/ppermute | solution.py:501
  70.7 3.1 %collective-permute-done.10.behind = f32[144,128]{1,0:T(8,128)S(1)} collective-permute-done((f32[144,128]{1,0:T(8,128)S(1)}, f32[144,128]{1,0:T(8,128)S(1)}, u32[]{:S(2)}, u32[]{:S(2)}) %collective-permute-start.10) | collective-permute-done | bytes 73760 | tf_op jit(solution)/shard_map/ppermute | solution.py:501
  73.8 3.4 %collective-permute-done.9.ahead = f32[144,128]{1,0:T(8,128)S(1)} collective-permute-done((f32[144,128]{1,0:T(8,128)S(1)}, f32[144,128]{1,0:T(8,128)S(1)}, u32[]{:S(2)}, u32[]{:S(2)}) %collective-permute-start.9) | collective-permute-done | bytes 73760 | tf_op jit(solution)/shard_map/ppermute | solution.py:501
  77.3 3.7 %collective-permute-start.11 = (f32[432,128]{1,0:T(8,128)S(1)}, f32[432,128]{1,0:T(8,128)S(1)}, u32[]{:S(2)}, u32[]{:S(2)}) collective-permute-start(f32[432,128]{1,0:T(8,128)S(1)} %pad_maximum_fusion), channel_id=1, source_target_pairs={{0,1},{1,2},{2,3},{3,4},{4,5},{5,6},{6,7},{7,0},{8,9},{9,10},{10,1... | collective-permute-start | bytes 663560 | tf_op jit(solution)/shard_map/ppermute | solution.py:501
  81.5 4.7 %collective-permute-done.12.down = f32[288,128]{1,0:T(8,128)S(1)} collective-permute-done((f32[288,128]{1,0:T(8,128)S(1)}, f32[288,128]{1,0:T(8,128)S(1)}, u32[]{:S(2)}, u32[]{:S(2)}) %collective-permute-start.12) | collective-permute-done | bytes 147488 | tf_op jit(solution)/shard_map/ppermute | solution.py:501
  86.2 1.5 %select_objects.1 = (f32[544,128]{1,0:T(8,128)S(1)}, f32[544,128]{1,0:T(8,128)}, f32[544,128]{1,0:T(8,128)}, f32[544,128]{1,0:T(8,128)}, f32[32,128]{1,0:T(8,128)S(1)}, /*index=5*/f32[40,128]{1,0:T(8,128)S(1)}) custom-call(s32[2]{0:T(128)S(1)} %pad_add_fusion.place, s32[64]{0:T(128)S(1)} %maximum_convert_fusion.ids, f32[144,128]{1,0:T(8,128)S(1)} %objects.1.own, ...), custom_call_target="tpu_custom_call" | custom-call | tf_op jit(solution)/shard_map/select_objects/pallas_call | solution.py:361
  88.6 1.7 %collective-permute-start.17 = (f32[32,128]{1,0:T(8,128)S(1)}, f32[32,128]{1,0:T(8,128)S(1)}, u32[]{:S(2)}, u32[]{:S(2)}) collective-permute-start(f32[32,128]{1,0:T(8,128)S(1)} %get-tuple-element.67.refs_0_), channel_id=1, source_target_pairs={{0,16},{1,17},{2,18},{3,19},{4,20},{5,21},{6,22},{7,23},{8,24},{9,... | collective-permute-start | bytes 49160 | tf_op jit(solution)/shard_map/ppermute | solution.py:501
  90.4 1.7 %collective-permute-start.13 = (f32[544,128]{1,0:T(8,128)}, f32[544,128]{1,0:T(8,128)}, u32[]{:S(2)}, u32[]{:S(2)}) collective-permute-start(f32[544,128]{1,0:T(8,128)} %get-tuple-element.60), channel_id=1, source_target_pairs={{0,8},{1,9},{2,10},{3,11},{4,12},{5,13},{6,14},{7,15},{8,16},{9,17... | collective-permute-start | bytes 835592 | tf_op jit(solution)/shard_map/ppermute | solution.py:501
  92.1 3.0 %collective-permute-start.14 = (f32[544,128]{1,0:T(8,128)}, f32[544,128]{1,0:T(8,128)}, u32[]{:S(2)}, u32[]{:S(2)}) collective-permute-start(f32[544,128]{1,0:T(8,128)} %get-tuple-element.61), channel_id=1, source_target_pairs={{0,16},{1,17},{2,18},{3,19},{4,20},{5,21},{6,22},{7,23},{8,24},{9,... | collective-permute-start | bytes 835592 | tf_op jit(solution)/shard_map/ppermute | solution.py:501
  95.1 1.5 %collective-permute-start.15 = (f32[544,128]{1,0:T(8,128)}, f32[544,128]{1,0:T(8,128)}, u32[]{:S(2)}, u32[]{:S(2)}) collective-permute-start(f32[544,128]{1,0:T(8,128)} %get-tuple-element.62), channel_id=1, source_target_pairs={{0,24},{1,25},{2,26},{3,27},{4,28},{5,29},{6,30},{7,31},{8,0},{9,1... | collective-permute-start | bytes 835592 | tf_op jit(solution)/shard_map/ppermute | solution.py:501
  96.7 5.5 %backward_wide.1 = (f32[16,32,128]{2,1,0:T(8,128)S(1)}, f32[2,128,128]{2,1,0:T(8,128)}) custom-call(s32[2]{0:T(128)S(1)} %pad_add_fusion.place, f32[16,64,128]{2,1,0:T(8,128)S(1)} %get-tuple-element.63.q_ref, f32[16,72,256]{2,1,0:T(8,128)S(1)} %get-tuple-element.64.s_ref, f32[16,72,256]{2,1,0:T(8,128)S(1)} %get-tuple-element.65.d_ref, ...), custom_call_target="tpu_custom_call" | custom-call | flops 199999995904 | bytes 8000000 | tf_op jit(solution)/shard_map/backward_wide/pallas_call | solution.py:469
  102.2 1.0 collective-permute-done.14.refs_2_.refs_6_
  103.2 5.8 %backward_narrow.1 = (f32[16,4096]{1,0:T(8,128)S(1)}, f32[2,128,128]{2,1,0:T(8,128)}) custom-call(s32[2]{0:T(128)S(1)} %pad_add_fusion.place, f32[16,64,128]{2,1,0:T(8,128)S(1)} %get-tuple-element.44.q_ref, f32[16,72,256]{2,1,0:T(8,128)S(1)} %get-tuple-element.45.s_ref, f32[16,72,256]{2,1,0:T(8,128)S(1)} %get-tuple-element.46.d_ref, ...), custom_call_target="tpu_custom_call" | custom-call | flops 199999995904 | bytes 8000000 | tf_op jit(solution)/shard_map/backward_narrow/pallas_call | solution.py:469
  108.9 1.7 %fusion = f32[16,150]{1,0:T(8,128)} fusion(f32[16,4096]{1,0:T(8,128)S(1)} %get-tuple-element.70, f32[150,4096]{1,0:T(8,128)S(1)} %copy-done), kind=kOutput, calls=%fused_computation.12 | convolution fusion | flops 58982400 | bytes 2729344 | tf_op jit(solution)/shard_map/dot_general | solution.py:551
  (77 shorter events, 4.4 us)
Async XLA Ops:
  5.6 7.7 %copy-start.23 = (s32[16,1]{0,1:T(1,128)S(1)}, s32[16,1]{0,1:T(1,128)}, u32[]{:S(2)}) copy-start(s32[16,1]{0,1:T(1,128)} %param.30) | copy-start | bytes 196
  5.6 7.7 %copy-start.2 = (f32[16,2,128,128]{3,2,1,0:T(8,128)S(1)}, f32[16,2,128,128]{3,2,1,0:T(8,128)}, u32[]{:S(2)}) copy-start(f32[16,2,128,128]{3,2,1,0:T(8,128)} %rest_0_.1) | copy-start | bytes 6291460
  5.6 7.7 %copy-start.3 = (f32[4096]{0:T(1024)S(1)}, f32[4096]{0:T(1024)}, u32[]{:S(2)}) copy-start(f32[4096]{0:T(1024)} %param.29) | copy-start | bytes 49156
  10.0 11.0 %collective-permute-start.3 = (f32[2,56,128]{2,1,0:T(8,128)}, f32[2,56,128]{2,1,0:T(8,128)}, u32[]{:S(2)}, u32[]{:S(2)}) collective-permute-start(f32[2,56,128]{2,1,0:T(8,128)} %get-tuple-element.53), channel_id=1, source_target_pairs={{0,16},{1,17},{2,18},{3,19},{4,20},{5,21},{6,22},{7,23},{8,24},{9,... | collective-permute-start | bytes 172040 | tf_op jit(solution)/shard_map/ppermute | solution.py:501
  17.4 14.2 %collective-permute-start = (f32[824,128]{1,0:T(8,128)S(1)}, f32[824,128]{1,0:T(8,128)S(1)}, u32[]{:S(2)}, u32[]{:S(2)}) collective-permute-start(f32[824,128]{1,0:T(8,128)S(1)} %get-tuple-element.49), channel_id=1, source_target_pairs={{0,16},{1,17},{2,18},{3,19},{4,20},{5,21},{6,22},{7,23},{8,24},{9,... | collective-permute-start | bytes 1265672 | tf_op jit(solution)/shard_map/ppermute | solution.py:501
  17.8 21.5 %collective-permute-start.1 = (f32[824,128]{1,0:T(8,128)S(1)}, f32[824,128]{1,0:T(8,128)S(1)}, u32[]{:S(2)}, u32[]{:S(2)}) collective-permute-start(f32[824,128]{1,0:T(8,128)S(1)} %get-tuple-element.50), channel_id=1, source_target_pairs={{0,8},{1,9},{2,10},{3,11},{4,12},{5,13},{6,14},{7,15},{8,16},{9,17... | collective-permute-start | bytes 1265672 | tf_op jit(solution)/shard_map/ppermute | solution.py:501
  19.4 19.9 %collective-permute-start.2 = (f32[824,128]{1,0:T(8,128)S(1)}, f32[824,128]{1,0:T(8,128)S(1)}, u32[]{:S(2)}, u32[]{:S(2)}) collective-permute-start(f32[824,128]{1,0:T(8,128)S(1)} %get-tuple-element.51), channel_id=1, source_target_pairs={{0,24},{1,25},{2,26},{3,27},{4,28},{5,29},{6,30},{7,31},{8,0},{9,1... | collective-permute-start | bytes 1265672 | tf_op jit(solution)/shard_map/ppermute | solution.py:501
  21.9 17.8 %collective-permute-start.4 = (f32[56,128]{1,0:T(8,128)S(1)}, f32[56,128]{1,0:T(8,128)S(1)}, u32[]{:S(2)}, u32[]{:S(2)}) collective-permute-start(f32[56,128]{1,0:T(8,128)S(1)} %get-tuple-element.73), channel_id=1, source_target_pairs={{0,8},{1,9},{2,10},{3,11},{4,12},{5,13},{6,14},{7,15},{8,16},{9,17... | collective-permute-start | bytes 86024 | tf_op jit(solution)/shard_map/ppermute | solution.py:501
  39.7 56.9 %copy-start.4 = (bf16[256,256]{1,0:T(8,128)(2,1)S(1)}, bf16[256,256]{1,0:T(8,128)(2,1)}, u32[]{:S(2)}) copy-start(bf16[256,256]{1,0:T(8,128)(2,1)} %constant.104.clone.refs_6_.refs_11_) | copy-start | bytes 393220
  39.7 56.9 %copy-start.5 = (bf16[256,256]{1,0:T(8,128)(2,1)S(1)}, bf16[256,256]{1,0:T(8,128)(2,1)}, u32[]{:S(2)}) copy-start(bf16[256,256]{1,0:T(8,128)(2,1)} %constant.103.clone.refs_5_.refs_10_) | copy-start | bytes 393220
  39.7 56.9 %copy-start.11 = (bf16[256,128]{1,0:T(8,128)(2,1)S(1)}, bf16[256,128]{1,0:T(8,128)(2,1)}, u32[]{:S(2)}) copy-start(bf16[256,128]{1,0:T(8,128)(2,1)} %constant.110.clone.refs_12_.refs_17_) | copy-start | bytes 196612
  39.7 56.9 %copy-start.12 = (bf16[256,128]{1,0:T(8,128)(2,1)S(1)}, bf16[256,128]{1,0:T(8,128)(2,1)}, u32[]{:S(2)}) copy-start(bf16[256,128]{1,0:T(8,128)(2,1)} %constant.109.clone.refs_11_.refs_16_) | copy-start | bytes 196612
  39.7 56.9 %copy-start.13 = (bf16[128,256]{1,0:T(8,128)(2,1)S(1)}, bf16[128,256]{1,0:T(8,128)(2,1)}, u32[]{:S(2)}) copy-start(bf16[128,256]{1,0:T(8,128)(2,1)} %constant.108.clone.refs_10_.refs_15_) | copy-start | bytes 196612
  39.7 56.9 %copy-start.14 = (bf16[128,256]{1,0:T(8,128)(2,1)S(1)}, bf16[128,256]{1,0:T(8,128)(2,1)}, u32[]{:S(2)}) copy-start(bf16[128,256]{1,0:T(8,128)(2,1)} %constant.107.clone.refs_9_.refs_14_) | copy-start | bytes 196612
  39.7 56.9 %copy-start.15 = (bf16[128,144]{1,0:T(8,128)(2,1)S(1)}, bf16[128,144]{1,0:T(8,128)(2,1)}, u32[]{:S(2)}) copy-start(bf16[128,144]{1,0:T(8,128)(2,1)} %constant.106.clone.refs_8_.refs_13_) | copy-start | bytes 110596
  39.7 56.9 %copy-start.16 = (bf16[128,144]{1,0:T(8,128)(2,1)S(1)}, bf16[128,144]{1,0:T(8,128)(2,1)}, u32[]{:S(2)}) copy-start(bf16[128,144]{1,0:T(8,128)(2,1)} %constant.105.clone.refs_7_.refs_12_) | copy-start | bytes 110596
  39.7 56.9 %copy-start.20 = (bf16[128,128]{1,0:T(8,128)(2,1)S(1)}, bf16[128,128]{1,0:T(8,128)(2,1)}, u32[]{:S(2)}) copy-start(bf16[128,128]{1,0:T(8,128)(2,1)} %constant.112.clone.refs_14_.refs_19_) | copy-start | bytes 98308
  39.7 56.9 %copy-start.21 = (bf16[128,128]{1,0:T(8,128)(2,1)S(1)}, bf16[128,128]{1,0:T(8,128)(2,1)}, u32[]{:S(2)}) copy-start(bf16[128,128]{1,0:T(8,128)(2,1)} %constant.111.clone.refs_13_.refs_18_) | copy-start | bytes 98308
  40.8 13.9 %collective-permute-start.5 = (f32[648,128]{1,0:T(8,128)S(1)}, f32[648,128]{1,0:T(8,128)S(1)}, u32[]{:S(2)}, u32[]{:S(2)}) collective-permute-start(f32[648,128]{1,0:T(8,128)S(1)} %get-tuple-element.55), channel_id=1, source_target_pairs={{0,1},{1,2},{2,3},{3,4},{4,5},{5,6},{6,7},{7,0},{8,9},{9,10},{10,1... | collective-permute-start | bytes 995336 | tf_op jit(solution)/shard_map/ppermute | solution.py:501
  42.9 8.7 %collective-permute-start.6 = (f32[432,128]{1,0:T(8,128)S(1)}, f32[432,128]{1,0:T(8,128)S(1)}, u32[]{:S(2)}, u32[]{:S(2)}) collective-permute-start(f32[432,128]{1,0:T(8,128)S(1)} %get-tuple-element.56), channel_id=1, source_target_pairs={{0,7},{1,0},{2,1},{3,2},{4,3},{5,4},{6,5},{7,6},{8,15},{9,8},{10,9... | collective-permute-start | bytes 663560 | tf_op jit(solution)/shard_map/ppermute | solution.py:501
  54.7 10.5 %collective-permute-start.7 = (f32[216,128]{1,0:T(8,128)S(1)}, f32[216,128]{1,0:T(8,128)S(1)}, u32[]{:S(2)}, u32[]{:S(2)}) collective-permute-start(f32[216,128]{1,0:T(8,128)S(1)} %get-tuple-element.57), channel_id=1, source_target_pairs={{0,3},{1,4},{2,5},{3,6},{4,7},{5,0},{6,1},{7,2},{8,11},{9,12},{10,... | collective-permute-start | bytes 331784 | tf_op jit(solution)/shard_map/ppermute | solution.py:501
  57.0 8.2 %collective-permute-start.8 = (f32[216,128]{1,0:T(8,128)S(1)}, f32[216,128]{1,0:T(8,128)S(1)}, u32[]{:S(2)}, u32[]{:S(2)}) collective-permute-start(f32[216,128]{1,0:T(8,128)S(1)} %get-tuple-element.58), channel_id=1, source_target_pairs={{0,5},{1,6},{2,7},{3,0},{4,1},{5,2},{6,3},{7,4},{8,13},{9,14},{10,... | collective-permute-start | bytes 331784 | tf_op jit(solution)/shard_map/ppermute | solution.py:501
  65.2 8.6 %collective-permute-start.10 = (f32[144,128]{1,0:T(8,128)S(1)}, f32[144,128]{1,0:T(8,128)S(1)}, u32[]{:S(2)}, u32[]{:S(2)}) collective-permute-start(f32[144,128]{1,0:T(8,128)S(1)} %objects.1.own), channel_id=1, source_target_pairs={{0,3},{1,4},{2,5},{3,6},{4,7},{5,0},{6,1},{7,2},{8,11},{9,12},{10,... | collective-permute-start | bytes 221192 | tf_op jit(solution)/shard_map/ppermute | solution.py:501
  70.1 7.1 %collective-permute-start.9 = (f32[144,128]{1,0:T(8,128)S(1)}, f32[144,128]{1,0:T(8,128)S(1)}, u32[]{:S(2)}, u32[]{:S(2)}) collective-permute-start(f32[144,128]{1,0:T(8,128)S(1)} %objects.1.own), channel_id=1, source_target_pairs={{0,5},{1,6},{2,7},{3,0},{4,1},{5,2},{6,3},{7,4},{8,13},{9,14},{10,... | collective-permute-start | bytes 221192 | tf_op jit(solution)/shard_map/ppermute | solution.py:501
  77.3 8.9 %collective-permute-start.11 = (f32[432,128]{1,0:T(8,128)S(1)}, f32[432,128]{1,0:T(8,128)S(1)}, u32[]{:S(2)}, u32[]{:S(2)}) collective-permute-start(f32[432,128]{1,0:T(8,128)S(1)} %pad_maximum_fusion), channel_id=1, source_target_pairs={{0,1},{1,2},{2,3},{3,4},{4,5},{5,6},{6,7},{7,0},{8,9},{9,10},{10,1... | collective-permute-start | bytes 663560 | tf_op jit(solution)/shard_map/ppermute | solution.py:501
  81.0 5.2 %collective-permute-start.12 = (f32[288,128]{1,0:T(8,128)S(1)}, f32[288,128]{1,0:T(8,128)S(1)}, u32[]{:S(2)}, u32[]{:S(2)}) collective-permute-start(f32[288,128]{1,0:T(8,128)S(1)} %pad_maximum_fusion.1), channel_id=1, source_target_pairs={{0,7},{1,0},{2,1},{3,2},{4,3},{5,4},{6,5},{7,6},{8,15},{9,8},{10,9... | collective-permute-start | bytes 442376 | tf_op jit(solution)/shard_map/ppermute | solution.py:501
  87.8 7.3 %collective-permute-start.18 = (f32[32,128]{1,0:T(8,128)S(1)}, f32[32,128]{1,0:T(8,128)S(1)}, u32[]{:S(2)}, u32[]{:S(2)}) collective-permute-start(f32[32,128]{1,0:T(8,128)S(1)} %get-tuple-element.67.refs_0_), channel_id=1, source_target_pairs={{0,24},{1,25},{2,26},{3,27},{4,28},{5,29},{6,30},{7,31},{8,0},{9,1... | collective-permute-start | bytes 49160 | tf_op jit(solution)/shard_map/ppermute | solution.py:501
  88.6 8.0 %collective-permute-start.17 = (f32[32,128]{1,0:T(8,128)S(1)}, f32[32,128]{1,0:T(8,128)S(1)}, u32[]{:S(2)}, u32[]{:S(2)}) collective-permute-start(f32[32,128]{1,0:T(8,128)S(1)} %get-tuple-element.67.refs_0_), channel_id=1, source_target_pairs={{0,16},{1,17},{2,18},{3,19},{4,20},{5,21},{6,22},{7,23},{8,24},{9,... | collective-permute-start | bytes 49160 | tf_op jit(solution)/shard_map/ppermute | solution.py:501
  90.3 6.2 %collective-permute-start.16 = (f32[32,128]{1,0:T(8,128)S(1)}, f32[32,128]{1,0:T(8,128)S(1)}, u32[]{:S(2)}, u32[]{:S(2)}) collective-permute-start(f32[32,128]{1,0:T(8,128)S(1)} %get-tuple-element.67.refs_0_), channel_id=1, source_target_pairs={{0,8},{1,9},{2,10},{3,11},{4,12},{5,13},{6,14},{7,15},{8,16},{9,17... | collective-permute-start | bytes 49160 | tf_op jit(solution)/shard_map/ppermute | solution.py:501
  90.4 11.9 %collective-permute-start.13 = (f32[544,128]{1,0:T(8,128)}, f32[544,128]{1,0:T(8,128)}, u32[]{:S(2)}, u32[]{:S(2)}) collective-permute-start(f32[544,128]{1,0:T(8,128)} %get-tuple-element.60), channel_id=1, source_target_pairs={{0,8},{1,9},{2,10},{3,11},{4,12},{5,13},{6,14},{7,15},{8,16},{9,17... | collective-permute-start | bytes 835592 | tf_op jit(solution)/shard_map/ppermute | solution.py:501
  92.1 11.1 %collective-permute-start.14 = (f32[544,128]{1,0:T(8,128)}, f32[544,128]{1,0:T(8,128)}, u32[]{:S(2)}, u32[]{:S(2)}) collective-permute-start(f32[544,128]{1,0:T(8,128)} %get-tuple-element.61), channel_id=1, source_target_pairs={{0,16},{1,17},{2,18},{3,19},{4,20},{5,21},{6,22},{7,23},{8,24},{9,... | collective-permute-start | bytes 835592 | tf_op jit(solution)/shard_map/ppermute | solution.py:501
  95.1 8.1 %collective-permute-start.15 = (f32[544,128]{1,0:T(8,128)}, f32[544,128]{1,0:T(8,128)}, u32[]{:S(2)}, u32[]{:S(2)}) collective-permute-start(f32[544,128]{1,0:T(8,128)} %get-tuple-element.62), channel_id=1, source_target_pairs={{0,24},{1,25},{2,26},{3,27},{4,28},{5,29},{6,30},{7,31},{8,0},{9,1... | collective-permute-start | bytes 835592 | tf_op jit(solution)/shard_map/ppermute | solution.py:501
  (11 other events, 32.6 us)

commit v3 on v2

--- a/solution.py
+++ b/solution.py
@@ -21,13 +21,13 @@
 PRIOR_WEIGHT = 0.1
 F32 = jnp.float32
 BF16 = jnp.bfloat16
-VMEM_LIMIT = 12 * 1024 * 1024
-VMEM_SMALL = 6 * 1024 * 1024
+VMEM_LIMIT = 8 * 1024 * 1024
+VMEM_SMALL = 4 * 1024 * 1024
 EDGES = FRAMES * 3 * GROUP
 IDS = EDGES + FRAMES * 3
 Y_ROWS = IDS + 8
 W_ROWS = 56
-ORDER = (0, 2, 1, 3)
+BASE = (0, W_ROWS, 0, W_ROWS)
 Z_ROWS = 216
 F_ROWS = 144
 R_ROWS = (FRAMES + 1) * 2 * GROUP
@@ -150,8 +150,9 @@
 def forward_kernel(wide, place, phase_ref, pupil_ref, *rest):
     if not wide:
         diversity_ref, ids_ref, *rest = rest
-    im_ref, r1, r2, l1, l2, h1, h2, f1, f2, q_ref, s_ref, d_ref, g_ref, *rest = rest
-    outs, scr = rest[:-1], rest[-1]
+    else:
+        _, _, *rest = rest
+    im_ref, r1, r2, l1, l2, h1, h2, f1, f2, q_ref, s_ref, d_ref, g_ref, *outs, scr = rest
     step = pl.program_id(0)
     y = place[0]
     low = low_lanes(PUP // 2)
@@ -175,7 +176,7 @@
             gr, gi = g[:SIZE, lanes], g[SIZE:, lanes]
             g_ref[k, 0], g_ref[k, 1] = gr, gi
             power = gr * gr + gi * gi
-            powers.append(power / jnp.sum(power, keepdims=True))
+            powers.append(power * (1.0 / jnp.sum(power, keepdims=True)))
     images = [im_ref[k, 0] for k in range(STEP)]
     spectra = pair_spectra(powers + images, (h1, h2), (f1, f2))
 
@@ -200,27 +201,27 @@
             for shift in range(NY):
                 row = pl.multiple_of(GROUP * lax.rem(y + shift, NY), GROUP)
                 for c in range(3):
-                    at = pl.multiple_of(frame * 3 * GROUP + c * GROUP, GROUP)
+                    at = pl.multiple_of(BASE[shift] + frame * 3 * GROUP + c * GROUP, 8)
                     outs[shift][pl.ds(at, GROUP), :] = scr[c, pl.ds(row, GROUP), :]
-                    outs[shift][pl.ds(EDGES + 3 * frame + c, 1), :] = scr[c, 64:65, :]
+                    outs[shift][pl.ds(BASE[shift] + EDGES + 3 * frame + c, 1), :] = scr[c, 64:65, :]
 
     @pl.when(step == 0)
     def _():
         if not wide:
             for shift in range(NY):
-                outs[shift][IDS:, :] = ids_ref[...]
+                outs[shift][BASE[shift] + IDS :, :] = ids_ref[...]
 
     if wide:
 
         @pl.when(step == FRAMES // STEP - 1)
         def _():
             for shift in range(NY):
-                out = outs[shift // 2]
+                out = outs[shift]
                 row = pl.multiple_of(GROUP * lax.rem(y + shift, NY), GROUP)
                 for c in range(3):
-                    out[shift % 2, c * GROUP : (c + 1) * GROUP, :] = scr[c, pl.ds(row, GROUP), :]
-                    out[shift % 2, 3 * GROUP + c : 3 * GROUP + c + 1, :] = scr[c, 64:65, :]
-                out[shift % 2, 3 * GROUP + 3 :, :] = jnp.zeros((W_ROWS - 3 * GROUP - 3, SIZE), F32)
+                    out[c * GROUP : (c + 1) * GROUP, :] = scr[c, pl.ds(row, GROUP), :]
+                    out[3 * GROUP + c : 3 * GROUP + c + 1, :] = scr[c, 64:65, :]
+                out[3 * GROUP + 3 :, :] = jnp.zeros((W_ROWS - 3 * GROUP - 3, SIZE), F32)
 
 
 def smem():
@@ -238,19 +239,20 @@
 def forward(wide, place, phase, pupil, extra, images, tables):
     camera = 0 if wide else 1
     outs = [shape(FRAMES, PUP, 2 * PUP)] + [shape(FRAMES, ROWS, 2 * SIZE)] * 2 + [shape(FRAMES, 2, SIZE, SIZE)]
-    terms = [shape(2, W_ROWS, SIZE)] * 2 if wide else [shape(Y_ROWS, SIZE)] * NY
+    terms = [shape(W_ROWS if wide and not base else Y_ROWS + base, SIZE) for base in BASE]
     return pl.pallas_call(
         functools.partial(forward_kernel, wide),
         grid=(FRAMES // STEP,),
         in_specs=[smem(), pl.BlockSpec((STEP, PUP // 2, SIZE), lambda i: (i, 0, 0)), whole(pupil)]
-        + [whole(e) for e in extra]
+        + [pl.BlockSpec(memory_space=pl.ANY) if wide else whole(e) for e in extra]
         + [pl.BlockSpec((STEP, 1, SIZE, SIZE), lambda i: (i, camera, 0, 0))]
         + [whole(t) for t in tables],
         out_specs=[pl.BlockSpec((STEP, PUP, 2 * PUP), lambda i: (i, 0, 0))]
         + [pl.BlockSpec((STEP, ROWS, 2 * SIZE), lambda i: (i, 0, 0))] * 2
         + [pl.BlockSpec((STEP, 2, SIZE, SIZE), lambda i: (i, 0, 0, 0))]
-        + [whole(t) for t in terms],
+        + [pl.BlockSpec((W_ROWS, SIZE), lambda i: (0, 0)) if wide else whole(t) for t in terms],
         out_shape=outs + terms,
+        input_output_aliases={3: len(outs) + 1, 4: len(outs) + 3} if wide else {},
         scratch_shapes=[pltpu.VMEM((3, ROWS, SIZE), F32)],
         compiler_params=pltpu.CompilerParams(vmem_limit_bytes=VMEM_LIMIT),
         cost_estimate=pl.CostEstimate(flops=200_000_000_000, bytes_accessed=8_000_000, transcendentals=0),
@@ -258,21 +260,52 @@
     )(place, phase, pupil, *extra, images, *tables)
 
 
-UP, DOWN, KEEP = (1, 4, 6), (7, 2), (0, 3, 5)
-
-
-def sum_kernel(place, ids, *refs):
-    narrow, (w1, w2, *outs, acc, edge) = refs[:NY], refs[NY:]
-    z = place[1]
+UP, DOWN, KEEP = (1, 6, 4), (7, 2, 4), (0, 3, 5)
+Z_FIRST, F_FIRST = 112, 72
+UP_ROWS, DOWN_ROWS = 2 * Z_ROWS + Z_FIRST, 3 * Z_ROWS - Z_FIRST
+
+
+def number_copies(sources, bases, numbers, arrived):
+    return [
+        pltpu.make_async_copy(source.at[pl.ds(base + IDS, 8)], numbers.at[n], arrived.at[n])
+        for n, (source, base) in enumerate(zip(sources, bases, strict=True))
+    ]
+
+
+def add_frames(sources, bases, acc, edge, numbers):
+    for n, (source, base) in enumerate(zip(sources, bases, strict=True)):
+        for f in range(FRAMES):
+            k = numbers[n, 0, f].astype(jnp.int32)
+            at = base + f * 3 * GROUP
+            acc[k] += source[at : at + 3 * GROUP, :]
+            at = base + EDGES + 3 * f
+            edge[k, 0:3, :] += source[at : at + 3, :]
+
+
+def first_sum_kernel(n0, n2, acc, edge, numbers, arrived):
+    copies = number_copies((n0, n2), (BASE[0], BASE[2]), numbers, arrived)
+    for copy in copies:
+        copy.start()
     acc[...] = jnp.zeros_like(acc)
     edge[...] = jnp.zeros_like(edge)
-    for source in range(NY):
-        for f in range(FRAMES):
-            k = ids[source * FRAMES + f]
-            acc[k] += narrow[source][f * 3 * GROUP : (f + 1) * 3 * GROUP, :]
-            at = EDGES + 3 * f
-            edge[k, 0:3, :] += narrow[source][at : at + 3, :]
-    for out, group in zip(outs, (KEEP, UP, DOWN), strict=True):
+    for copy in copies:
+        copy.wait()
+    add_frames((n0, n2), (BASE[0], BASE[2]), acc, edge, numbers)
+
+
+def sum_kernel(place, first, first_edge, n1, n3, w0, w2, keep, up, down, acc, edge, block, total, numbers, arrived):
+    z = place[1]
+    copies = number_copies((n1, n3), (BASE[1], BASE[3]), numbers, arrived)
+    for copy in copies:
+        copy.start()
+    acc[...] = first[...]
+    edge[...] = first_edge[...]
+    total[...] = (w0[...] + w2[...]) + (n1[:W_ROWS, :] + n3[:W_ROWS, :])
+    for copy in copies:
+        copy.wait()
+    add_frames((n1, n3), (BASE[1], BASE[3]), acc, edge, numbers)
+
+    def pack(out, group):
         for n, shift in enumerate(group):
             to = lax.rem(z + shift, NZ)
             start = n * Z_ROWS
@@ -285,16 +318,25 @@
             for c in range(3):
                 for j in range(2):
                     row = pl.ds(GROUP * c + 2 * to + j, 1)
-                    out[at + 2 * c + j : at + 2 * c + j + 1, :] = w1[row, :] + w2[row, :]
+                    out[at + 2 * c + j : at + 2 * c + j + 1, :] = total[row, :]
             row = slice(3 * GROUP, 3 * GROUP + 3)
-            out[at + 6 : at + 9, :] = w1[row, :] + w2[row, :]
+            out[at + 6 : at + 9, :] = total[row, :]
             out[at + 9 : start + Z_ROWS, :] = jnp.zeros((Z_ROWS - OWN * (3 * GROUP + 3) - 9, SIZE), F32)
 
+    pack(keep, KEEP)
+    pack(up, UP[:2])
+    pack(down, DOWN[:2])
+    pack(block, UP[2:])
+    up[2 * Z_ROWS :, :] = block[:Z_FIRST, :]
+    down[2 * Z_ROWS :, :] = block[Z_FIRST:, :]
+
 
 def relay_kernel(keep, up, down, far, back):
-    one, two = slice(Z_ROWS, 2 * Z_ROWS), slice(2 * Z_ROWS, 3 * Z_ROWS)
-    far[...] = keep[one, :] + (up[one, :] + down[one, :])
-    back[...] = keep[two, :] + up[two, :]
+    end = 2 * Z_ROWS
+    far[:Z_FIRST, :] = keep[Z_ROWS : Z_ROWS + Z_FIRST, :] + (up[end:, :] + down[Z_ROWS : Z_ROWS + Z_FIRST, :])
+    far[Z_FIRST:, :] = keep[Z_ROWS + Z_FIRST : end, :] + down[Z_ROWS + Z_FIRST : end, :]
+    back[:Z_FIRST, :] = keep[end : end + Z_FIRST, :] + up[Z_ROWS : Z_ROWS + Z_FIRST, :]
+    back[Z_FIRST:, :] = keep[end + Z_FIRST :, :] + (up[Z_ROWS + Z_FIRST : end, :] + down[end:, :])
 
 
 def quotient(num_re, num_im, den):
@@ -327,9 +369,11 @@
 
 
 def select_kernel(place, ids, own, ahead, behind, up, down, *refs):
-    outs, (wide, near, objects, edge, total) = refs[:NY], refs[NY:]
+    outs, (wide, near, objects, edge, total, other) = refs[:NY], refs[NY:]
+    other[:F_FIRST, :] = up[2 * F_ROWS :, :]
+    other[F_FIRST:, :] = down[2 * F_ROWS :, :]
     y, z = place[0], place[1]
-    parts = ((0, own, 0), (3, ahead, 0), (5, behind, 0), (7, up, 0), (2, up, 1), (4, up, 2), (1, down, 0), (6, down, 1))
+    parts = ((0, own, 0), (3, ahead, 0), (5, behind, 0), (7, up, 0), (2, up, 1), (1, down, 0), (6, down, 1), (4, other, 0))
     for shift, part, n in parts:
         source = lax.rem(z + shift, NZ)
         start = n * F_ROWS
@@ -345,9 +389,9 @@
     wide[...] = total[...]
     for shift in range(NY):
         out = outs[shift]
-        source = ORDER.index((NY - shift) % NY)
+        start = (NY - shift) % NY * FRAMES
         for f in range(FRAMES):
-            out[f * 2 * GROUP : (f + 1) * 2 * GROUP, :] = objects[ids[source * FRAMES + f]]
+            out[f * 2 * GROUP : (f + 1) * 2 * GROUP, :] = objects[ids[start + f]]
         out[FRAMES * 2 * GROUP :, :] = objects[lax.rem(y + shift, NY) * NZ + z]
     for f in range(FRAMES):
         near[2 * f : 2 * f + 2, :] = edge[ids[f], 0:2, :]
@@ -357,7 +401,7 @@
     near[2 * FRAMES + 4 :, :] = jnp.zeros((4, SIZE), F32)
 
 
-def plain(kernel, name, smems, arrays, outs, scratch):
+def plain(kernel, name, smems, arrays, outs, scratch, cost=None):
     return pl.pallas_call(
         kernel,
         in_specs=[smem()] * len(smems) + [pl.BlockSpec(memory_space=pltpu.VMEM)] * len(arrays),
@@ -365,6 +409,7 @@
         out_shape=outs,
         scratch_shapes=scratch,
         compiler_params=pltpu.CompilerParams(vmem_limit_bytes=VMEM_SMALL),
+        cost_estimate=cost,
         name=name,
     )(*smems, *arrays)
 
@@ -514,34 +559,49 @@
     extra = [diversity.reshape(PUP // 2, SIZE), own_ids]
 
     *narrow_kept, n0, n1, n2, n3 = forward(False, place, phase, pupil, extra, images, tables_f)
-    narrow_in = [n0] + [send((n0, n1, n2, n3)[k], "y", k) for k in ORDER[1:]]
-    *wide_kept, near, far = forward(True, place, phase, pupil, [], images, tables_f)
-    near = near + send(far, "y", 2)
-    wide_in = [near[0], send(near[1], "y", 1)]
-    ids = jnp.concatenate([part[IDS, :FRAMES] for part in narrow_in]).astype(jnp.int32)
-
+    *wide_kept, w0, n1, w2, n3 = forward(True, place, phase, pupil, [n1, n3], images, tables_f)
+    n2 = send(n2, "y", 2)
+    reading = [pltpu.SMEM((2, 8, SIZE), F32), pltpu.SemaphoreType.DMA((2,))]
+    first, first_edge = plain(
+        first_sum_kernel,
+        "sum_first",
+        [],
+        [n0, n2],
+        [shape(32, 3 * GROUP, SIZE), shape(32, 8, SIZE)],
+        reading,
+        pl.CostEstimate(flops=200_000_000_000, bytes_accessed=2_000_000, transcendentals=0),
+    )
+    n1, n3 = send(n1, "y", 1), send(n3, "y", 3)
     keep, up, down = plain(
         sum_kernel,
         "sum_channels",
-        [place, ids],
-        narrow_in + wide_in,
-        [shape(len(group) * Z_ROWS, SIZE) for group in (KEEP, UP, DOWN)],
-        [pltpu.VMEM((32, 3 * GROUP, SIZE), F32), pltpu.VMEM((32, 8, SIZE), F32)],
+        [place],
+        [first, first_edge, n1, n3, w0, send(w2, "y", 2)],
+        [shape(rows, SIZE) for rows in (3 * Z_ROWS, UP_ROWS, DOWN_ROWS)],
+        [
+            pltpu.VMEM((32, 3 * GROUP, SIZE), F32),
+            pltpu.VMEM((32, 8, SIZE), F32),
+            pltpu.VMEM((Z_ROWS, SIZE), F32),
+            pltpu.VMEM((W_ROWS, SIZE), F32),
+            *reading,
+        ],
     )
+    ids = jnp.concatenate([n[base + IDS, :FRAMES] for n, base in zip((n0, n1, n2, n3), BASE, strict=True)])
+    ids = ids.astype(jnp.int32)
     up, down = send(up, "z", 1), send(down, "z", -1)
     far, back = plain(relay_kernel, "relay", [], [keep, up, down], [shape(Z_ROWS, SIZE)] * 2, [])
     far, back = send(far, "z", 3), send(back, "z", -3)
     (own,) = plain(object_kernel, "objects", [], [keep, up, down, far, back], [shape(F_ROWS, SIZE)], [])
     ahead, behind = send(own, "z", -3), send(own, "z", 3)
-    up = send(jnp.concatenate([own, ahead, behind]), "z", 1)
-    down = send(jnp.concatenate([own, behind]), "z", -1)
+    up = send(jnp.concatenate([own, ahead, behind[:F_FIRST]]), "z", 1)
+    down = send(jnp.concatenate([own, behind, ahead[F_FIRST:]]), "z", -1)
     *back, wide_own, near = plain(
         select_kernel,
         "select_objects",
         [place, ids],
         [own, ahead, behind, up, down],
         [shape(R_ROWS, SIZE)] * NY + [shape(2 * GROUP, SIZE), shape(2 * FRAMES + 8, SIZE)],
-        [pltpu.VMEM((32, 2 * GROUP, SIZE), F32), pltpu.VMEM((32, 8, SIZE), F32), pltpu.VMEM((2 * GROUP, SIZE), F32)],
+        [pltpu.VMEM((32, 2 * GROUP, SIZE), F32), pltpu.VMEM((32, 8, SIZE), F32), pltpu.VMEM((2 * GROUP, SIZE), F32), pltpu.VMEM((F_ROWS, SIZE), F32)],
     )
     wide_back = [wide_own] + [send(wide_own, "y", k) for k in range(1, NY)]
     back = [back[0]] + [send(back[k], "y", k) for k in range(1, NY)]

time: 112 us -> 108 us (0.964)
  waiting for transfers between devices: 42.5 us -> 35.7 us
  Pallas kernels: 22.5 us -> 26.6 us
  starting transfers between devices: 37.1 us -> 34.6 us
  local copies, waits for them, and re-layouts: 3.36 us -> 5.38 us
    ppermute x19 -> x18, waiting for transfers between devices: 42.5 us -> 35.7 us  [send(): return lax.ppermute(x, 'chan', along(axis, shift))]
    pallas_call x4 -> x5, Pallas kernels: 2.62 us -> 5.72 us  [plain(): pl.pallas_call(kernel, in_specs=[smem()] * len(smems) + [pl.BlockSpec(mem...]
    ppermute x19 -> x18, starting transfers between devices: 37.1 us -> 34.6 us  [send(): return lax.ppermute(x, 'chan', along(axis, shift))]
    squeeze x5 -> x4, local copies, waits for them, and re-layouts: 0.01 us -> 2.03 us  [shards(): n[base + IDS, :FRAMES]]
  transfers between devices with their start and end apart: 19 -> 18, of which waited for: 10 -> 12; matrix products, arithmetic and copies ran while one was open for 1% -> 2% of each run, Pallas kernels for 9% -> 11%
where the time goes in v3:
time: 108 us; the launch traced here: 107 us
  waiting for transfers between devices  35.7 us (33%)
  starting transfers between devices  34.6 us (32%)
  Pallas kernels  26.6 us (25%)
  local copies, waits for them, and re-layouts  5.38 us (5%)
  matrix products  3.14 us (3%)
    ppermute x18, waiting for transfers between devices, send(): return lax.ppermute(x, 'chan', along(axis, shift))  35.7 us
    ppermute x18, starting transfers between devices, send(): return lax.ppermute(x, 'chan', along(axis, shift))  34.6 us
    pallas_call x2, Pallas kernels, backward(): pl.pallas_call(functools.partial(backward_kernel, wide), grid=(FRAMES //...  11.2 us
    pallas_call x2, Pallas kernels, forward(): pl.pallas_call(functools.partial(forward_kernel, wide), grid=(FRAMES // S...  9.61 us
    pallas_call x5, Pallas kernels, plain(): pl.pallas_call(kernel, in_specs=[smem()] * len(smems) + [pl.BlockSpec(mem...  5.72 us
    unnamed x49, local copies, waits for them, and re-layouts  3.33 us
  transfers between devices with their start and end apart: 18, of which 12 were waited for; matrix products, arithmetic and copies ran while one was open for 2% of the time, Pallas kernels for 11%

profile of v3, /device:TPU:2, one launch (start us, length us, event | category | flops | bytes accessed | tf_op | source)
XLA Modules:
  0.0 106.7 jit_solution(657905068014657581)
XLA Ops:
  0.8 1.6 %copy-done = f32[150,4096]{1,0:T(8,128)S(1)} copy-done((f32[150,4096]{1,0:T(8,128)S(1)}, f32[150,4096]{1,0:T(8,128)}, u32[]{:S(2)}) %copy-start) | copy-done | bytes 2457624
  2.3 1.4 %convolution_bitcast_fusion = f32[2,8,32,128]{3,1,2,0:T(8,128)S(1)} fusion(f32[16,150]{1,0:T(8,128)} %param.26, f32[150,4096]{1,0:T(8,128)S(1)} %copy-done), kind=kOutput, calls=%fused_computation | convolution fusion | flops 58982400 | bytes 2729344 | tf_op jit(solution)/shard_map/dot_general | solution.py:555
  4.1 1.6 %copy-done.1 = f32[16,2,128,128]{3,2,1,0:T(8,128)S(1)} copy-done((f32[16,2,128,128]{3,2,1,0:T(8,128)S(1)}, f32[16,2,128,128]{3,2,1,0:T(8,128)}, u32[]{:S(2)}) %copy-start.1) | copy-done | bytes 2097176
  5.7 5.2 %forward_narrow.1 = (f32[16,64,128]{2,1,0:T(8,128)S(1)}, f32[16,72,256]{2,1,0:T(8,128)S(1)}, f32[16,72,256]{2,1,0:T(8,128)S(1)}, f32[16,2,128,128]{3,2,1,0:T(8,1...) custom-call(s32[2]{0:T(128)S(1)} %pad_add_fusion.place, ...), custom_call_target="tpu_custom_call" | custom-call | flops 199999995904 | bytes 8000000 | tf_op jit(solution)/shard_map/forward_narrow/pallas_call | solution.py:243
  10.8 3.2 %collective-permute-start.1 = (f32[824,128]{1,0:T(8,128)}, f32[824,128]{1,0:T(8,128)}, u32[]{:S(2)}, u32[]{:S(2)}) collective-permute-start(f32[824,128]{1,0:T(8,128)} %get-tuple-element.56), channel_id=1, source_target_pairs={{0,16},{1,17},{2,18},{3,19},{4,20},{5,21},{6,22},{7,23},{8,24},{9,... | collective-permute-start | bytes 1265672 | tf_op jit(solution)/shard_map/ppermute | solution.py:546
  14.0 4.5 %forward_wide.1 = (f32[16,64,128]{2,1,0:T(8,128)S(1)}, f32[16,72,256]{2,1,0:T(8,128)S(1)}, f32[16,72,256]{2,1,0:T(8,128)S(1)}, f32[16,2,128,128]{3,2,1,0:T(8,128...) custom-call(s32[2]{0:T(128)S(1)} %pad_add_fusion.place, ...), custom_call_target="tpu_custom_call", output_to_operand_aliasing={{5}: (3, {}), {7}: (4, {})} | custom-call | flops 199999995904 | bytes 8000000 | tf_op jit(solution)/shard_map/forward_wide/pallas_call | solution.py:243
  18.5 1.1 collective-permute-start.2
  21.2 4.0 %collective-permute-done.1.n2 = f32[824,128]{1,0:T(8,128)} collective-permute-done((f32[824,128]{1,0:T(8,128)}, f32[824,128]{1,0:T(8,128)}, u32[]{:S(2)}, u32[]{:S(2)}) %collective-permute-start.1) | collective-permute-done | bytes 421920 | tf_op jit(solution)/shard_map/ppermute | solution.py:546
  25.2 1.9 %sum_first.1 = (f32[32,48,128]{2,1,0:T(8,128)S(1)}, f32[32,8,128]{2,1,0:T(8,128)S(1)}) custom-call(f32[824,128]{1,0:T(8,128)S(1)} %get-tuple-element.52.n0, f32[824,128]{1,0:T(8,128)} %collective-permute-done.1.n2), custom_call_target="tpu_custom_call" | custom-call | flops 199999995904 | bytes 2000000 | tf_op jit(solution)/shard_map/sum_first/pallas_call | solution.py:405
  27.1 7.2 %collective-permute-done.3.w2 = f32[56,128]{1,0:T(8,128)} collective-permute-done((f32[56,128]{1,0:T(8,128)}, f32[56,128]{1,0:T(8,128)}, u32[]{:S(2)}, u32[]{:S(2)}) %collective-permute-start.3) | collective-permute-done | bytes 28704 | tf_op jit(solution)/shard_map/ppermute | solution.py:546
  34.6 2.2 %sum_channels.1 = (f32[648,128]{1,0:T(8,128)S(1)}, f32[544,128]{1,0:T(8,128)S(1)}, f32[536,128]{1,0:T(8,128)S(1)}) custom-call(s32[2]{0:T(128)S(1)} %pad_add_fusion.place, f32[32,48,128]{2,1,0:T(8,128)S(1)} %get-tuple-element.58.first, f32[32,8,128]{2,1,0:T(8,128)S(1)} %get-tuple-element.59.first_edge, f32[880,128]{1,0:T(8,128)} %collective-permute-done.n1, ...), custom_call_target="tpu_custom_call" | custom-call | tf_op jit(solution)/shard_map/sum_channels/pallas_call | solution.py:405
  36.8 2.0 %collective-permute-start.4 = (f32[544,128]{1,0:T(8,128)S(1)}, f32[544,128]{1,0:T(8,128)S(1)}, u32[]{:S(2)}, u32[]{:S(2)}) collective-permute-start(f32[544,128]{1,0:T(8,128)S(1)} %get-tuple-element.63), channel_id=1, source_target_pairs={{0,1},{1,2},{2,3},{3,4},{4,5},{5,6},{6,7},{7,0},{8,9},{9,10},{10,1... | collective-permute-start | bytes 835592 | tf_op jit(solution)/shard_map/ppermute | solution.py:546
  38.8 4.2 %collective-permute-start.5 = (f32[536,128]{1,0:T(8,128)S(1)}, f32[536,128]{1,0:T(8,128)S(1)}, u32[]{:S(2)}, u32[]{:S(2)}) collective-permute-start(f32[536,128]{1,0:T(8,128)S(1)} %get-tuple-element.64), channel_id=1, source_target_pairs={{0,7},{1,0},{2,1},{3,2},{4,3},{5,4},{6,5},{7,6},{8,15},{9,8},{10,9... | collective-permute-start | bytes 823304 | tf_op jit(solution)/shard_map/ppermute | solution.py:546
  43.0 4.8 %collective-permute-done.5.down = f32[536,128]{1,0:T(8,128)S(1)} collective-permute-done((f32[536,128]{1,0:T(8,128)S(1)}, f32[536,128]{1,0:T(8,128)S(1)}, u32[]{:S(2)}, u32[]{:S(2)}) %collective-permute-start.5) | collective-permute-done | bytes 274464 | tf_op jit(solution)/shard_map/ppermute | solution.py:546
  48.4 4.6 %collective-permute-start.6 = (f32[216,128]{1,0:T(8,128)S(1)}, f32[216,128]{1,0:T(8,128)S(1)}, u32[]{:S(2)}, u32[]{:S(2)}) collective-permute-start(f32[216,128]{1,0:T(8,128)S(1)} %get-tuple-element.65), channel_id=1, source_target_pairs={{0,3},{1,4},{2,5},{3,6},{4,7},{5,0},{6,1},{7,2},{8,11},{9,12},{10,... | collective-permute-start | bytes 331784 | tf_op jit(solution)/shard_map/ppermute | solution.py:546
  54.2 4.7 %collective-permute-done.6.far = f32[216,128]{1,0:T(8,128)S(1)} collective-permute-done((f32[216,128]{1,0:T(8,128)S(1)}, f32[216,128]{1,0:T(8,128)S(1)}, u32[]{:S(2)}, u32[]{:S(2)}) %collective-permute-start.6) | collective-permute-done | bytes 110624 | tf_op jit(solution)/shard_map/ppermute | solution.py:546
  58.8 4.5 %collective-permute-done.7.back = f32[216,128]{1,0:T(8,128)S(1)} collective-permute-done((f32[216,128]{1,0:T(8,128)S(1)}, f32[216,128]{1,0:T(8,128)S(1)}, u32[]{:S(2)}, u32[]{:S(2)}) %collective-permute-start.7) | collective-permute-done | bytes 110624 | tf_op jit(solution)/shard_map/ppermute | solution.py:546
  64.0 3.3 %collective-permute-start.9 = (f32[144,128]{1,0:T(8,128)S(1)}, f32[144,128]{1,0:T(8,128)S(1)}, u32[]{:S(2)}, u32[]{:S(2)}) collective-permute-start(f32[144,128]{1,0:T(8,128)S(1)} %objects.1.own), channel_id=1, source_target_pairs={{0,3},{1,4},{2,5},{3,6},{4,7},{5,0},{6,1},{7,2},{8,11},{9,12},{10,... | collective-permute-start | bytes 221192 | tf_op jit(solution)/shard_map/ppermute | solution.py:546
  68.0 1.9 %collective-permute-done.8.ahead = f32[144,128]{1,0:T(8,128)S(1)} collective-permute-done((f32[144,128]{1,0:T(8,128)S(1)}, f32[144,128]{1,0:T(8,128)S(1)}, u32[]{:S(2)}, u32[]{:S(2)}) %collective-permute-start.8) | collective-permute-done | bytes 73760 | tf_op jit(solution)/shard_map/ppermute | solution.py:546
  69.9 2.2 %collective-permute-done.9.behind = f32[144,128]{1,0:T(8,128)S(1)} collective-permute-done((f32[144,128]{1,0:T(8,128)S(1)}, f32[144,128]{1,0:T(8,128)S(1)}, u32[]{:S(2)}, u32[]{:S(2)}) %collective-permute-start.9) | collective-permute-done | bytes 73760 | tf_op jit(solution)/shard_map/ppermute | solution.py:546
  72.2 1.2 %collective-permute-start.10 = (f32[360,128]{1,0:T(8,128)S(1)}, f32[360,128]{1,0:T(8,128)S(1)}, u32[]{:S(2)}, u32[]{:S(2)}) collective-permute-start(f32[360,128]{1,0:T(8,128)S(1)} %get-tuple-element.82), channel_id=1, source_target_pairs={{0,1},{1,2},{2,3},{3,4},{4,5},{5,6},{6,7},{7,0},{8,9},{9,10},{10,1... | collective-permute-start | bytes 552968 | tf_op jit(solution)/shard_map/ppermute | solution.py:546
  73.4 2.1 %collective-permute-start.11 = (f32[360,128]{1,0:T(8,128)S(1)}, f32[360,128]{1,0:T(8,128)S(1)}, u32[]{:S(2)}, u32[]{:S(2)}) collective-permute-start(f32[360,128]{1,0:T(8,128)S(1)} %get-tuple-element.81), channel_id=1, source_target_pairs={{0,7},{1,0},{2,1},{3,2},{4,3},{5,4},{6,5},{7,6},{8,15},{9,8},{10,9... | collective-permute-start | bytes 552968 | tf_op jit(solution)/shard_map/ppermute | solution.py:546
  76.2 2.8 %collective-permute-done.10.up = f32[360,128]{1,0:T(8,128)S(1)} collective-permute-done((f32[360,128]{1,0:T(8,128)S(1)}, f32[360,128]{1,0:T(8,128)S(1)}, u32[]{:S(2)}, u32[]{:S(2)}) %collective-permute-start.10) | collective-permute-done | bytes 184352 | tf_op jit(solution)/shard_map/ppermute | solution.py:546
  79.0 1.5 %select_objects.1 = (f32[544,128]{1,0:T(8,128)S(1)}, f32[544,128]{1,0:T(8,128)}, f32[544,128]{1,0:T(8,128)}, f32[544,128]{1,0:T(8,128)}, f32[32,128]{1,0:T(8,128)S(1)}, /*index=5*/f32[40,128]{1,0:T(8,128)S(1)}) custom-call(s32[2]{0:T(128)S(1)} %pad_add_fusion.place, s32[64]{0:T(128)S(1)} %maximum_convert_fusion.ids, f32[144,128]{1,0:T(8,128)S(1)} %objects.1.own, ...), custom_call_target="tpu_custom_call" | custom-call | tf_op jit(solution)/shard_map/select_objects/pallas_call | solution.py:405
  80.5 2.5 %collective-permute-start.15 = (f32[32,128]{1,0:T(8,128)S(1)}, f32[32,128]{1,0:T(8,128)S(1)}, u32[]{:S(2)}, u32[]{:S(2)}) collective-permute-start(f32[32,128]{1,0:T(8,128)S(1)} %get-tuple-element.75.refs_0_), channel_id=1, source_target_pairs={{0,8},{1,9},{2,10},{3,11},{4,12},{5,13},{6,14},{7,15},{8,16},{9,17... | collective-permute-start | bytes 49160 | tf_op jit(solution)/shard_map/ppermute | solution.py:546
  83.1 2.9 %collective-permute-start.16 = (f32[32,128]{1,0:T(8,128)S(1)}, f32[32,128]{1,0:T(8,128)S(1)}, u32[]{:S(2)}, u32[]{:S(2)}) collective-permute-start(f32[32,128]{1,0:T(8,128)S(1)} %get-tuple-element.75.refs_0_), channel_id=1, source_target_pairs={{0,16},{1,17},{2,18},{3,19},{4,20},{5,21},{6,22},{7,23},{8,24},{9,... | collective-permute-start | bytes 49160 | tf_op jit(solution)/shard_map/ppermute | solution.py:546
  86.0 1.3 %collective-permute-start.17 = (f32[32,128]{1,0:T(8,128)S(1)}, f32[32,128]{1,0:T(8,128)S(1)}, u32[]{:S(2)}, u32[]{:S(2)}) collective-permute-start(f32[32,128]{1,0:T(8,128)S(1)} %get-tuple-element.75.refs_0_), channel_id=1, source_target_pairs={{0,24},{1,25},{2,26},{3,27},{4,28},{5,29},{6,30},{7,31},{8,0},{9,1... | collective-permute-start | bytes 49160 | tf_op jit(solution)/shard_map/ppermute | solution.py:546
  88.8 1.9 %collective-permute-start.14 = (f32[544,128]{1,0:T(8,128)}, f32[544,128]{1,0:T(8,128)}, u32[]{:S(2)}, u32[]{:S(2)}) collective-permute-start(f32[544,128]{1,0:T(8,128)} %get-tuple-element.70), channel_id=1, source_target_pairs={{0,24},{1,25},{2,26},{3,27},{4,28},{5,29},{6,30},{7,31},{8,0},{9,1... | collective-permute-start | bytes 835592 | tf_op jit(solution)/shard_map/ppermute | solution.py:546
  90.8 5.5 %backward_wide.1 = (f32[16,32,128]{2,1,0:T(8,128)S(1)}, f32[2,128,128]{2,1,0:T(8,128)}) custom-call(s32[2]{0:T(128)S(1)} %pad_add_fusion.place, f32[16,64,128]{2,1,0:T(8,128)S(1)} %get-tuple-element.71.q_ref, f32[16,72,256]{2,1,0:T(8,128)S(1)} %get-tuple-element.72.s_ref, f32[16,72,256]{2,1,0:T(8,128)S(1)} %get-tuple-element.73.d_ref, ...), custom_call_target="tpu_custom_call" | custom-call | flops 199999995904 | bytes 8000000 | tf_op jit(solution)/shard_map/backward_wide/pallas_call | solution.py:514
  96.3 2.1 %collective-permute-done.12.refs_1_.refs_5_ = f32[544,128]{1,0:T(8,128)} collective-permute-done((f32[544,128]{1,0:T(8,128)}, f32[544,128]{1,0:T(8,128)}, u32[]{:S(2)}, u32[]{:S(2)}) %collective-permute-start.12) | collective-permute-done | bytes 278560 | tf_op jit(solution)/shard_map/ppermute | solution.py:546
  99.3 5.7 %backward_narrow.1 = (f32[16,4096]{1,0:T(8,128)S(1)}, f32[2,128,128]{2,1,0:T(8,128)}) custom-call(s32[2]{0:T(128)S(1)} %pad_add_fusion.place, f32[16,64,128]{2,1,0:T(8,128)S(1)} %get-tuple-element.48.q_ref, f32[16,72,256]{2,1,0:T(8,128)S(1)} %get-tuple-element.49.s_ref, f32[16,72,256]{2,1,0:T(8,128)S(1)} %get-tuple-element.50.d_ref, ...), custom_call_target="tpu_custom_call" | custom-call | flops 199999995904 | bytes 8000000 | tf_op jit(solution)/shard_map/backward_narrow/pallas_call | solution.py:514
  105.0 1.7 %fusion.2 = f32[16,150]{1,0:T(8,128)} fusion(f32[16,4096]{1,0:T(8,128)S(1)} %get-tuple-element.78, f32[150,4096]{1,0:T(8,128)S(1)} %copy-done), kind=kOutput, calls=%fused_computation.12 | convolution fusion | flops 58982400 | bytes 2729344 | tf_op jit(solution)/shard_map/dot_general | solution.py:611
  (75 shorter events, 8.3 us)
Async XLA Ops:
  0.6 3.3 %copy-start.22 = (f32[32,128]{1,0:T(8,128)S(1)}, f32[32,128]{1,0:T(8,128)}, u32[]{:S(2)}) copy-start(f32[32,128]{1,0:T(8,128)} %constant.113.clone.pupil_ref) | copy-start | bytes 49156
  0.7 3.3 %copy-start.6 = (bf16[256,256]{1,0:T(8,128)(2,1)S(1)}, bf16[256,256]{1,0:T(8,128)(2,1)}, u32[]{:S(2)}) copy-start(bf16[256,256]{1,0:T(8,128)(2,1)} %constant.95.clone.rest_3_) | copy-start | bytes 393220
  0.7 3.3 %copy-start.17 = (bf16[128,256]{1,0:T(8,128)(2,1)S(1)}, bf16[128,256]{1,0:T(8,128)(2,1)}, u32[]{:S(2)}) copy-start(bf16[128,256]{1,0:T(8,128)(2,1)} %constant.96.clone.rest_4_) | copy-start | bytes 196612
  5.7 8.4 %copy-start.2 = (f32[16,2,128,128]{3,2,1,0:T(8,128)S(1)}, f32[16,2,128,128]{3,2,1,0:T(8,128)}, u32[]{:S(2)}) copy-start(f32[16,2,128,128]{3,2,1,0:T(8,128)} %rest_2_.3) | copy-start | bytes 6291460
  10.8 14.4 %collective-permute-start.1 = (f32[824,128]{1,0:T(8,128)}, f32[824,128]{1,0:T(8,128)}, u32[]{:S(2)}, u32[]{:S(2)}) collective-permute-start(f32[824,128]{1,0:T(8,128)} %get-tuple-element.56), channel_id=1, source_target_pairs={{0,16},{1,17},{2,18},{3,19},{4,20},{5,21},{6,22},{7,23},{8,24},{9,... | collective-permute-start | bytes 1265672 | tf_op jit(solution)/shard_map/ppermute | solution.py:546
  18.5 16.0 %collective-permute-start.2 = (f32[880,128]{1,0:T(8,128)}, f32[880,128]{1,0:T(8,128)}, u32[]{:S(2)}, u32[]{:S(2)}) collective-permute-start(f32[880,128]{1,0:T(8,128)} %get-tuple-element.57), channel_id=1, source_target_pairs={{0,24},{1,25},{2,26},{3,27},{4,28},{5,29},{6,30},{7,31},{8,0},{9,1... | collective-permute-start | bytes 1351688 | tf_op jit(solution)/shard_map/ppermute | solution.py:546
  19.5 14.9 %collective-permute-start = (f32[880,128]{1,0:T(8,128)}, f32[880,128]{1,0:T(8,128)}, u32[]{:S(2)}, u32[]{:S(2)}) collective-permute-start(f32[880,128]{1,0:T(8,128)} %get-tuple-element.55), channel_id=1, source_target_pairs={{0,8},{1,9},{2,10},{3,11},{4,12},{5,13},{6,14},{7,15},{8,16},{9,17... | collective-permute-start | bytes 1351688 | tf_op jit(solution)/shard_map/ppermute | solution.py:546
  20.5 13.9 %collective-permute-start.3 = (f32[56,128]{1,0:T(8,128)}, f32[56,128]{1,0:T(8,128)}, u32[]{:S(2)}, u32[]{:S(2)}) collective-permute-start(f32[56,128]{1,0:T(8,128)} %get-tuple-element.61), channel_id=1, source_target_pairs={{0,16},{1,17},{2,18},{3,19},{4,20},{5,21},{6,22},{7,23},{8,24},{9,... | collective-permute-start | bytes 86024 | tf_op jit(solution)/shard_map/ppermute | solution.py:546
  34.5 56.2 %copy-start.4 = (bf16[256,256]{1,0:T(8,128)(2,1)S(1)}, bf16[256,256]{1,0:T(8,128)(2,1)}, u32[]{:S(2)}) copy-start(bf16[256,256]{1,0:T(8,128)(2,1)} %constant.103.clone.refs_5_.refs_10_) | copy-start | bytes 393220
  34.5 56.2 %copy-start.5 = (bf16[256,256]{1,0:T(8,128)(2,1)S(1)}, bf16[256,256]{1,0:T(8,128)(2,1)}, u32[]{:S(2)}) copy-start(bf16[256,256]{1,0:T(8,128)(2,1)} %constant.104.clone.refs_6_.refs_11_) | copy-start | bytes 393220
  34.5 56.2 %copy-start.11 = (bf16[128,144]{1,0:T(8,128)(2,1)S(1)}, bf16[128,144]{1,0:T(8,128)(2,1)}, u32[]{:S(2)}) copy-start(bf16[128,144]{1,0:T(8,128)(2,1)} %constant.105.clone.refs_7_.refs_12_) | copy-start | bytes 110596
  34.5 56.2 %copy-start.12 = (bf16[128,144]{1,0:T(8,128)(2,1)S(1)}, bf16[128,144]{1,0:T(8,128)(2,1)}, u32[]{:S(2)}) copy-start(bf16[128,144]{1,0:T(8,128)(2,1)} %constant.106.clone.refs_8_.refs_13_) | copy-start | bytes 110596
  34.5 56.2 %copy-start.13 = (bf16[128,256]{1,0:T(8,128)(2,1)S(1)}, bf16[128,256]{1,0:T(8,128)(2,1)}, u32[]{:S(2)}) copy-start(bf16[128,256]{1,0:T(8,128)(2,1)} %constant.107.clone.refs_9_.refs_14_) | copy-start | bytes 196612
  34.5 56.2 %copy-start.14 = (bf16[128,256]{1,0:T(8,128)(2,1)S(1)}, bf16[128,256]{1,0:T(8,128)(2,1)}, u32[]{:S(2)}) copy-start(bf16[128,256]{1,0:T(8,128)(2,1)} %constant.108.clone.refs_10_.refs_15_) | copy-start | bytes 196612
  34.5 56.2 %copy-start.15 = (bf16[256,128]{1,0:T(8,128)(2,1)S(1)}, bf16[256,128]{1,0:T(8,128)(2,1)}, u32[]{:S(2)}) copy-start(bf16[256,128]{1,0:T(8,128)(2,1)} %constant.109.clone.refs_11_.refs_16_) | copy-start | bytes 196612
  34.5 56.2 %copy-start.16 = (bf16[256,128]{1,0:T(8,128)(2,1)S(1)}, bf16[256,128]{1,0:T(8,128)(2,1)}, u32[]{:S(2)}) copy-start(bf16[256,128]{1,0:T(8,128)(2,1)} %constant.110.clone.refs_12_.refs_17_) | copy-start | bytes 196612
  34.5 56.2 %copy-start.20 = (bf16[128,128]{1,0:T(8,128)(2,1)S(1)}, bf16[128,128]{1,0:T(8,128)(2,1)}, u32[]{:S(2)}) copy-start(bf16[128,128]{1,0:T(8,128)(2,1)} %constant.111.clone.refs_13_.refs_18_) | copy-start | bytes 98308
  34.5 56.2 %copy-start.21 = (bf16[128,128]{1,0:T(8,128)(2,1)S(1)}, bf16[128,128]{1,0:T(8,128)(2,1)}, u32[]{:S(2)}) copy-start(bf16[128,128]{1,0:T(8,128)(2,1)} %constant.112.clone.refs_14_.refs_19_) | copy-start | bytes 98308
  36.8 11.6 %collective-permute-start.4 = (f32[544,128]{1,0:T(8,128)S(1)}, f32[544,128]{1,0:T(8,128)S(1)}, u32[]{:S(2)}, u32[]{:S(2)}) collective-permute-start(f32[544,128]{1,0:T(8,128)S(1)} %get-tuple-element.63), channel_id=1, source_target_pairs={{0,1},{1,2},{2,3},{3,4},{4,5},{5,6},{6,7},{7,0},{8,9},{9,10},{10,1... | collective-permute-start | bytes 835592 | tf_op jit(solution)/shard_map/ppermute | solution.py:546
  38.8 9.0 %collective-permute-start.5 = (f32[536,128]{1,0:T(8,128)S(1)}, f32[536,128]{1,0:T(8,128)S(1)}, u32[]{:S(2)}, u32[]{:S(2)}) collective-permute-start(f32[536,128]{1,0:T(8,128)S(1)} %get-tuple-element.64), channel_id=1, source_target_pairs={{0,7},{1,0},{2,1},{3,2},{4,3},{5,4},{6,5},{7,6},{8,15},{9,8},{10,9... | collective-permute-start | bytes 823304 | tf_op jit(solution)/shard_map/ppermute | solution.py:546
  48.4 10.4 %collective-permute-start.6 = (f32[216,128]{1,0:T(8,128)S(1)}, f32[216,128]{1,0:T(8,128)S(1)}, u32[]{:S(2)}, u32[]{:S(2)}) collective-permute-start(f32[216,128]{1,0:T(8,128)S(1)} %get-tuple-element.65), channel_id=1, source_target_pairs={{0,3},{1,4},{2,5},{3,6},{4,7},{5,0},{6,1},{7,2},{8,11},{9,12},{10,... | collective-permute-start | bytes 331784 | tf_op jit(solution)/shard_map/ppermute | solution.py:546
  53.0 10.4 %collective-permute-start.7 = (f32[216,128]{1,0:T(8,128)S(1)}, f32[216,128]{1,0:T(8,128)S(1)}, u32[]{:S(2)}, u32[]{:S(2)}) collective-permute-start(f32[216,128]{1,0:T(8,128)S(1)} %get-tuple-element.66), channel_id=1, source_target_pairs={{0,5},{1,6},{2,7},{3,0},{4,1},{5,2},{6,3},{7,4},{8,13},{9,14},{10,... | collective-permute-start | bytes 331784 | tf_op jit(solution)/shard_map/ppermute | solution.py:546
  63.4 6.5 %collective-permute-start.8 = (f32[144,128]{1,0:T(8,128)S(1)}, f32[144,128]{1,0:T(8,128)S(1)}, u32[]{:S(2)}, u32[]{:S(2)}) collective-permute-start(f32[144,128]{1,0:T(8,128)S(1)} %objects.1.own), channel_id=1, source_target_pairs={{0,5},{1,6},{2,7},{3,0},{4,1},{5,2},{6,3},{7,4},{8,13},{9,14},{10,... | collective-permute-start | bytes 221192 | tf_op jit(solution)/shard_map/ppermute | solution.py:546
  64.0 8.1 %collective-permute-start.9 = (f32[144,128]{1,0:T(8,128)S(1)}, f32[144,128]{1,0:T(8,128)S(1)}, u32[]{:S(2)}, u32[]{:S(2)}) collective-permute-start(f32[144,128]{1,0:T(8,128)S(1)} %objects.1.own), channel_id=1, source_target_pairs={{0,3},{1,4},{2,5},{3,6},{4,7},{5,0},{6,1},{7,2},{8,11},{9,12},{10,... | collective-permute-start | bytes 221192 | tf_op jit(solution)/shard_map/ppermute | solution.py:546
  72.2 6.8 %collective-permute-start.10 = (f32[360,128]{1,0:T(8,128)S(1)}, f32[360,128]{1,0:T(8,128)S(1)}, u32[]{:S(2)}, u32[]{:S(2)}) collective-permute-start(f32[360,128]{1,0:T(8,128)S(1)} %get-tuple-element.82), channel_id=1, source_target_pairs={{0,1},{1,2},{2,3},{3,4},{4,5},{5,6},{6,7},{7,0},{8,9},{9,10},{10,1... | collective-permute-start | bytes 552968 | tf_op jit(solution)/shard_map/ppermute | solution.py:546
  73.4 5.6 %collective-permute-start.11 = (f32[360,128]{1,0:T(8,128)S(1)}, f32[360,128]{1,0:T(8,128)S(1)}, u32[]{:S(2)}, u32[]{:S(2)}) collective-permute-start(f32[360,128]{1,0:T(8,128)S(1)} %get-tuple-element.81), channel_id=1, source_target_pairs={{0,7},{1,0},{2,1},{3,2},{4,3},{5,4},{6,5},{7,6},{8,15},{9,8},{10,9... | collective-permute-start | bytes 552968 | tf_op jit(solution)/shard_map/ppermute | solution.py:546
  80.5 8.2 %collective-permute-start.15 = (f32[32,128]{1,0:T(8,128)S(1)}, f32[32,128]{1,0:T(8,128)S(1)}, u32[]{:S(2)}, u32[]{:S(2)}) collective-permute-start(f32[32,128]{1,0:T(8,128)S(1)} %get-tuple-element.75.refs_0_), channel_id=1, source_target_pairs={{0,8},{1,9},{2,10},{3,11},{4,12},{5,13},{6,14},{7,15},{8,16},{9,17... | collective-permute-start | bytes 49160 | tf_op jit(solution)/shard_map/ppermute | solution.py:546
  83.1 7.6 %collective-permute-start.16 = (f32[32,128]{1,0:T(8,128)S(1)}, f32[32,128]{1,0:T(8,128)S(1)}, u32[]{:S(2)}, u32[]{:S(2)}) collective-permute-start(f32[32,128]{1,0:T(8,128)S(1)} %get-tuple-element.75.refs_0_), channel_id=1, source_target_pairs={{0,16},{1,17},{2,18},{3,19},{4,20},{5,21},{6,22},{7,23},{8,24},{9,... | collective-permute-start | bytes 49160 | tf_op jit(solution)/shard_map/ppermute | solution.py:546
  86.0 4.7 %collective-permute-start.17 = (f32[32,128]{1,0:T(8,128)S(1)}, f32[32,128]{1,0:T(8,128)S(1)}, u32[]{:S(2)}, u32[]{:S(2)}) collective-permute-start(f32[32,128]{1,0:T(8,128)S(1)} %get-tuple-element.75.refs_0_), channel_id=1, source_target_pairs={{0,24},{1,25},{2,26},{3,27},{4,28},{5,29},{6,30},{7,31},{8,0},{9,1... | collective-permute-start | bytes 49160 | tf_op jit(solution)/shard_map/ppermute | solution.py:546
  87.3 11.1 %collective-permute-start.12 = (f32[544,128]{1,0:T(8,128)}, f32[544,128]{1,0:T(8,128)}, u32[]{:S(2)}, u32[]{:S(2)}) collective-permute-start(f32[544,128]{1,0:T(8,128)} %get-tuple-element.68), channel_id=1, source_target_pairs={{0,8},{1,9},{2,10},{3,11},{4,12},{5,13},{6,14},{7,15},{8,16},{9,17... | collective-permute-start | bytes 835592 | tf_op jit(solution)/shard_map/ppermute | solution.py:546
  88.0 10.4 %collective-permute-start.13 = (f32[544,128]{1,0:T(8,128)}, f32[544,128]{1,0:T(8,128)}, u32[]{:S(2)}, u32[]{:S(2)}) collective-permute-start(f32[544,128]{1,0:T(8,128)} %get-tuple-element.69), channel_id=1, source_target_pairs={{0,16},{1,17},{2,18},{3,19},{4,20},{5,21},{6,22},{7,23},{8,24},{9,... | collective-permute-start | bytes 835592 | tf_op jit(solution)/shard_map/ppermute | solution.py:546
  88.8 10.5 %collective-permute-start.14 = (f32[544,128]{1,0:T(8,128)}, f32[544,128]{1,0:T(8,128)}, u32[]{:S(2)}, u32[]{:S(2)}) collective-permute-start(f32[544,128]{1,0:T(8,128)} %get-tuple-element.70), channel_id=1, source_target_pairs={{0,24},{1,25},{2,26},{3,27},{4,28},{5,29},{6,30},{7,31},{8,0},{9,1... | collective-permute-start | bytes 835592 | tf_op jit(solution)/shard_map/ppermute | solution.py:546
  (10 other events, 27.9 us)

commit v4 on v3

--- a/solution.py
+++ b/solution.py
@@ -255,7 +255,7 @@
         input_output_aliases={3: len(outs) + 1, 4: len(outs) + 3} if wide else {},
         scratch_shapes=[pltpu.VMEM((3, ROWS, SIZE), F32)],
         compiler_params=pltpu.CompilerParams(vmem_limit_bytes=VMEM_LIMIT),
-        cost_estimate=pl.CostEstimate(flops=200_000_000_000, bytes_accessed=8_000_000, transcendentals=0),
+        cost_estimate=pl.CostEstimate(flops=4_000_000_000, bytes_accessed=8_000_000, transcendentals=0),
         name="forward_wide" if wide else "forward_narrow",
     )(place, phase, pupil, *extra, images, *tables)
 
@@ -528,7 +528,7 @@
         out_shape=[dphase, shape(2, SIZE, SIZE)],
         scratch_shapes=[pltpu.VMEM((2, ROWS, SIZE), F32)],
         compiler_params=pltpu.CompilerParams(vmem_limit_bytes=VMEM_LIMIT),
-        cost_estimate=pl.CostEstimate(flops=200_000_000_000, bytes_accessed=8_000_000, transcendentals=0),
+        cost_estimate=pl.CostEstimate(flops=4_000_000_000, bytes_accessed=8_000_000, transcendentals=0),
         name="backward_wide" if wide else "backward_narrow",
     )(place, q, s, d, g, *sources, near, *tables)
 
@@ -569,7 +569,7 @@
         [n0, n2],
         [shape(32, 3 * GROUP, SIZE), shape(32, 8, SIZE)],
         reading,
-        pl.CostEstimate(flops=200_000_000_000, bytes_accessed=2_000_000, transcendentals=0),
+        pl.CostEstimate(flops=4_000_000_000, bytes_accessed=2_000_000, transcendentals=0),
     )
     n1, n3 = send(n1, "y", 1), send(n3, "y", 3)
     keep, up, down = plain(

time: 108 us -> 104 us (0.963)
  Pallas kernels: 26.6 us -> 21.6 us
  waiting for transfers between devices: 35.7 us -> 39.2 us
  local copies, waits for them, and re-layouts: 5.38 us -> 3.35 us
    ppermute x18, waiting for transfers between devices: 35.7 us -> 39.2 us  [send(): return lax.ppermute(x, 'chan', along(axis, shift))]
    pallas_call x5, Pallas kernels: 5.72 us -> 3.1 us  [plain(): pl.pallas_call(kernel, in_specs=[smem()] * len(smems) + [pl.BlockSpec(mem...]
    squeeze x4, local copies, waits for them, and re-layouts: 2.03 us -> 0.01 us  [shards(): n[base + IDS, :FRAMES]]
    pallas_call x2, Pallas kernels: 9.61 us -> 7.87 us  [forward(): pl.pallas_call(functools.partial(forward_kernel, wide), grid=(FRAMES // S...]
  transfers between devices with their start and end apart: 18 -> 18, of which waited for: 12 -> 13; matrix products, arithmetic and copies ran while one was open for 2% -> 0% of each run, Pallas kernels for 11% -> 10%
where the time goes in v4:
time: 104 us; the launch traced here: 103 us
  waiting for transfers between devices  39.2 us (38%)
  starting transfers between devices  34.4 us (33%)
  Pallas kernels  21.6 us (21%)
  local copies, waits for them, and re-layouts  3.35 us (3%)
  matrix products  3.14 us (3%)
  between operations  1.06 us (1%)
    ppermute x18, waiting for transfers between devices, send(): return lax.ppermute(x, 'chan', along(axis, shift))  39.2 us
    ppermute x18, starting transfers between devices, send(): return lax.ppermute(x, 'chan', along(axis, shift))  34.4 us
    pallas_call x2, Pallas kernels, backward(): pl.pallas_call(functools.partial(backward_kernel, wide), grid=(FRAMES //...  10.6 us
    pallas_call x2, Pallas kernels, forward(): pl.pallas_call(functools.partial(forward_kernel, wide), grid=(FRAMES // S...  7.87 us
    unnamed x49, local copies, waits for them, and re-layouts  3.33 us
    pallas_call x5, Pallas kernels, plain(): pl.pallas_call(kernel, in_specs=[smem()] * len(smems) + [pl.BlockSpec(mem...  3.1 us
  transfers between devices with their start and end apart: 18, of which 13 were waited for; matrix products, arithmetic and copies ran while one was open for 0% of the time, Pallas kernels for 10%

profile of v4, /device:TPU:2, one launch (start us, length us, event | category | flops | bytes accessed | tf_op | source)
XLA Modules:
  0.0 102.9 jit_solution(4817959539218317739)
XLA Ops:
  0.8 1.6 %copy-done = f32[150,4096]{1,0:T(8,128)S(1)} copy-done((f32[150,4096]{1,0:T(8,128)S(1)}, f32[150,4096]{1,0:T(8,128)}, u32[]{:S(2)}) %copy-start) | copy-done | bytes 2457624
  2.3 1.4 %convolution_bitcast_fusion = f32[2,8,32,128]{3,1,2,0:T(8,128)S(1)} fusion(f32[16,150]{1,0:T(8,128)} %param.26, f32[150,4096]{1,0:T(8,128)S(1)} %copy-done), kind=kOutput, calls=%fused_computation | convolution fusion | flops 58982400 | bytes 2729344 | tf_op jit(solution)/shard_map/dot_general | solution.py:555
  4.1 1.6 %copy-done.1 = f32[16,2,128,128]{3,2,1,0:T(8,128)S(1)} copy-done((f32[16,2,128,128]{3,2,1,0:T(8,128)S(1)}, f32[16,2,128,128]{3,2,1,0:T(8,128)}, u32[]{:S(2)}) %copy-start.1) | copy-done | bytes 2097176
  5.7 4.1 %forward_narrow.1 = (f32[16,64,128]{2,1,0:T(8,128)S(1)}, f32[16,72,256]{2,1,0:T(8,128)S(1)}, f32[16,72,256]{2,1,0:T(8,128)S(1)}, f32[16,2,128,128]{3,2,1,0:T(8,1...) custom-call(s32[2]{0:T(128)S(1)} %pad_add_fusion.place, ...), custom_call_target="tpu_custom_call" | custom-call | flops 4000000000 | bytes 8000000 | tf_op jit(solution)/shard_map/forward_narrow/pallas_call | solution.py:243
  9.7 3.3 %collective-permute-start.1 = (f32[824,128]{1,0:T(8,128)S(1)}, f32[824,128]{1,0:T(8,128)S(1)}, u32[]{:S(2)}, u32[]{:S(2)}) collective-permute-start(f32[824,128]{1,0:T(8,128)S(1)} %get-tuple-element.56), channel_id=1, source_target_pairs={{0,16},{1,17},{2,18},{3,19},{4,20},{5,21},{6,22},{7,23},{8,24},{9,... | collective-permute-start | bytes 1265672 | tf_op jit(solution)/shard_map/ppermute | solution.py:546
  13.0 3.8 %forward_wide.1 = (f32[16,64,128]{2,1,0:T(8,128)S(1)}, f32[16,72,256]{2,1,0:T(8,128)S(1)}, f32[16,72,256]{2,1,0:T(8,128)S(1)}, f32[16,2,128,128]{3,2,1,0:T(8,128...) custom-call(s32[2]{0:T(128)S(1)} %pad_add_fusion.place, ...), custom_call_target="tpu_custom_call", output_to_operand_aliasing={{5}: (3, {}), {7}: (4, {})} | custom-call | flops 4000000000 | bytes 8000000 | tf_op jit(solution)/shard_map/forward_wide/pallas_call | solution.py:243
  16.8 1.1 %collective-permute-start.2 = (f32[880,128]{1,0:T(8,128)S(1)}, f32[880,128]{1,0:T(8,128)S(1)}, u32[]{:S(2)}, u32[]{:S(2)}) collective-permute-start(f32[880,128]{1,0:T(8,128)S(1)} %get-tuple-element.57), channel_id=1, source_target_pairs={{0,24},{1,25},{2,26},{3,27},{4,28},{5,29},{6,30},{7,31},{8,0},{9,1... | collective-permute-start | bytes 1351688 | tf_op jit(solution)/shard_map/ppermute | solution.py:546
  18.0 1.0 collective-permute-start
  19.7 4.3 %collective-permute-done.1.n2 = f32[824,128]{1,0:T(8,128)S(1)} collective-permute-done((f32[824,128]{1,0:T(8,128)S(1)}, f32[824,128]{1,0:T(8,128)S(1)}, u32[]{:S(2)}, u32[]{:S(2)}) %collective-permute-start.1) | collective-permute-done | bytes 421920 | tf_op jit(solution)/shard_map/ppermute | solution.py:546
  24.0 0.9 sum_first.1
  24.8 8.3 %collective-permute-done.3.w2 = f32[56,128]{1,0:T(8,128)S(1)} collective-permute-done((f32[56,128]{1,0:T(8,128)S(1)}, f32[56,128]{1,0:T(8,128)S(1)}, u32[]{:S(2)}, u32[]{:S(2)}) %collective-permute-start.3) | collective-permute-done | bytes 28704 | tf_op jit(solution)/shard_map/ppermute | solution.py:546
  33.3 1.5 %sum_channels.1 = (f32[648,128]{1,0:T(8,128)S(1)}, f32[544,128]{1,0:T(8,128)S(1)}, f32[536,128]{1,0:T(8,128)S(1)}) custom-call(s32[2]{0:T(128)S(1)} %pad_add_fusion.place, f32[32,48,128]{2,1,0:T(8,128)S(1)} %get-tuple-element.58.first, f32[32,8,128]{2,1,0:T(8,128)S(1)} %get-tuple-element.59.first_edge, f32[880,128]{1,0:T(8,128)S(1)} %collective-permute-done.n1, ...), custom_call_target="tpu_custom_call" | custom-call | tf_op jit(solution)/shard_map/sum_channels/pallas_call | solution.py:405
  34.7 2.0 %collective-permute-start.4 = (f32[544,128]{1,0:T(8,128)S(1)}, f32[544,128]{1,0:T(8,128)S(1)}, u32[]{:S(2)}, u32[]{:S(2)}) collective-permute-start(f32[544,128]{1,0:T(8,128)S(1)} %get-tuple-element.63), channel_id=1, source_target_pairs={{0,1},{1,2},{2,3},{3,4},{4,5},{5,6},{6,7},{7,0},{8,9},{9,10},{10,1... | collective-permute-start | bytes 835592 | tf_op jit(solution)/shard_map/ppermute | solution.py:546
  36.7 4.2 %collective-permute-start.5 = (f32[536,128]{1,0:T(8,128)S(1)}, f32[536,128]{1,0:T(8,128)S(1)}, u32[]{:S(2)}, u32[]{:S(2)}) collective-permute-start(f32[536,128]{1,0:T(8,128)S(1)} %get-tuple-element.64), channel_id=1, source_target_pairs={{0,7},{1,0},{2,1},{3,2},{4,3},{5,4},{6,5},{7,6},{8,15},{9,8},{10,9... | collective-permute-start | bytes 823304 | tf_op jit(solution)/shard_map/ppermute | solution.py:546
  41.0 5.1 %collective-permute-done.5.down = f32[536,128]{1,0:T(8,128)S(1)} collective-permute-done((f32[536,128]{1,0:T(8,128)S(1)}, f32[536,128]{1,0:T(8,128)S(1)}, u32[]{:S(2)}, u32[]{:S(2)}) %collective-permute-start.5) | collective-permute-done | bytes 274464 | tf_op jit(solution)/shard_map/ppermute | solution.py:546
  46.7 4.6 %collective-permute-start.6 = (f32[216,128]{1,0:T(8,128)S(1)}, f32[216,128]{1,0:T(8,128)S(1)}, u32[]{:S(2)}, u32[]{:S(2)}) collective-permute-start(f32[216,128]{1,0:T(8,128)S(1)} %get-tuple-element.65), channel_id=1, source_target_pairs={{0,3},{1,4},{2,5},{3,6},{4,7},{5,0},{6,1},{7,2},{8,11},{9,12},{10,... | collective-permute-start | bytes 331784 | tf_op jit(solution)/shard_map/ppermute | solution.py:546
  51.8 5.6 %collective-permute-done.6.far = f32[216,128]{1,0:T(8,128)S(1)} collective-permute-done((f32[216,128]{1,0:T(8,128)S(1)}, f32[216,128]{1,0:T(8,128)S(1)}, u32[]{:S(2)}, u32[]{:S(2)}) %collective-permute-start.6) | collective-permute-done | bytes 110624 | tf_op jit(solution)/shard_map/ppermute | solution.py:546
  57.3 4.7 %collective-permute-done.7.back = f32[216,128]{1,0:T(8,128)S(1)} collective-permute-done((f32[216,128]{1,0:T(8,128)S(1)}, f32[216,128]{1,0:T(8,128)S(1)}, u32[]{:S(2)}, u32[]{:S(2)}) %collective-permute-start.7) | collective-permute-done | bytes 110624 | tf_op jit(solution)/shard_map/ppermute | solution.py:546
  62.2 3.8 %collective-permute-start.9 = (f32[144,128]{1,0:T(8,128)S(1)}, f32[144,128]{1,0:T(8,128)S(1)}, u32[]{:S(2)}, u32[]{:S(2)}) collective-permute-start(f32[144,128]{1,0:T(8,128)S(1)} %objects.1.own), channel_id=1, source_target_pairs={{0,3},{1,4},{2,5},{3,6},{4,7},{5,0},{6,1},{7,2},{8,11},{9,12},{10,... | collective-permute-start | bytes 221192 | tf_op jit(solution)/shard_map/ppermute | solution.py:546
  66.0 3.2 %collective-permute-done.8.ahead = f32[144,128]{1,0:T(8,128)S(1)} collective-permute-done((f32[144,128]{1,0:T(8,128)S(1)}, f32[144,128]{1,0:T(8,128)S(1)}, u32[]{:S(2)}, u32[]{:S(2)}) %collective-permute-start.8) | collective-permute-done | bytes 73760 | tf_op jit(solution)/shard_map/ppermute | solution.py:546
  69.2 1.2 %collective-permute-done.9.behind = f32[144,128]{1,0:T(8,128)S(1)} collective-permute-done((f32[144,128]{1,0:T(8,128)S(1)}, f32[144,128]{1,0:T(8,128)S(1)}, u32[]{:S(2)}, u32[]{:S(2)}) %collective-permute-start.9) | collective-permute-done | bytes 73760 | tf_op jit(solution)/shard_map/ppermute | solution.py:546
  70.4 1.5 %collective-permute-start.10 = (f32[360,128]{1,0:T(8,128)S(1)}, f32[360,128]{1,0:T(8,128)S(1)}, u32[]{:S(2)}, u32[]{:S(2)}) collective-permute-start(f32[360,128]{1,0:T(8,128)S(1)} %get-tuple-element.82), channel_id=1, source_target_pairs={{0,1},{1,2},{2,3},{3,4},{4,5},{5,6},{6,7},{7,0},{8,9},{9,10},{10,1... | collective-permute-start | bytes 552968 | tf_op jit(solution)/shard_map/ppermute | solution.py:546
  71.9 1.8 %collective-permute-start.11 = (f32[360,128]{1,0:T(8,128)S(1)}, f32[360,128]{1,0:T(8,128)S(1)}, u32[]{:S(2)}, u32[]{:S(2)}) collective-permute-start(f32[360,128]{1,0:T(8,128)S(1)} %get-tuple-element.81), channel_id=1, source_target_pairs={{0,7},{1,0},{2,1},{3,2},{4,3},{5,4},{6,5},{7,6},{8,15},{9,8},{10,9... | collective-permute-start | bytes 552968 | tf_op jit(solution)/shard_map/ppermute | solution.py:546
  73.8 3.4 %collective-permute-done.10.up = f32[360,128]{1,0:T(8,128)S(1)} collective-permute-done((f32[360,128]{1,0:T(8,128)S(1)}, f32[360,128]{1,0:T(8,128)S(1)}, u32[]{:S(2)}, u32[]{:S(2)}) %collective-permute-start.10) | collective-permute-done | bytes 184352 | tf_op jit(solution)/shard_map/ppermute | solution.py:546
  78.2 2.1 %collective-permute-start.15 = (f32[32,128]{1,0:T(8,128)S(1)}, f32[32,128]{1,0:T(8,128)S(1)}, u32[]{:S(2)}, u32[]{:S(2)}) collective-permute-start(f32[32,128]{1,0:T(8,128)S(1)} %get-tuple-element.75.refs_0_), channel_id=1, source_target_pairs={{0,8},{1,9},{2,10},{3,11},{4,12},{5,13},{6,14},{7,15},{8,16},{9,17... | collective-permute-start | bytes 49160 | tf_op jit(solution)/shard_map/ppermute | solution.py:546
  80.3 2.9 %collective-permute-start.16 = (f32[32,128]{1,0:T(8,128)S(1)}, f32[32,128]{1,0:T(8,128)S(1)}, u32[]{:S(2)}, u32[]{:S(2)}) collective-permute-start(f32[32,128]{1,0:T(8,128)S(1)} %get-tuple-element.75.refs_0_), channel_id=1, source_target_pairs={{0,16},{1,17},{2,18},{3,19},{4,20},{5,21},{6,22},{7,23},{8,24},{9,... | collective-permute-start | bytes 49160 | tf_op jit(solution)/shard_map/ppermute | solution.py:546
  83.2 1.3 %collective-permute-start.17 = (f32[32,128]{1,0:T(8,128)S(1)}, f32[32,128]{1,0:T(8,128)S(1)}, u32[]{:S(2)}, u32[]{:S(2)}) collective-permute-start(f32[32,128]{1,0:T(8,128)S(1)} %get-tuple-element.75.refs_0_), channel_id=1, source_target_pairs={{0,24},{1,25},{2,26},{3,27},{4,28},{5,29},{6,30},{7,31},{8,0},{9,1... | collective-permute-start | bytes 49160 | tf_op jit(solution)/shard_map/ppermute | solution.py:546
  85.9 2.0 %collective-permute-start.14 = (f32[544,128]{1,0:T(8,128)S(1)}, f32[544,128]{1,0:T(8,128)S(1)}, u32[]{:S(2)}, u32[]{:S(2)}) collective-permute-start(f32[544,128]{1,0:T(8,128)S(1)} %get-tuple-element.70), channel_id=1, source_target_pairs={{0,24},{1,25},{2,26},{3,27},{4,28},{5,29},{6,30},{7,31},{8,0},{9,1... | collective-permute-start | bytes 835592 | tf_op jit(solution)/shard_map/ppermute | solution.py:546
  88.0 5.5 %backward_wide.1 = (f32[16,32,128]{2,1,0:T(8,128)S(1)}, f32[2,128,128]{2,1,0:T(8,128)}) custom-call(s32[2]{0:T(128)S(1)} %pad_add_fusion.place, f32[16,64,128]{2,1,0:T(8,128)S(1)} %get-tuple-element.71.q_ref, f32[16,72,256]{2,1,0:T(8,128)S(1)} %get-tuple-element.72.s_ref, f32[16,72,256]{2,1,0:T(8,128)S(1)} %get-tuple-element.73.d_ref, ...), custom_call_target="tpu_custom_call" | custom-call | flops 4000000000 | bytes 8000000 | tf_op jit(solution)/shard_map/backward_wide/pallas_call | solution.py:514
  93.5 1.9 %collective-permute-done.12.refs_1_.refs_5_ = f32[544,128]{1,0:T(8,128)S(1)} collective-permute-done((f32[544,128]{1,0:T(8,128)S(1)}, f32[544,128]{1,0:T(8,128)S(1)}, u32[]{:S(2)}, u32[]{:S(2)}) %collective-permute-start.12) | collective-permute-done | bytes 278560 | tf_op jit(solution)/shard_map/ppermute | solution.py:546
  96.1 5.1 %backward_narrow.1 = (f32[16,4096]{1,0:T(8,128)S(1)}, f32[2,128,128]{2,1,0:T(8,128)}) custom-call(s32[2]{0:T(128)S(1)} %pad_add_fusion.place, f32[16,64,128]{2,1,0:T(8,128)S(1)} %get-tuple-element.48.q_ref, f32[16,72,256]{2,1,0:T(8,128)S(1)} %get-tuple-element.49.s_ref, f32[16,72,256]{2,1,0:T(8,128)S(1)} %get-tuple-element.50.d_ref, ...), custom_call_target="tpu_custom_call" | custom-call | flops 4000000000 | bytes 8000000 | tf_op jit(solution)/shard_map/backward_narrow/pallas_call | solution.py:514
  101.2 1.7 %fusion.2 = f32[16,150]{1,0:T(8,128)} fusion(f32[16,4096]{1,0:T(8,128)S(1)} %get-tuple-element.78, f32[150,4096]{1,0:T(8,128)S(1)} %copy-done), kind=kOutput, calls=%fused_computation.12 | convolution fusion | flops 58982400 | bytes 2729344 | tf_op jit(solution)/shard_map/dot_general | solution.py:611
  (75 shorter events, 5.6 us)
Async XLA Ops:
  0.6 3.3 %copy-start.22 = (f32[32,128]{1,0:T(8,128)S(1)}, f32[32,128]{1,0:T(8,128)}, u32[]{:S(2)}) copy-start(f32[32,128]{1,0:T(8,128)} %constant.113.clone.pupil_ref) | copy-start | bytes 49156
  0.7 3.3 %copy-start.6 = (bf16[256,256]{1,0:T(8,128)(2,1)S(1)}, bf16[256,256]{1,0:T(8,128)(2,1)}, u32[]{:S(2)}) copy-start(bf16[256,256]{1,0:T(8,128)(2,1)} %constant.95.clone.rest_3_) | copy-start | bytes 393220
  0.7 3.3 %copy-start.17 = (bf16[128,256]{1,0:T(8,128)(2,1)S(1)}, bf16[128,256]{1,0:T(8,128)(2,1)}, u32[]{:S(2)}) copy-start(bf16[128,256]{1,0:T(8,128)(2,1)} %constant.96.clone.rest_4_) | copy-start | bytes 196612
  5.7 7.4 %copy-start.2 = (f32[16,2,128,128]{3,2,1,0:T(8,128)S(1)}, f32[16,2,128,128]{3,2,1,0:T(8,128)}, u32[]{:S(2)}) copy-start(f32[16,2,128,128]{3,2,1,0:T(8,128)} %rest_2_.3) | copy-start | bytes 6291460
  9.7 14.2 %collective-permute-start.1 = (f32[824,128]{1,0:T(8,128)S(1)}, f32[824,128]{1,0:T(8,128)S(1)}, u32[]{:S(2)}, u32[]{:S(2)}) collective-permute-start(f32[824,128]{1,0:T(8,128)S(1)} %get-tuple-element.56), channel_id=1, source_target_pairs={{0,16},{1,17},{2,18},{3,19},{4,20},{5,21},{6,22},{7,23},{8,24},{9,... | collective-permute-start | bytes 1265672 | tf_op jit(solution)/shard_map/ppermute | solution.py:546
  16.8 16.3 %collective-permute-start.2 = (f32[880,128]{1,0:T(8,128)S(1)}, f32[880,128]{1,0:T(8,128)S(1)}, u32[]{:S(2)}, u32[]{:S(2)}) collective-permute-start(f32[880,128]{1,0:T(8,128)S(1)} %get-tuple-element.57), channel_id=1, source_target_pairs={{0,24},{1,25},{2,26},{3,27},{4,28},{5,29},{6,30},{7,31},{8,0},{9,1... | collective-permute-start | bytes 1351688 | tf_op jit(solution)/shard_map/ppermute | solution.py:546
  18.0 15.2 %collective-permute-start = (f32[880,128]{1,0:T(8,128)S(1)}, f32[880,128]{1,0:T(8,128)S(1)}, u32[]{:S(2)}, u32[]{:S(2)}) collective-permute-start(f32[880,128]{1,0:T(8,128)S(1)} %get-tuple-element.55), channel_id=1, source_target_pairs={{0,8},{1,9},{2,10},{3,11},{4,12},{5,13},{6,14},{7,15},{8,16},{9,17... | collective-permute-start | bytes 1351688 | tf_op jit(solution)/shard_map/ppermute | solution.py:546
  18.9 14.1 %collective-permute-start.3 = (f32[56,128]{1,0:T(8,128)S(1)}, f32[56,128]{1,0:T(8,128)S(1)}, u32[]{:S(2)}, u32[]{:S(2)}) collective-permute-start(f32[56,128]{1,0:T(8,128)S(1)} %get-tuple-element.61), channel_id=1, source_target_pairs={{0,16},{1,17},{2,18},{3,19},{4,20},{5,21},{6,22},{7,23},{8,24},{9,... | collective-permute-start | bytes 86024 | tf_op jit(solution)/shard_map/ppermute | solution.py:546
  33.2 54.8 %copy-start.4 = (bf16[256,256]{1,0:T(8,128)(2,1)S(1)}, bf16[256,256]{1,0:T(8,128)(2,1)}, u32[]{:S(2)}) copy-start(bf16[256,256]{1,0:T(8,128)(2,1)} %constant.103.clone.refs_5_.refs_10_) | copy-start | bytes 393220
  33.2 54.8 %copy-start.5 = (bf16[256,256]{1,0:T(8,128)(2,1)S(1)}, bf16[256,256]{1,0:T(8,128)(2,1)}, u32[]{:S(2)}) copy-start(bf16[256,256]{1,0:T(8,128)(2,1)} %constant.104.clone.refs_6_.refs_11_) | copy-start | bytes 393220
  33.2 54.8 %copy-start.11 = (bf16[128,144]{1,0:T(8,128)(2,1)S(1)}, bf16[128,144]{1,0:T(8,128)(2,1)}, u32[]{:S(2)}) copy-start(bf16[128,144]{1,0:T(8,128)(2,1)} %constant.105.clone.refs_7_.refs_12_) | copy-start | bytes 110596
  33.2 54.8 %copy-start.12 = (bf16[128,144]{1,0:T(8,128)(2,1)S(1)}, bf16[128,144]{1,0:T(8,128)(2,1)}, u32[]{:S(2)}) copy-start(bf16[128,144]{1,0:T(8,128)(2,1)} %constant.106.clone.refs_8_.refs_13_) | copy-start | bytes 110596
  33.2 54.8 %copy-start.13 = (bf16[128,256]{1,0:T(8,128)(2,1)S(1)}, bf16[128,256]{1,0:T(8,128)(2,1)}, u32[]{:S(2)}) copy-start(bf16[128,256]{1,0:T(8,128)(2,1)} %constant.107.clone.refs_9_.refs_14_) | copy-start | bytes 196612
  33.2 54.8 %copy-start.14 = (bf16[128,256]{1,0:T(8,128)(2,1)S(1)}, bf16[128,256]{1,0:T(8,128)(2,1)}, u32[]{:S(2)}) copy-start(bf16[128,256]{1,0:T(8,128)(2,1)} %constant.108.clone.refs_10_.refs_15_) | copy-start | bytes 196612
  33.2 54.8 %copy-start.15 = (bf16[256,128]{1,0:T(8,128)(2,1)S(1)}, bf16[256,128]{1,0:T(8,128)(2,1)}, u32[]{:S(2)}) copy-start(bf16[256,128]{1,0:T(8,128)(2,1)} %constant.109.clone.refs_11_.refs_16_) | copy-start | bytes 196612
  33.2 54.8 %copy-start.16 = (bf16[256,128]{1,0:T(8,128)(2,1)S(1)}, bf16[256,128]{1,0:T(8,128)(2,1)}, u32[]{:S(2)}) copy-start(bf16[256,128]{1,0:T(8,128)(2,1)} %constant.110.clone.refs_12_.refs_17_) | copy-start | bytes 196612
  33.2 54.8 %copy-start.20 = (bf16[128,128]{1,0:T(8,128)(2,1)S(1)}, bf16[128,128]{1,0:T(8,128)(2,1)}, u32[]{:S(2)}) copy-start(bf16[128,128]{1,0:T(8,128)(2,1)} %constant.111.clone.refs_13_.refs_18_) | copy-start | bytes 98308
  33.2 54.7 %copy-start.21 = (bf16[128,128]{1,0:T(8,128)(2,1)S(1)}, bf16[128,128]{1,0:T(8,128)(2,1)}, u32[]{:S(2)}) copy-start(bf16[128,128]{1,0:T(8,128)(2,1)} %constant.112.clone.refs_14_.refs_19_) | copy-start | bytes 98308
  34.7 11.9 %collective-permute-start.4 = (f32[544,128]{1,0:T(8,128)S(1)}, f32[544,128]{1,0:T(8,128)S(1)}, u32[]{:S(2)}, u32[]{:S(2)}) collective-permute-start(f32[544,128]{1,0:T(8,128)S(1)} %get-tuple-element.63), channel_id=1, source_target_pairs={{0,1},{1,2},{2,3},{3,4},{4,5},{5,6},{6,7},{7,0},{8,9},{9,10},{10,1... | collective-permute-start | bytes 835592 | tf_op jit(solution)/shard_map/ppermute | solution.py:546
  36.7 9.3 %collective-permute-start.5 = (f32[536,128]{1,0:T(8,128)S(1)}, f32[536,128]{1,0:T(8,128)S(1)}, u32[]{:S(2)}, u32[]{:S(2)}) collective-permute-start(f32[536,128]{1,0:T(8,128)S(1)} %get-tuple-element.64), channel_id=1, source_target_pairs={{0,7},{1,0},{2,1},{3,2},{4,3},{5,4},{6,5},{7,6},{8,15},{9,8},{10,9... | collective-permute-start | bytes 823304 | tf_op jit(solution)/shard_map/ppermute | solution.py:546
  46.7 10.7 %collective-permute-start.6 = (f32[216,128]{1,0:T(8,128)S(1)}, f32[216,128]{1,0:T(8,128)S(1)}, u32[]{:S(2)}, u32[]{:S(2)}) collective-permute-start(f32[216,128]{1,0:T(8,128)S(1)} %get-tuple-element.65), channel_id=1, source_target_pairs={{0,3},{1,4},{2,5},{3,6},{4,7},{5,0},{6,1},{7,2},{8,11},{9,12},{10,... | collective-permute-start | bytes 331784 | tf_op jit(solution)/shard_map/ppermute | solution.py:546
  51.2 10.8 %collective-permute-start.7 = (f32[216,128]{1,0:T(8,128)S(1)}, f32[216,128]{1,0:T(8,128)S(1)}, u32[]{:S(2)}, u32[]{:S(2)}) collective-permute-start(f32[216,128]{1,0:T(8,128)S(1)} %get-tuple-element.66), channel_id=1, source_target_pairs={{0,5},{1,6},{2,7},{3,0},{4,1},{5,2},{6,3},{7,4},{8,13},{9,14},{10,... | collective-permute-start | bytes 331784 | tf_op jit(solution)/shard_map/ppermute | solution.py:546
  62.1 7.1 %collective-permute-start.8 = (f32[144,128]{1,0:T(8,128)S(1)}, f32[144,128]{1,0:T(8,128)S(1)}, u32[]{:S(2)}, u32[]{:S(2)}) collective-permute-start(f32[144,128]{1,0:T(8,128)S(1)} %objects.1.own), channel_id=1, source_target_pairs={{0,5},{1,6},{2,7},{3,0},{4,1},{5,2},{6,3},{7,4},{8,13},{9,14},{10,... | collective-permute-start | bytes 221192 | tf_op jit(solution)/shard_map/ppermute | solution.py:546
  62.2 8.2 %collective-permute-start.9 = (f32[144,128]{1,0:T(8,128)S(1)}, f32[144,128]{1,0:T(8,128)S(1)}, u32[]{:S(2)}, u32[]{:S(2)}) collective-permute-start(f32[144,128]{1,0:T(8,128)S(1)} %objects.1.own), channel_id=1, source_target_pairs={{0,3},{1,4},{2,5},{3,6},{4,7},{5,0},{6,1},{7,2},{8,11},{9,12},{10,... | collective-permute-start | bytes 221192 | tf_op jit(solution)/shard_map/ppermute | solution.py:546
  70.4 6.8 %collective-permute-start.10 = (f32[360,128]{1,0:T(8,128)S(1)}, f32[360,128]{1,0:T(8,128)S(1)}, u32[]{:S(2)}, u32[]{:S(2)}) collective-permute-start(f32[360,128]{1,0:T(8,128)S(1)} %get-tuple-element.82), channel_id=1, source_target_pairs={{0,1},{1,2},{2,3},{3,4},{4,5},{5,6},{6,7},{7,0},{8,9},{9,10},{10,1... | collective-permute-start | bytes 552968 | tf_op jit(solution)/shard_map/ppermute | solution.py:546
  71.9 5.5 %collective-permute-start.11 = (f32[360,128]{1,0:T(8,128)S(1)}, f32[360,128]{1,0:T(8,128)S(1)}, u32[]{:S(2)}, u32[]{:S(2)}) collective-permute-start(f32[360,128]{1,0:T(8,128)S(1)} %get-tuple-element.81), channel_id=1, source_target_pairs={{0,7},{1,0},{2,1},{3,2},{4,3},{5,4},{6,5},{7,6},{8,15},{9,8},{10,9... | collective-permute-start | bytes 552968 | tf_op jit(solution)/shard_map/ppermute | solution.py:546
  78.2 7.8 %collective-permute-start.15 = (f32[32,128]{1,0:T(8,128)S(1)}, f32[32,128]{1,0:T(8,128)S(1)}, u32[]{:S(2)}, u32[]{:S(2)}) collective-permute-start(f32[32,128]{1,0:T(8,128)S(1)} %get-tuple-element.75.refs_0_), channel_id=1, source_target_pairs={{0,8},{1,9},{2,10},{3,11},{4,12},{5,13},{6,14},{7,15},{8,16},{9,17... | collective-permute-start | bytes 49160 | tf_op jit(solution)/shard_map/ppermute | solution.py:546
  80.3 7.6 %collective-permute-start.16 = (f32[32,128]{1,0:T(8,128)S(1)}, f32[32,128]{1,0:T(8,128)S(1)}, u32[]{:S(2)}, u32[]{:S(2)}) collective-permute-start(f32[32,128]{1,0:T(8,128)S(1)} %get-tuple-element.75.refs_0_), channel_id=1, source_target_pairs={{0,16},{1,17},{2,18},{3,19},{4,20},{5,21},{6,22},{7,23},{8,24},{9,... | collective-permute-start | bytes 49160 | tf_op jit(solution)/shard_map/ppermute | solution.py:546
  83.2 4.7 %collective-permute-start.17 = (f32[32,128]{1,0:T(8,128)S(1)}, f32[32,128]{1,0:T(8,128)S(1)}, u32[]{:S(2)}, u32[]{:S(2)}) collective-permute-start(f32[32,128]{1,0:T(8,128)S(1)} %get-tuple-element.75.refs_0_), channel_id=1, source_target_pairs={{0,24},{1,25},{2,26},{3,27},{4,28},{5,29},{6,30},{7,31},{8,0},{9,1... | collective-permute-start | bytes 49160 | tf_op jit(solution)/shard_map/ppermute | solution.py:546
  84.5 10.9 %collective-permute-start.12 = (f32[544,128]{1,0:T(8,128)S(1)}, f32[544,128]{1,0:T(8,128)S(1)}, u32[]{:S(2)}, u32[]{:S(2)}) collective-permute-start(f32[544,128]{1,0:T(8,128)S(1)} %get-tuple-element.68), channel_id=1, source_target_pairs={{0,8},{1,9},{2,10},{3,11},{4,12},{5,13},{6,14},{7,15},{8,16},{9,17... | collective-permute-start | bytes 835592 | tf_op jit(solution)/shard_map/ppermute | solution.py:546
  85.2 10.2 %collective-permute-start.13 = (f32[544,128]{1,0:T(8,128)S(1)}, f32[544,128]{1,0:T(8,128)S(1)}, u32[]{:S(2)}, u32[]{:S(2)}) collective-permute-start(f32[544,128]{1,0:T(8,128)S(1)} %get-tuple-element.69), channel_id=1, source_target_pairs={{0,16},{1,17},{2,18},{3,19},{4,20},{5,21},{6,22},{7,23},{8,24},{9,... | collective-permute-start | bytes 835592 | tf_op jit(solution)/shard_map/ppermute | solution.py:546
  85.9 10.2 %collective-permute-start.14 = (f32[544,128]{1,0:T(8,128)S(1)}, f32[544,128]{1,0:T(8,128)S(1)}, u32[]{:S(2)}, u32[]{:S(2)}) collective-permute-start(f32[544,128]{1,0:T(8,128)S(1)} %get-tuple-element.70), channel_id=1, source_target_pairs={{0,24},{1,25},{2,26},{3,27},{4,28},{5,29},{6,30},{7,31},{8,0},{9,1... | collective-permute-start | bytes 835592 | tf_op jit(solution)/shard_map/ppermute | solution.py:546
  (10 other events, 27.9 us)

commit v5 on v4

--- a/solution.py
+++ b/solution.py
@@ -30,7 +30,7 @@
 BASE = (0, W_ROWS, 0, W_ROWS)
 Z_ROWS = 216
 F_ROWS = 144
-R_ROWS = (FRAMES + 1) * 2 * GROUP
+R_ROWS = FRAMES * 2 * GROUP
 
 
 def dft(length, columns):
@@ -369,7 +369,7 @@
 
 
 def select_kernel(place, ids, own, ahead, behind, up, down, *refs):
-    outs, (wide, near, objects, edge, total, other) = refs[:NY], refs[NY:]
+    outs, wides, (near, objects, edge, total, other) = refs[:NY], refs[NY : 2 * NY], refs[2 * NY :]
     other[:F_FIRST, :] = up[2 * F_ROWS :, :]
     other[F_FIRST:, :] = down[2 * F_ROWS :, :]
     y, z = place[0], place[1]
@@ -386,13 +386,13 @@
         for j in range(2):
             total[pl.ds(2 * source + j, 1), :] = part[at + j : at + j + 1, :]
             total[pl.ds(GROUP + 2 * source + j, 1), :] = part[at + 2 + j : at + 3 + j, :]
-    wide[...] = total[...]
     for shift in range(NY):
         out = outs[shift]
         start = (NY - shift) % NY * FRAMES
         for f in range(FRAMES):
             out[f * 2 * GROUP : (f + 1) * 2 * GROUP, :] = objects[ids[start + f]]
-        out[FRAMES * 2 * GROUP :, :] = objects[lax.rem(y + shift, NY) * NZ + z]
+        wides[shift][: 2 * GROUP, :] = objects[lax.rem(y + shift, NY) * NZ + z]
+        wides[shift][2 * GROUP :, :] = total[...]
     for f in range(FRAMES):
         near[2 * f : 2 * f + 2, :] = edge[ids[f], 0:2, :]
     near[2 * FRAMES : 2 * FRAMES + 2, :] = edge[y * NZ + z, 0:2, :]
@@ -417,8 +417,8 @@
 def backward_kernel(wide, place, q_ref, s_ref, d_ref, g_ref, *refs):
     parts, refs = refs[:NY], refs[NY:]
     if not wide:
-        own, (other, *refs) = refs[:NY], refs[NY:]
-    near, a1, a2, b1, b2, e1, e2, f1, f2, m1, m2, out, obj, scr = refs
+        other, *refs = refs
+    near, a1, a2, b1, b2, e1, e2, f1, f2, m1, m2, out, *objs, scr = refs
     step = pl.program_id(0)
     y = place[0]
 
@@ -431,20 +431,21 @@
     @pl.when(step == 0)
     def _():
         scr[...] = jnp.zeros_like(scr)
-        gather(parts if wide else own, 0)
-        at = 2 * FRAMES + (2 if wide else 0)
-        for c in range(2):
-            scr[c, 64:65, :] = near[at + c : at + c + 1, :]
-        half = jnp.concatenate([scr[0, :64, :], scr[1, :64, :]], 0)
-        high = half.astype(BF16)
-        middle, low = cut(half - high.astype(F32))
-        turned = jnp.zeros((SIZE, SIZE), F32)
-        for part in (high, middle, low):
-            turned = turned + mm(m1[...], mm(part, m2[...]).astype(BF16))
-        for c in range(2):
-            obj[c, :64, :] = scr[c, :64, :]
-            obj[c, 64:, :] = turned[64 * c : 64 * (c + 1)]
-            obj[c, 64:65, :] = scr[c, 64:65, :]
+        for item, obj in enumerate(objs):
+            gather(parts, item * 2 * GROUP)
+            at = 2 * (FRAMES + item)
+            for c in range(2):
+                scr[c, 64:65, :] = near[at + c : at + c + 1, :]
+            half = jnp.concatenate([scr[0, :64, :], scr[1, :64, :]], 0)
+            high = half.astype(BF16)
+            middle, low = cut(half - high.astype(F32))
+            turned = jnp.zeros((SIZE, SIZE), F32)
+            for part in (high, middle, low):
+                turned = turned + mm(m1[...], mm(part, m2[...]).astype(BF16))
+            for c in range(2):
+                obj[c, :64, :] = scr[c, :64, :]
+                obj[c, 64:, :] = turned[64 * c : 64 * (c + 1)]
+                obj[c, 64:65, :] = scr[c, 64:65, :]
 
     cots = []
     for k in range(STEP):
@@ -506,9 +507,9 @@
         sources, specs = list(parts), [whole(p) for p in parts]
         dphase, dphase_spec = shape(FRAMES, PUP // 2, SIZE), pairs
     else:
-        sources = list(parts) * 2 + [other]
+        sources = list(parts) + [other]
         specs = [pl.BlockSpec((STEP * block, SIZE), lambda i: (i, 0))] * NY
-        specs += [pl.BlockSpec((block, SIZE), lambda i: (FRAMES, 0))] * NY + [pairs]
+        specs += [pairs]
         dphase = shape(FRAMES, PUP * PUP)
         dphase_spec = pl.BlockSpec(dphase.shape, lambda i: (0, 0))
     return pl.pallas_call(
@@ -524,8 +525,8 @@
         + specs
         + [whole(near)]
         + [whole(t) for t in tables],
-        out_specs=[dphase_spec, pl.BlockSpec((2, SIZE, SIZE), lambda i: (0, 0, 0))],
-        out_shape=[dphase, shape(2, SIZE, SIZE)],
+        out_specs=[dphase_spec] + [pl.BlockSpec((2, SIZE, SIZE), lambda i: (0, 0, 0))] * (2 * wide),
+        out_shape=[dphase] + [shape(2, SIZE, SIZE)] * (2 * wide),
         scratch_shapes=[pltpu.VMEM((2, ROWS, SIZE), F32)],
         compiler_params=pltpu.CompilerParams(vmem_limit_bytes=VMEM_LIMIT),
         cost_estimate=pl.CostEstimate(flops=4_000_000_000, bytes_accessed=8_000_000, transcendentals=0),
@@ -595,19 +596,20 @@
     ahead, behind = send(own, "z", -3), send(own, "z", 3)
     up = send(jnp.concatenate([own, ahead, behind[:F_FIRST]]), "z", 1)
     down = send(jnp.concatenate([own, behind, ahead[F_FIRST:]]), "z", -1)
-    *back, wide_own, near = plain(
+    *back, near = plain(
         select_kernel,
         "select_objects",
         [place, ids],
         [own, ahead, behind, up, down],
-        [shape(R_ROWS, SIZE)] * NY + [shape(2 * GROUP, SIZE), shape(2 * FRAMES + 8, SIZE)],
+        [shape(R_ROWS, SIZE)] * NY + [shape(4 * GROUP, SIZE)] * NY + [shape(2 * FRAMES + 8, SIZE)],
         [pltpu.VMEM((32, 2 * GROUP, SIZE), F32), pltpu.VMEM((32, 8, SIZE), F32), pltpu.VMEM((2 * GROUP, SIZE), F32), pltpu.VMEM((F_ROWS, SIZE), F32)],
     )
-    wide_back = [wide_own] + [send(wide_own, "y", k) for k in range(1, NY)]
+    back, wide_back = back[:NY], back[NY:]
+    wide_back = [wide_back[0]] + [send(wide_back[k], "y", k) for k in range(1, NY)]
     back = [back[0]] + [send(back[k], "y", k) for k in range(1, NY)]
 
-    wide_dphase, wide_object = backward(True, place, *wide_kept, wide_back, near, None, tables_b)
-    dphase, narrow_object = backward(False, place, *narrow_kept, back, near, wide_dphase, tables_b)
+    wide_dphase, narrow_object, wide_object = backward(True, place, *wide_kept, wide_back, near, None, tables_b)
+    (dphase,) = backward(False, place, *narrow_kept, back, near, wide_dphase, tables_b)
     gradient = lax.dot_general(dphase, modes, (((1,), (1,)), ((), ())), precision=lax.Precision.HIGH)
     return gradient, narrow_object[None], wide_object
 

time: 104 us -> 103 us (level)
  no operation moved by 1% of the time
where the time goes in v5:
time: 103 us; the launch traced here: 102 us
  waiting for transfers between devices  38.8 us (38%)
  starting transfers between devices  34.4 us (33%)
  Pallas kernels  21.5 us (21%)
  local copies, waits for them, and re-layouts  3.35 us (3%)
  matrix products  3.14 us (3%)
  between operations  1.07 us (1%)
    ppermute x18, waiting for transfers between devices, send(): return lax.ppermute(x, 'chan', along(axis, shift))  38.8 us
    ppermute x18, starting transfers between devices, send(): return lax.ppermute(x, 'chan', along(axis, shift))  34.4 us
    pallas_call x2, Pallas kernels, backward(): pl.pallas_call(functools.partial(backward_kernel, wide), grid=(FRAMES //...  10.5 us
    pallas_call x2, Pallas kernels, forward(): pl.pallas_call(functools.partial(forward_kernel, wide), grid=(FRAMES // S...  7.87 us
    unnamed x49, local copies, waits for them, and re-layouts  3.33 us
    pallas_call x5, Pallas kernels, plain(): pl.pallas_call(kernel, in_specs=[smem()] * len(smems) + [pl.BlockSpec(mem...  3.11 us
  transfers between devices with their start and end apart: 18, of which 13 were waited for; matrix products, arithmetic and copies ran while one was open for 0% of the time, Pallas kernels for 10%

profile of v5, /device:TPU:2, one launch (start us, length us, event | category | flops | bytes accessed | tf_op | source)
XLA Modules:
  0.0 102.4 jit_solution(14391332178810588460)
XLA Ops:
  0.8 1.6 %copy-done = f32[150,4096]{1,0:T(8,128)S(1)} copy-done((f32[150,4096]{1,0:T(8,128)S(1)}, f32[150,4096]{1,0:T(8,128)}, u32[]{:S(2)}) %copy-start) | copy-done | bytes 2457624
  2.3 1.4 %convolution_bitcast_fusion = f32[2,8,32,128]{3,1,2,0:T(8,128)S(1)} fusion(f32[16,150]{1,0:T(8,128)} %param.26, f32[150,4096]{1,0:T(8,128)S(1)} %copy-done), kind=kOutput, calls=%fused_computation | convolution fusion | flops 58982400 | bytes 2729344 | tf_op jit(solution)/shard_map/dot_general | solution.py:556
  4.1 1.6 %copy-done.1 = f32[16,2,128,128]{3,2,1,0:T(8,128)S(1)} copy-done((f32[16,2,128,128]{3,2,1,0:T(8,128)S(1)}, f32[16,2,128,128]{3,2,1,0:T(8,128)}, u32[]{:S(2)}) %copy-start.1) | copy-done | bytes 2097176
  5.7 4.1 %forward_narrow.1 = (f32[16,64,128]{2,1,0:T(8,128)S(1)}, f32[16,72,256]{2,1,0:T(8,128)S(1)}, f32[16,72,256]{2,1,0:T(8,128)S(1)}, f32[16,2,128,128]{3,2,1,0:T(8,1...) custom-call(s32[2]{0:T(128)S(1)} %pad_add_fusion.place, ...), custom_call_target="tpu_custom_call" | custom-call | flops 4000000000 | bytes 8000000 | tf_op jit(solution)/shard_map/forward_narrow/pallas_call | solution.py:243
  9.7 3.3 %collective-permute-start.1 = (f32[824,128]{1,0:T(8,128)S(1)}, f32[824,128]{1,0:T(8,128)S(1)}, u32[]{:S(2)}, u32[]{:S(2)}) collective-permute-start(f32[824,128]{1,0:T(8,128)S(1)} %get-tuple-element.58), channel_id=1, source_target_pairs={{0,16},{1,17},{2,18},{3,19},{4,20},{5,21},{6,22},{7,23},{8,24},{9,... | collective-permute-start | bytes 1265672 | tf_op jit(solution)/shard_map/ppermute | solution.py:547
  13.0 3.8 %forward_wide.1 = (f32[16,64,128]{2,1,0:T(8,128)S(1)}, f32[16,72,256]{2,1,0:T(8,128)S(1)}, f32[16,72,256]{2,1,0:T(8,128)S(1)}, f32[16,2,128,128]{3,2,1,0:T(8,128...) custom-call(s32[2]{0:T(128)S(1)} %pad_add_fusion.place, ...), custom_call_target="tpu_custom_call", output_to_operand_aliasing={{5}: (3, {}), {7}: (4, {})} | custom-call | flops 4000000000 | bytes 8000000 | tf_op jit(solution)/shard_map/forward_wide/pallas_call | solution.py:243
  16.8 1.1 %collective-permute-start.2 = (f32[880,128]{1,0:T(8,128)S(1)}, f32[880,128]{1,0:T(8,128)S(1)}, u32[]{:S(2)}, u32[]{:S(2)}) collective-permute-start(f32[880,128]{1,0:T(8,128)S(1)} %get-tuple-element.59), channel_id=1, source_target_pairs={{0,24},{1,25},{2,26},{3,27},{4,28},{5,29},{6,30},{7,31},{8,0},{9,1... | collective-permute-start | bytes 1351688 | tf_op jit(solution)/shard_map/ppermute | solution.py:547
  18.0 1.0 collective-permute-start
  19.7 4.3 %collective-permute-done.1.n2 = f32[824,128]{1,0:T(8,128)S(1)} collective-permute-done((f32[824,128]{1,0:T(8,128)S(1)}, f32[824,128]{1,0:T(8,128)S(1)}, u32[]{:S(2)}, u32[]{:S(2)}) %collective-permute-start.1) | collective-permute-done | bytes 421920 | tf_op jit(solution)/shard_map/ppermute | solution.py:547
  24.0 0.9 sum_first.1
  24.8 8.3 %collective-permute-done.3.w2 = f32[56,128]{1,0:T(8,128)S(1)} collective-permute-done((f32[56,128]{1,0:T(8,128)S(1)}, f32[56,128]{1,0:T(8,128)S(1)}, u32[]{:S(2)}, u32[]{:S(2)}) %collective-permute-start.3) | collective-permute-done | bytes 28704 | tf_op jit(solution)/shard_map/ppermute | solution.py:547
  33.3 1.5 %sum_channels.1 = (f32[648,128]{1,0:T(8,128)S(1)}, f32[544,128]{1,0:T(8,128)S(1)}, f32[536,128]{1,0:T(8,128)S(1)}) custom-call(s32[2]{0:T(128)S(1)} %pad_add_fusion.place, f32[32,48,128]{2,1,0:T(8,128)S(1)} %get-tuple-element.60.first, f32[32,8,128]{2,1,0:T(8,128)S(1)} %get-tuple-element.61.first_edge, f32[880,128]{1,0:T(8,128)S(1)} %collective-permute-done.n1, ...), custom_call_target="tpu_custom_call" | custom-call | tf_op jit(solution)/shard_map/sum_channels/pallas_call | solution.py:405
  34.8 2.0 %collective-permute-start.4 = (f32[544,128]{1,0:T(8,128)S(1)}, f32[544,128]{1,0:T(8,128)S(1)}, u32[]{:S(2)}, u32[]{:S(2)}) collective-permute-start(f32[544,128]{1,0:T(8,128)S(1)} %get-tuple-element.65), channel_id=1, source_target_pairs={{0,1},{1,2},{2,3},{3,4},{4,5},{5,6},{6,7},{7,0},{8,9},{9,10},{10,1... | collective-permute-start | bytes 835592 | tf_op jit(solution)/shard_map/ppermute | solution.py:547
  36.7 4.2 %collective-permute-start.5 = (f32[536,128]{1,0:T(8,128)S(1)}, f32[536,128]{1,0:T(8,128)S(1)}, u32[]{:S(2)}, u32[]{:S(2)}) collective-permute-start(f32[536,128]{1,0:T(8,128)S(1)} %get-tuple-element.66), channel_id=1, source_target_pairs={{0,7},{1,0},{2,1},{3,2},{4,3},{5,4},{6,5},{7,6},{8,15},{9,8},{10,9... | collective-permute-start | bytes 823304 | tf_op jit(solution)/shard_map/ppermute | solution.py:547
  41.0 5.1 %collective-permute-done.5.down = f32[536,128]{1,0:T(8,128)S(1)} collective-permute-done((f32[536,128]{1,0:T(8,128)S(1)}, f32[536,128]{1,0:T(8,128)S(1)}, u32[]{:S(2)}, u32[]{:S(2)}) %collective-permute-start.5) | collective-permute-done | bytes 274464 | tf_op jit(solution)/shard_map/ppermute | solution.py:547
  46.6 4.6 %collective-permute-start.6 = (f32[216,128]{1,0:T(8,128)S(1)}, f32[216,128]{1,0:T(8,128)S(1)}, u32[]{:S(2)}, u32[]{:S(2)}) collective-permute-start(f32[216,128]{1,0:T(8,128)S(1)} %get-tuple-element.67), channel_id=1, source_target_pairs={{0,3},{1,4},{2,5},{3,6},{4,7},{5,0},{6,1},{7,2},{8,11},{9,12},{10,... | collective-permute-start | bytes 331784 | tf_op jit(solution)/shard_map/ppermute | solution.py:547
  51.8 5.5 %collective-permute-done.6.far = f32[216,128]{1,0:T(8,128)S(1)} collective-permute-done((f32[216,128]{1,0:T(8,128)S(1)}, f32[216,128]{1,0:T(8,128)S(1)}, u32[]{:S(2)}, u32[]{:S(2)}) %collective-permute-start.6) | collective-permute-done | bytes 110624 | tf_op jit(solution)/shard_map/ppermute | solution.py:547
  57.3 4.7 %collective-permute-done.7.back = f32[216,128]{1,0:T(8,128)S(1)} collective-permute-done((f32[216,128]{1,0:T(8,128)S(1)}, f32[216,128]{1,0:T(8,128)S(1)}, u32[]{:S(2)}, u32[]{:S(2)}) %collective-permute-start.7) | collective-permute-done | bytes 110624 | tf_op jit(solution)/shard_map/ppermute | solution.py:547
  62.2 3.8 %collective-permute-start.9 = (f32[144,128]{1,0:T(8,128)S(1)}, f32[144,128]{1,0:T(8,128)S(1)}, u32[]{:S(2)}, u32[]{:S(2)}) collective-permute-start(f32[144,128]{1,0:T(8,128)S(1)} %objects.1.own), channel_id=1, source_target_pairs={{0,3},{1,4},{2,5},{3,6},{4,7},{5,0},{6,1},{7,2},{8,11},{9,12},{10,... | collective-permute-start | bytes 221192 | tf_op jit(solution)/shard_map/ppermute | solution.py:547
  66.0 3.1 %collective-permute-done.8.ahead = f32[144,128]{1,0:T(8,128)S(1)} collective-permute-done((f32[144,128]{1,0:T(8,128)S(1)}, f32[144,128]{1,0:T(8,128)S(1)}, u32[]{:S(2)}, u32[]{:S(2)}) %collective-permute-start.8) | collective-permute-done | bytes 73760 | tf_op jit(solution)/shard_map/ppermute | solution.py:547
  69.1 1.3 %collective-permute-done.9.behind = f32[144,128]{1,0:T(8,128)S(1)} collective-permute-done((f32[144,128]{1,0:T(8,128)S(1)}, f32[144,128]{1,0:T(8,128)S(1)}, u32[]{:S(2)}, u32[]{:S(2)}) %collective-permute-start.9) | collective-permute-done | bytes 73760 | tf_op jit(solution)/shard_map/ppermute | solution.py:547
  70.4 1.5 %collective-permute-start.10 = (f32[360,128]{1,0:T(8,128)S(1)}, f32[360,128]{1,0:T(8,128)S(1)}, u32[]{:S(2)}, u32[]{:S(2)}) collective-permute-start(f32[360,128]{1,0:T(8,128)S(1)} %get-tuple-element.86), channel_id=1, source_target_pairs={{0,1},{1,2},{2,3},{3,4},{4,5},{5,6},{6,7},{7,0},{8,9},{9,10},{10,1... | collective-permute-start | bytes 552968 | tf_op jit(solution)/shard_map/ppermute | solution.py:547
  71.9 1.8 %collective-permute-start.11 = (f32[360,128]{1,0:T(8,128)S(1)}, f32[360,128]{1,0:T(8,128)S(1)}, u32[]{:S(2)}, u32[]{:S(2)}) collective-permute-start(f32[360,128]{1,0:T(8,128)S(1)} %get-tuple-element.85), channel_id=1, source_target_pairs={{0,7},{1,0},{2,1},{3,2},{4,3},{5,4},{6,5},{7,6},{8,15},{9,8},{10,9... | collective-permute-start | bytes 552968 | tf_op jit(solution)/shard_map/ppermute | solution.py:547
  73.8 3.4 %collective-permute-done.10.up = f32[360,128]{1,0:T(8,128)S(1)} collective-permute-done((f32[360,128]{1,0:T(8,128)S(1)}, f32[360,128]{1,0:T(8,128)S(1)}, u32[]{:S(2)}, u32[]{:S(2)}) %collective-permute-start.10) | collective-permute-done | bytes 184352 | tf_op jit(solution)/shard_map/ppermute | solution.py:547
  78.1 2.1 %collective-permute-start.15 = (f32[64,128]{1,0:T(8,128)S(1)}, f32[64,128]{1,0:T(8,128)S(1)}, u32[]{:S(2)}, u32[]{:S(2)}) collective-permute-start(f32[64,128]{1,0:T(8,128)S(1)} %get-tuple-element.78), channel_id=1, source_target_pairs={{0,8},{1,9},{2,10},{3,11},{4,12},{5,13},{6,14},{7,15},{8,16},{9,17... | collective-permute-start | bytes 98312 | tf_op jit(solution)/shard_map/ppermute | solution.py:547
  80.3 2.9 %collective-permute-start.16 = (f32[64,128]{1,0:T(8,128)S(1)}, f32[64,128]{1,0:T(8,128)S(1)}, u32[]{:S(2)}, u32[]{:S(2)}) collective-permute-start(f32[64,128]{1,0:T(8,128)S(1)} %get-tuple-element.79), channel_id=1, source_target_pairs={{0,16},{1,17},{2,18},{3,19},{4,20},{5,21},{6,22},{7,23},{8,24},{9,... | collective-permute-start | bytes 98312 | tf_op jit(solution)/shard_map/ppermute | solution.py:547
  83.2 1.3 %collective-permute-start.17 = (f32[64,128]{1,0:T(8,128)S(1)}, f32[64,128]{1,0:T(8,128)S(1)}, u32[]{:S(2)}, u32[]{:S(2)}) collective-permute-start(f32[64,128]{1,0:T(8,128)S(1)} %get-tuple-element.80), channel_id=1, source_target_pairs={{0,24},{1,25},{2,26},{3,27},{4,28},{5,29},{6,30},{7,31},{8,0},{9,1... | collective-permute-start | bytes 98312 | tf_op jit(solution)/shard_map/ppermute | solution.py:547
  85.9 2.0 %collective-permute-start.14 = (f32[512,128]{1,0:T(8,128)S(1)}, f32[512,128]{1,0:T(8,128)S(1)}, u32[]{:S(2)}, u32[]{:S(2)}) collective-permute-start(f32[512,128]{1,0:T(8,128)S(1)} %get-tuple-element.72), channel_id=1, source_target_pairs={{0,24},{1,25},{2,26},{3,27},{4,28},{5,29},{6,30},{7,31},{8,0},{9,1... | collective-permute-start | bytes 786440 | tf_op jit(solution)/shard_map/ppermute | solution.py:547
  88.0 5.6 %backward_wide.1 = (f32[16,32,128]{2,1,0:T(8,128)S(1)}, f32[2,128,128]{2,1,0:T(8,128)}, f32[2,128,128]{2,1,0:T(8,128)}) custom-call(s32[2]{0:T(128)S(1)} %pad_add_fusion.place, f32[16,64,128]{2,1,0:T(8,128)S(1)} %get-tuple-element.73.q_ref, f32[16,72,256]{2,1,0:T(8,128)S(1)} %get-tuple-element.74.s_ref, f32[16,72,256]{2,1,0:T(8,128)S(1)} %get-tuple-element.75.d_ref, ...), custom_call_target="tpu_custom_call" | custom-call | flops 4000000000 | bytes 8000000 | tf_op jit(solution)/shard_map/backward_wide/pallas_call | solution.py:515
  93.6 1.5 %collective-permute-done.12.refs_1_ = f32[512,128]{1,0:T(8,128)S(1)} collective-permute-done((f32[512,128]{1,0:T(8,128)S(1)}, f32[512,128]{1,0:T(8,128)S(1)}, u32[]{:S(2)}, u32[]{:S(2)}) %collective-permute-start.12) | collective-permute-done | bytes 262176 | tf_op jit(solution)/shard_map/ppermute | solution.py:547
  95.8 5.0 %backward_narrow.1 = f32[16,4096]{1,0:T(8,128)S(1)} custom-call(s32[2]{0:T(128)S(1)} %pad_add_fusion.place, f32[16,64,128]{2,1,0:T(8,128)S(1)} %get-tuple-element.50.q_ref, f32[16,72,256]{2,1,0:T(8,128)S(1)} %get-tuple-element.51.s_ref, f32[16,72,256]{2,1,0:T(8,128)S(1)} %get-tuple-element.52.d_ref, f32[16,2,128,128]{3,2,1,0:T(8,128)S(1)} %get-tuple-element.53.g_ref, ...), custom_call_target="tpu_custom_call" | custom-call | flops 4000000000 | bytes 8000000 | tf_op jit(solution)/shard_map/backward_narrow/pallas_call | solution.py:515
  100.8 1.7 %fusion.2 = f32[16,150]{1,0:T(8,128)} fusion(f32[16,4096]{1,0:T(8,128)S(1)} %backward_narrow.1, f32[150,4096]{1,0:T(8,128)S(1)} %copy-done), kind=kOutput, calls=%fused_computation.12 | convolution fusion | flops 58982400 | bytes 2729344 | tf_op jit(solution)/shard_map/dot_general | solution.py:613
  (75 shorter events, 5.6 us)
Async XLA Ops:
  0.6 3.3 %copy-start.22 = (f32[32,128]{1,0:T(8,128)S(1)}, f32[32,128]{1,0:T(8,128)}, u32[]{:S(2)}) copy-start(f32[32,128]{1,0:T(8,128)} %constant.113.clone.pupil_ref) | copy-start | bytes 49156
  0.7 3.3 %copy-start.6 = (bf16[256,256]{1,0:T(8,128)(2,1)S(1)}, bf16[256,256]{1,0:T(8,128)(2,1)}, u32[]{:S(2)}) copy-start(bf16[256,256]{1,0:T(8,128)(2,1)} %constant.95.clone.rest_3_) | copy-start | bytes 393220
  0.7 3.3 %copy-start.17 = (bf16[128,256]{1,0:T(8,128)(2,1)S(1)}, bf16[128,256]{1,0:T(8,128)(2,1)}, u32[]{:S(2)}) copy-start(bf16[128,256]{1,0:T(8,128)(2,1)} %constant.96.clone.rest_4_) | copy-start | bytes 196612
  5.7 7.4 %copy-start.2 = (f32[16,2,128,128]{3,2,1,0:T(8,128)S(1)}, f32[16,2,128,128]{3,2,1,0:T(8,128)}, u32[]{:S(2)}) copy-start(f32[16,2,128,128]{3,2,1,0:T(8,128)} %rest_2_.3) | copy-start | bytes 6291460
  9.7 14.2 %collective-permute-start.1 = (f32[824,128]{1,0:T(8,128)S(1)}, f32[824,128]{1,0:T(8,128)S(1)}, u32[]{:S(2)}, u32[]{:S(2)}) collective-permute-start(f32[824,128]{1,0:T(8,128)S(1)} %get-tuple-element.58), channel_id=1, source_target_pairs={{0,16},{1,17},{2,18},{3,19},{4,20},{5,21},{6,22},{7,23},{8,24},{9,... | collective-permute-start | bytes 1265672 | tf_op jit(solution)/shard_map/ppermute | solution.py:547
  16.8 16.3 %collective-permute-start.2 = (f32[880,128]{1,0:T(8,128)S(1)}, f32[880,128]{1,0:T(8,128)S(1)}, u32[]{:S(2)}, u32[]{:S(2)}) collective-permute-start(f32[880,128]{1,0:T(8,128)S(1)} %get-tuple-element.59), channel_id=1, source_target_pairs={{0,24},{1,25},{2,26},{3,27},{4,28},{5,29},{6,30},{7,31},{8,0},{9,1... | collective-permute-start | bytes 1351688 | tf_op jit(solution)/shard_map/ppermute | solution.py:547
  18.0 15.2 %collective-permute-start = (f32[880,128]{1,0:T(8,128)S(1)}, f32[880,128]{1,0:T(8,128)S(1)}, u32[]{:S(2)}, u32[]{:S(2)}) collective-permute-start(f32[880,128]{1,0:T(8,128)S(1)} %get-tuple-element.57), channel_id=1, source_target_pairs={{0,8},{1,9},{2,10},{3,11},{4,12},{5,13},{6,14},{7,15},{8,16},{9,17... | collective-permute-start | bytes 1351688 | tf_op jit(solution)/shard_map/ppermute | solution.py:547
  18.9 14.1 %collective-permute-start.3 = (f32[56,128]{1,0:T(8,128)S(1)}, f32[56,128]{1,0:T(8,128)S(1)}, u32[]{:S(2)}, u32[]{:S(2)}) collective-permute-start(f32[56,128]{1,0:T(8,128)S(1)} %get-tuple-element.63), channel_id=1, source_target_pairs={{0,16},{1,17},{2,18},{3,19},{4,20},{5,21},{6,22},{7,23},{8,24},{9,... | collective-permute-start | bytes 86024 | tf_op jit(solution)/shard_map/ppermute | solution.py:547
  33.2 54.8 %copy-start.4 = (bf16[256,256]{1,0:T(8,128)(2,1)S(1)}, bf16[256,256]{1,0:T(8,128)(2,1)}, u32[]{:S(2)}) copy-start(bf16[256,256]{1,0:T(8,128)(2,1)} %constant.103.clone.refs_5_.refs_6_) | copy-start | bytes 393220
  33.2 54.8 %copy-start.5 = (bf16[256,256]{1,0:T(8,128)(2,1)S(1)}, bf16[256,256]{1,0:T(8,128)(2,1)}, u32[]{:S(2)}) copy-start(bf16[256,256]{1,0:T(8,128)(2,1)} %constant.104.clone.refs_6_.refs_7_) | copy-start | bytes 393220
  33.2 54.8 %copy-start.11 = (bf16[128,144]{1,0:T(8,128)(2,1)S(1)}, bf16[128,144]{1,0:T(8,128)(2,1)}, u32[]{:S(2)}) copy-start(bf16[128,144]{1,0:T(8,128)(2,1)} %constant.105.clone.refs_7_.refs_8_) | copy-start | bytes 110596
  33.2 54.8 %copy-start.12 = (bf16[128,144]{1,0:T(8,128)(2,1)S(1)}, bf16[128,144]{1,0:T(8,128)(2,1)}, u32[]{:S(2)}) copy-start(bf16[128,144]{1,0:T(8,128)(2,1)} %constant.106.clone.refs_8_.refs_9_) | copy-start | bytes 110596
  33.2 54.8 %copy-start.13 = (bf16[128,256]{1,0:T(8,128)(2,1)S(1)}, bf16[128,256]{1,0:T(8,128)(2,1)}, u32[]{:S(2)}) copy-start(bf16[128,256]{1,0:T(8,128)(2,1)} %constant.107.clone.refs_9_.refs_10_) | copy-start | bytes 196612
  33.2 54.8 %copy-start.14 = (bf16[128,256]{1,0:T(8,128)(2,1)S(1)}, bf16[128,256]{1,0:T(8,128)(2,1)}, u32[]{:S(2)}) copy-start(bf16[128,256]{1,0:T(8,128)(2,1)} %constant.108.clone.refs_10_.refs_11_) | copy-start | bytes 196612
  33.2 54.8 %copy-start.15 = (bf16[256,128]{1,0:T(8,128)(2,1)S(1)}, bf16[256,128]{1,0:T(8,128)(2,1)}, u32[]{:S(2)}) copy-start(bf16[256,128]{1,0:T(8,128)(2,1)} %constant.109.clone.refs_11_.refs_12_) | copy-start | bytes 196612
  33.2 54.8 %copy-start.16 = (bf16[256,128]{1,0:T(8,128)(2,1)S(1)}, bf16[256,128]{1,0:T(8,128)(2,1)}, u32[]{:S(2)}) copy-start(bf16[256,128]{1,0:T(8,128)(2,1)} %constant.110.clone.refs_12_.refs_13_) | copy-start | bytes 196612
  33.2 54.8 %copy-start.20 = (bf16[128,128]{1,0:T(8,128)(2,1)S(1)}, bf16[128,128]{1,0:T(8,128)(2,1)}, u32[]{:S(2)}) copy-start(bf16[128,128]{1,0:T(8,128)(2,1)} %constant.111.clone.refs_13_.refs_14_) | copy-start | bytes 98308
  33.2 54.8 %copy-start.21 = (bf16[128,128]{1,0:T(8,128)(2,1)S(1)}, bf16[128,128]{1,0:T(8,128)(2,1)}, u32[]{:S(2)}) copy-start(bf16[128,128]{1,0:T(8,128)(2,1)} %constant.112.clone.refs_14_.refs_15_) | copy-start | bytes 98308
  34.8 11.9 %collective-permute-start.4 = (f32[544,128]{1,0:T(8,128)S(1)}, f32[544,128]{1,0:T(8,128)S(1)}, u32[]{:S(2)}, u32[]{:S(2)}) collective-permute-start(f32[544,128]{1,0:T(8,128)S(1)} %get-tuple-element.65), channel_id=1, source_target_pairs={{0,1},{1,2},{2,3},{3,4},{4,5},{5,6},{6,7},{7,0},{8,9},{9,10},{10,1... | collective-permute-start | bytes 835592 | tf_op jit(solution)/shard_map/ppermute | solution.py:547
  36.7 9.3 %collective-permute-start.5 = (f32[536,128]{1,0:T(8,128)S(1)}, f32[536,128]{1,0:T(8,128)S(1)}, u32[]{:S(2)}, u32[]{:S(2)}) collective-permute-start(f32[536,128]{1,0:T(8,128)S(1)} %get-tuple-element.66), channel_id=1, source_target_pairs={{0,7},{1,0},{2,1},{3,2},{4,3},{5,4},{6,5},{7,6},{8,15},{9,8},{10,9... | collective-permute-start | bytes 823304 | tf_op jit(solution)/shard_map/ppermute | solution.py:547
  46.6 10.7 %collective-permute-start.6 = (f32[216,128]{1,0:T(8,128)S(1)}, f32[216,128]{1,0:T(8,128)S(1)}, u32[]{:S(2)}, u32[]{:S(2)}) collective-permute-start(f32[216,128]{1,0:T(8,128)S(1)} %get-tuple-element.67), channel_id=1, source_target_pairs={{0,3},{1,4},{2,5},{3,6},{4,7},{5,0},{6,1},{7,2},{8,11},{9,12},{10,... | collective-permute-start | bytes 331784 | tf_op jit(solution)/shard_map/ppermute | solution.py:547
  51.2 10.8 %collective-permute-start.7 = (f32[216,128]{1,0:T(8,128)S(1)}, f32[216,128]{1,0:T(8,128)S(1)}, u32[]{:S(2)}, u32[]{:S(2)}) collective-permute-start(f32[216,128]{1,0:T(8,128)S(1)} %get-tuple-element.68), channel_id=1, source_target_pairs={{0,5},{1,6},{2,7},{3,0},{4,1},{5,2},{6,3},{7,4},{8,13},{9,14},{10,... | collective-permute-start | bytes 331784 | tf_op jit(solution)/shard_map/ppermute | solution.py:547
  62.1 7.0 %collective-permute-start.8 = (f32[144,128]{1,0:T(8,128)S(1)}, f32[144,128]{1,0:T(8,128)S(1)}, u32[]{:S(2)}, u32[]{:S(2)}) collective-permute-start(f32[144,128]{1,0:T(8,128)S(1)} %objects.1.own), channel_id=1, source_target_pairs={{0,5},{1,6},{2,7},{3,0},{4,1},{5,2},{6,3},{7,4},{8,13},{9,14},{10,... | collective-permute-start | bytes 221192 | tf_op jit(solution)/shard_map/ppermute | solution.py:547
  62.2 8.2 %collective-permute-start.9 = (f32[144,128]{1,0:T(8,128)S(1)}, f32[144,128]{1,0:T(8,128)S(1)}, u32[]{:S(2)}, u32[]{:S(2)}) collective-permute-start(f32[144,128]{1,0:T(8,128)S(1)} %objects.1.own), channel_id=1, source_target_pairs={{0,3},{1,4},{2,5},{3,6},{4,7},{5,0},{6,1},{7,2},{8,11},{9,12},{10,... | collective-permute-start | bytes 221192 | tf_op jit(solution)/shard_map/ppermute | solution.py:547
  70.4 6.8 %collective-permute-start.10 = (f32[360,128]{1,0:T(8,128)S(1)}, f32[360,128]{1,0:T(8,128)S(1)}, u32[]{:S(2)}, u32[]{:S(2)}) collective-permute-start(f32[360,128]{1,0:T(8,128)S(1)} %get-tuple-element.86), channel_id=1, source_target_pairs={{0,1},{1,2},{2,3},{3,4},{4,5},{5,6},{6,7},{7,0},{8,9},{9,10},{10,1... | collective-permute-start | bytes 552968 | tf_op jit(solution)/shard_map/ppermute | solution.py:547
  71.9 5.5 %collective-permute-start.11 = (f32[360,128]{1,0:T(8,128)S(1)}, f32[360,128]{1,0:T(8,128)S(1)}, u32[]{:S(2)}, u32[]{:S(2)}) collective-permute-start(f32[360,128]{1,0:T(8,128)S(1)} %get-tuple-element.85), channel_id=1, source_target_pairs={{0,7},{1,0},{2,1},{3,2},{4,3},{5,4},{6,5},{7,6},{8,15},{9,8},{10,9... | collective-permute-start | bytes 552968 | tf_op jit(solution)/shard_map/ppermute | solution.py:547
  78.1 7.8 %collective-permute-start.15 = (f32[64,128]{1,0:T(8,128)S(1)}, f32[64,128]{1,0:T(8,128)S(1)}, u32[]{:S(2)}, u32[]{:S(2)}) collective-permute-start(f32[64,128]{1,0:T(8,128)S(1)} %get-tuple-element.78), channel_id=1, source_target_pairs={{0,8},{1,9},{2,10},{3,11},{4,12},{5,13},{6,14},{7,15},{8,16},{9,17... | collective-permute-start | bytes 98312 | tf_op jit(solution)/shard_map/ppermute | solution.py:547
  80.3 7.6 %collective-permute-start.16 = (f32[64,128]{1,0:T(8,128)S(1)}, f32[64,128]{1,0:T(8,128)S(1)}, u32[]{:S(2)}, u32[]{:S(2)}) collective-permute-start(f32[64,128]{1,0:T(8,128)S(1)} %get-tuple-element.79), channel_id=1, source_target_pairs={{0,16},{1,17},{2,18},{3,19},{4,20},{5,21},{6,22},{7,23},{8,24},{9,... | collective-permute-start | bytes 98312 | tf_op jit(solution)/shard_map/ppermute | solution.py:547
  83.2 4.7 %collective-permute-start.17 = (f32[64,128]{1,0:T(8,128)S(1)}, f32[64,128]{1,0:T(8,128)S(1)}, u32[]{:S(2)}, u32[]{:S(2)}) collective-permute-start(f32[64,128]{1,0:T(8,128)S(1)} %get-tuple-element.80), channel_id=1, source_target_pairs={{0,24},{1,25},{2,26},{3,27},{4,28},{5,29},{6,30},{7,31},{8,0},{9,1... | collective-permute-start | bytes 98312 | tf_op jit(solution)/shard_map/ppermute | solution.py:547
  84.5 10.6 %collective-permute-start.12 = (f32[512,128]{1,0:T(8,128)S(1)}, f32[512,128]{1,0:T(8,128)S(1)}, u32[]{:S(2)}, u32[]{:S(2)}) collective-permute-start(f32[512,128]{1,0:T(8,128)S(1)} %get-tuple-element.70), channel_id=1, source_target_pairs={{0,8},{1,9},{2,10},{3,11},{4,12},{5,13},{6,14},{7,15},{8,16},{9,17... | collective-permute-start | bytes 786440 | tf_op jit(solution)/shard_map/ppermute | solution.py:547
  85.2 9.8 %collective-permute-start.13 = (f32[512,128]{1,0:T(8,128)S(1)}, f32[512,128]{1,0:T(8,128)S(1)}, u32[]{:S(2)}, u32[]{:S(2)}) collective-permute-start(f32[512,128]{1,0:T(8,128)S(1)} %get-tuple-element.71), channel_id=1, source_target_pairs={{0,16},{1,17},{2,18},{3,19},{4,20},{5,21},{6,22},{7,23},{8,24},{9,... | collective-permute-start | bytes 786440 | tf_op jit(solution)/shard_map/ppermute | solution.py:547
  85.9 9.8 %collective-permute-start.14 = (f32[512,128]{1,0:T(8,128)S(1)}, f32[512,128]{1,0:T(8,128)S(1)}, u32[]{:S(2)}, u32[]{:S(2)}) collective-permute-start(f32[512,128]{1,0:T(8,128)S(1)} %get-tuple-element.72), channel_id=1, source_target_pairs={{0,24},{1,25},{2,26},{3,27},{4,28},{5,29},{6,30},{7,31},{8,0},{9,1... | collective-permute-start | bytes 786440 | tf_op jit(solution)/shard_map/ppermute | solution.py:547
  (10 other events, 27.9 us)

commit v6 on v5

--- a/solution.py
+++ b/solution.py
@@ -237,7 +237,6 @@
 
 
 def forward(wide, place, phase, pupil, extra, images, tables):
-    camera = 0 if wide else 1
     outs = [shape(FRAMES, PUP, 2 * PUP)] + [shape(FRAMES, ROWS, 2 * SIZE)] * 2 + [shape(FRAMES, 2, SIZE, SIZE)]
     terms = [shape(W_ROWS if wide and not base else Y_ROWS + base, SIZE) for base in BASE]
     return pl.pallas_call(
@@ -245,7 +244,7 @@
         grid=(FRAMES // STEP,),
         in_specs=[smem(), pl.BlockSpec((STEP, PUP // 2, SIZE), lambda i: (i, 0, 0)), whole(pupil)]
         + [pl.BlockSpec(memory_space=pl.ANY) if wide else whole(e) for e in extra]
-        + [pl.BlockSpec((STEP, 1, SIZE, SIZE), lambda i: (i, camera, 0, 0))]
+        + [pl.BlockSpec((STEP, 1, SIZE, SIZE), lambda i: (i, 0, 0, 0))]
         + [whole(t) for t in tables],
         out_specs=[pl.BlockSpec((STEP, PUP, 2 * PUP), lambda i: (i, 0, 0))]
         + [pl.BlockSpec((STEP, ROWS, 2 * SIZE), lambda i: (i, 0, 0))] * 2
@@ -559,7 +558,7 @@
     pupil = jnp.asarray(pupil.reshape(PUP // 2, SIZE))
     extra = [diversity.reshape(PUP // 2, SIZE), own_ids]
 
-    *narrow_kept, n0, n1, n2, n3 = forward(False, place, phase, pupil, extra, images, tables_f)
+    *narrow_kept, n0, n1, n2, n3 = forward(False, place, phase, pupil, extra, images[:, 1:], tables_f)
     *wide_kept, w0, n1, w2, n3 = forward(True, place, phase, pupil, [n1, n3], images, tables_f)
     n2 = send(n2, "y", 2)
     reading = [pltpu.SMEM((2, 8, SIZE), F32), pltpu.SemaphoreType.DMA((2,))]

time: 103 us -> 113 us (1.097)
  local copies, waits for them, and re-layouts: 3.35 us -> 11.9 us
    unnamed x49 -> x55, local copies, waits for them, and re-layouts: 3.33 us -> 11.1 us
  transfers between devices with their start and end apart: 18 -> 18, of which waited for: 13 -> 13; matrix products, arithmetic and copies ran while one was open for 0% -> 0% of each run, Pallas kernels for 10% -> 9%
where the time goes in v6:
time: 113 us; the launch traced here: 112 us
  waiting for transfers between devices  38.8 us (34%)
  starting transfers between devices  34.3 us (30%)
  Pallas kernels  21.6 us (19%)
  local copies, waits for them, and re-layouts  11.9 us (11%)
  matrix products  3.27 us (3%)
    ppermute x18, waiting for transfers between devices, send(): return lax.ppermute(x, 'chan', along(axis, shift))  38.8 us
    ppermute x18, starting transfers between devices, send(): return lax.ppermute(x, 'chan', along(axis, shift))  34.3 us
    unnamed x55, local copies, waits for them, and re-layouts  11.1 us
    pallas_call x2, Pallas kernels, backward(): pl.pallas_call(functools.partial(backward_kernel, wide), grid=(FRAMES //...  10.5 us
    pallas_call x2, Pallas kernels, forward(): pl.pallas_call(functools.partial(forward_kernel, wide), grid=(FRAMES // S...  7.95 us
    pallas_call x5, Pallas kernels, plain(): pl.pallas_call(kernel, in_specs=[smem()] * len(smems) + [pl.BlockSpec(mem...  3.1 us
  transfers between devices with their start and end apart: 18, of which 13 were waited for; matrix products, arithmetic and copies ran while one was open for 0% of the time, Pallas kernels for 9%

profile of v6, /device:TPU:2, one launch (start us, length us, event | category | flops | bytes accessed | tf_op | source)
XLA Modules:
  0.0 111.5 jit_solution(6544621310799981097)
XLA Ops:
  0.7 1.7 %copy-done = f32[150,4096]{1,0:T(8,128)S(1)} copy-done((f32[150,4096]{1,0:T(8,128)S(1)}, f32[150,4096]{1,0:T(8,128)}, u32[]{:S(2)}) %copy-start) | copy-done | bytes 2457624
  2.3 1.6 %convolution_bitcast_fusion = f32[2,8,32,128]{3,1,2,0:T(8,128)S(1)} fusion(f32[16,150]{1,0:T(8,128)} %param.26, f32[150,4096]{1,0:T(8,128)S(1)} %copy-done), kind=kOutput, calls=%fused_computation | convolution fusion | flops 58982400 | bytes 2729344 | tf_op jit(solution)/shard_map/dot_general | solution.py:555
  6.1 0.9 copy-done.3
  8.8 0.9 copy-done.10
  14.7 4.1 %forward_narrow.1 = (f32[16,64,128]{2,1,0:T(8,128)S(1)}, f32[16,72,256]{2,1,0:T(8,128)S(1)}, f32[16,72,256]{2,1,0:T(8,128)S(1)}, f32[16,2,128,128]{3,2,1,0:T(8,1...) custom-call(s32[2]{0:T(128)S(1)} %pad_add_fusion.place, ...), custom_call_target="tpu_custom_call" | custom-call | flops 4000000000 | bytes 8000000 | tf_op jit(solution)/shard_map/forward_narrow/pallas_call | solution.py:242
  18.8 3.3 %collective-permute-start.1 = (f32[824,128]{1,0:T(8,128)S(1)}, f32[824,128]{1,0:T(8,128)S(1)}, u32[]{:S(2)}, u32[]{:S(2)}) collective-permute-start(f32[824,128]{1,0:T(8,128)S(1)} %get-tuple-element.58), channel_id=1, source_target_pairs={{0,16},{1,17},{2,18},{3,19},{4,20},{5,21},{6,22},{7,23},{8,24},{9,... | collective-permute-start | bytes 1265672 | tf_op jit(solution)/shard_map/ppermute | solution.py:546
  22.1 3.8 %forward_wide.1 = (f32[16,64,128]{2,1,0:T(8,128)S(1)}, f32[16,72,256]{2,1,0:T(8,128)S(1)}, f32[16,72,256]{2,1,0:T(8,128)S(1)}, f32[16,2,128,128]{3,2,1,0:T(8,128...) custom-call(s32[2]{0:T(128)S(1)} %pad_add_fusion.place, ...), custom_call_target="tpu_custom_call", output_to_operand_aliasing={{5}: (3, {}), {7}: (4, {})} | custom-call | flops 4000000000 | bytes 8000000 | tf_op jit(solution)/shard_map/forward_wide/pallas_call | solution.py:242
  25.9 1.1 %collective-permute-start.2 = (f32[880,128]{1,0:T(8,128)S(1)}, f32[880,128]{1,0:T(8,128)S(1)}, u32[]{:S(2)}, u32[]{:S(2)}) collective-permute-start(f32[880,128]{1,0:T(8,128)S(1)} %get-tuple-element.59), channel_id=1, source_target_pairs={{0,24},{1,25},{2,26},{3,27},{4,28},{5,29},{6,30},{7,31},{8,0},{9,1... | collective-permute-start | bytes 1351688 | tf_op jit(solution)/shard_map/ppermute | solution.py:546
  27.1 1.0 collective-permute-start
  28.8 4.2 %collective-permute-done.1.n2 = f32[824,128]{1,0:T(8,128)S(1)} collective-permute-done((f32[824,128]{1,0:T(8,128)S(1)}, f32[824,128]{1,0:T(8,128)S(1)}, u32[]{:S(2)}, u32[]{:S(2)}) %collective-permute-start.1) | collective-permute-done | bytes 421920 | tf_op jit(solution)/shard_map/ppermute | solution.py:546
  33.9 8.3 %collective-permute-done.3.w2 = f32[56,128]{1,0:T(8,128)S(1)} collective-permute-done((f32[56,128]{1,0:T(8,128)S(1)}, f32[56,128]{1,0:T(8,128)S(1)}, u32[]{:S(2)}, u32[]{:S(2)}) %collective-permute-start.3) | collective-permute-done | bytes 28704 | tf_op jit(solution)/shard_map/ppermute | solution.py:546
  42.3 1.5 %sum_channels.1 = (f32[648,128]{1,0:T(8,128)S(1)}, f32[544,128]{1,0:T(8,128)S(1)}, f32[536,128]{1,0:T(8,128)S(1)}) custom-call(s32[2]{0:T(128)S(1)} %pad_add_fusion.place, f32[32,48,128]{2,1,0:T(8,128)S(1)} %get-tuple-element.60.first, f32[32,8,128]{2,1,0:T(8,128)S(1)} %get-tuple-element.61.first_edge, f32[880,128]{1,0:T(8,128)S(1)} %collective-permute-done.n1, ...), custom_call_target="tpu_custom_call" | custom-call | tf_op jit(solution)/shard_map/sum_channels/pallas_call | solution.py:404
  43.8 2.0 %collective-permute-start.4 = (f32[544,128]{1,0:T(8,128)S(1)}, f32[544,128]{1,0:T(8,128)S(1)}, u32[]{:S(2)}, u32[]{:S(2)}) collective-permute-start(f32[544,128]{1,0:T(8,128)S(1)} %get-tuple-element.65), channel_id=1, source_target_pairs={{0,1},{1,2},{2,3},{3,4},{4,5},{5,6},{6,7},{7,0},{8,9},{9,10},{10,1... | collective-permute-start | bytes 835592 | tf_op jit(solution)/shard_map/ppermute | solution.py:546
  45.8 4.2 %collective-permute-start.5 = (f32[536,128]{1,0:T(8,128)S(1)}, f32[536,128]{1,0:T(8,128)S(1)}, u32[]{:S(2)}, u32[]{:S(2)}) collective-permute-start(f32[536,128]{1,0:T(8,128)S(1)} %get-tuple-element.66), channel_id=1, source_target_pairs={{0,7},{1,0},{2,1},{3,2},{4,3},{5,4},{6,5},{7,6},{8,15},{9,8},{10,9... | collective-permute-start | bytes 823304 | tf_op jit(solution)/shard_map/ppermute | solution.py:546
  50.0 5.1 %collective-permute-done.5.down = f32[536,128]{1,0:T(8,128)S(1)} collective-permute-done((f32[536,128]{1,0:T(8,128)S(1)}, f32[536,128]{1,0:T(8,128)S(1)}, u32[]{:S(2)}, u32[]{:S(2)}) %collective-permute-start.5) | collective-permute-done | bytes 274464 | tf_op jit(solution)/shard_map/ppermute | solution.py:546
  55.7 4.6 %collective-permute-start.6 = (f32[216,128]{1,0:T(8,128)S(1)}, f32[216,128]{1,0:T(8,128)S(1)}, u32[]{:S(2)}, u32[]{:S(2)}) collective-permute-start(f32[216,128]{1,0:T(8,128)S(1)} %get-tuple-element.67), channel_id=1, source_target_pairs={{0,3},{1,4},{2,5},{3,6},{4,7},{5,0},{6,1},{7,2},{8,11},{9,12},{10,... | collective-permute-start | bytes 331784 | tf_op jit(solution)/shard_map/ppermute | solution.py:546
  60.8 5.4 %collective-permute-done.6.far = f32[216,128]{1,0:T(8,128)S(1)} collective-permute-done((f32[216,128]{1,0:T(8,128)S(1)}, f32[216,128]{1,0:T(8,128)S(1)}, u32[]{:S(2)}, u32[]{:S(2)}) %collective-permute-start.6) | collective-permute-done | bytes 110624 | tf_op jit(solution)/shard_map/ppermute | solution.py:546
  66.3 4.8 %collective-permute-done.7.back = f32[216,128]{1,0:T(8,128)S(1)} collective-permute-done((f32[216,128]{1,0:T(8,128)S(1)}, f32[216,128]{1,0:T(8,128)S(1)}, u32[]{:S(2)}, u32[]{:S(2)}) %collective-permute-start.7) | collective-permute-done | bytes 110624 | tf_op jit(solution)/shard_map/ppermute | solution.py:546
  71.2 3.8 %collective-permute-start.9 = (f32[144,128]{1,0:T(8,128)S(1)}, f32[144,128]{1,0:T(8,128)S(1)}, u32[]{:S(2)}, u32[]{:S(2)}) collective-permute-start(f32[144,128]{1,0:T(8,128)S(1)} %objects.1.own), channel_id=1, source_target_pairs={{0,3},{1,4},{2,5},{3,6},{4,7},{5,0},{6,1},{7,2},{8,11},{9,12},{10,... | collective-permute-start | bytes 221192 | tf_op jit(solution)/shard_map/ppermute | solution.py:546
  75.0 3.1 %collective-permute-done.8.ahead = f32[144,128]{1,0:T(8,128)S(1)} collective-permute-done((f32[144,128]{1,0:T(8,128)S(1)}, f32[144,128]{1,0:T(8,128)S(1)}, u32[]{:S(2)}, u32[]{:S(2)}) %collective-permute-start.8) | collective-permute-done | bytes 73760 | tf_op jit(solution)/shard_map/ppermute | solution.py:546
  78.1 1.2 %collective-permute-done.9.behind = f32[144,128]{1,0:T(8,128)S(1)} collective-permute-done((f32[144,128]{1,0:T(8,128)S(1)}, f32[144,128]{1,0:T(8,128)S(1)}, u32[]{:S(2)}, u32[]{:S(2)}) %collective-permute-start.9) | collective-permute-done | bytes 73760 | tf_op jit(solution)/shard_map/ppermute | solution.py:546
  79.4 1.7 %collective-permute-start.10 = (f32[360,128]{1,0:T(8,128)S(1)}, f32[360,128]{1,0:T(8,128)S(1)}, u32[]{:S(2)}, u32[]{:S(2)}) collective-permute-start(f32[360,128]{1,0:T(8,128)S(1)} %get-tuple-element.86), channel_id=1, source_target_pairs={{0,1},{1,2},{2,3},{3,4},{4,5},{5,6},{6,7},{7,0},{8,9},{9,10},{10,1... | collective-permute-start | bytes 552968 | tf_op jit(solution)/shard_map/ppermute | solution.py:546
  81.0 1.7 %collective-permute-start.11 = (f32[360,128]{1,0:T(8,128)S(1)}, f32[360,128]{1,0:T(8,128)S(1)}, u32[]{:S(2)}, u32[]{:S(2)}) collective-permute-start(f32[360,128]{1,0:T(8,128)S(1)} %get-tuple-element.85), channel_id=1, source_target_pairs={{0,7},{1,0},{2,1},{3,2},{4,3},{5,4},{6,5},{7,6},{8,15},{9,8},{10,9... | collective-permute-start | bytes 552968 | tf_op jit(solution)/shard_map/ppermute | solution.py:546
  82.8 3.4 %collective-permute-done.10.up = f32[360,128]{1,0:T(8,128)S(1)} collective-permute-done((f32[360,128]{1,0:T(8,128)S(1)}, f32[360,128]{1,0:T(8,128)S(1)}, u32[]{:S(2)}, u32[]{:S(2)}) %collective-permute-start.10) | collective-permute-done | bytes 184352 | tf_op jit(solution)/shard_map/ppermute | solution.py:546
  87.3 2.1 %collective-permute-start.15 = (f32[64,128]{1,0:T(8,128)S(1)}, f32[64,128]{1,0:T(8,128)S(1)}, u32[]{:S(2)}, u32[]{:S(2)}) collective-permute-start(f32[64,128]{1,0:T(8,128)S(1)} %get-tuple-element.78), channel_id=1, source_target_pairs={{0,8},{1,9},{2,10},{3,11},{4,12},{5,13},{6,14},{7,15},{8,16},{9,17... | collective-permute-start | bytes 98312 | tf_op jit(solution)/shard_map/ppermute | solution.py:546
  89.3 2.9 %collective-permute-start.16 = (f32[64,128]{1,0:T(8,128)S(1)}, f32[64,128]{1,0:T(8,128)S(1)}, u32[]{:S(2)}, u32[]{:S(2)}) collective-permute-start(f32[64,128]{1,0:T(8,128)S(1)} %get-tuple-element.79), channel_id=1, source_target_pairs={{0,16},{1,17},{2,18},{3,19},{4,20},{5,21},{6,22},{7,23},{8,24},{9,... | collective-permute-start | bytes 98312 | tf_op jit(solution)/shard_map/ppermute | solution.py:546
  92.2 1.3 %collective-permute-start.17 = (f32[64,128]{1,0:T(8,128)S(1)}, f32[64,128]{1,0:T(8,128)S(1)}, u32[]{:S(2)}, u32[]{:S(2)}) collective-permute-start(f32[64,128]{1,0:T(8,128)S(1)} %get-tuple-element.80), channel_id=1, source_target_pairs={{0,24},{1,25},{2,26},{3,27},{4,28},{5,29},{6,30},{7,31},{8,0},{9,1... | collective-permute-start | bytes 98312 | tf_op jit(solution)/shard_map/ppermute | solution.py:546
  95.0 1.9 %collective-permute-start.14 = (f32[512,128]{1,0:T(8,128)S(1)}, f32[512,128]{1,0:T(8,128)S(1)}, u32[]{:S(2)}, u32[]{:S(2)}) collective-permute-start(f32[512,128]{1,0:T(8,128)S(1)} %get-tuple-element.72), channel_id=1, source_target_pairs={{0,24},{1,25},{2,26},{3,27},{4,28},{5,29},{6,30},{7,31},{8,0},{9,1... | collective-permute-start | bytes 786440 | tf_op jit(solution)/shard_map/ppermute | solution.py:546
  97.1 5.6 %backward_wide.1 = (f32[16,32,128]{2,1,0:T(8,128)S(1)}, f32[2,128,128]{2,1,0:T(8,128)}, f32[2,128,128]{2,1,0:T(8,128)}) custom-call(s32[2]{0:T(128)S(1)} %pad_add_fusion.place, f32[16,64,128]{2,1,0:T(8,128)S(1)} %get-tuple-element.73.q_ref, f32[16,72,256]{2,1,0:T(8,128)S(1)} %get-tuple-element.74.s_ref, f32[16,72,256]{2,1,0:T(8,128)S(1)} %get-tuple-element.75.d_ref, ...), custom_call_target="tpu_custom_call" | custom-call | flops 4000000000 | bytes 8000000 | tf_op jit(solution)/shard_map/backward_wide/pallas_call | solution.py:514
  102.6 1.5 %collective-permute-done.12.refs_1_ = f32[512,128]{1,0:T(8,128)S(1)} collective-permute-done((f32[512,128]{1,0:T(8,128)S(1)}, f32[512,128]{1,0:T(8,128)S(1)}, u32[]{:S(2)}, u32[]{:S(2)}) %collective-permute-start.12) | collective-permute-done | bytes 262176 | tf_op jit(solution)/shard_map/ppermute | solution.py:546
  104.9 5.0 %backward_narrow.1 = f32[16,4096]{1,0:T(8,128)S(1)} custom-call(s32[2]{0:T(128)S(1)} %pad_add_fusion.place, f32[16,64,128]{2,1,0:T(8,128)S(1)} %get-tuple-element.50.q_ref, f32[16,72,256]{2,1,0:T(8,128)S(1)} %get-tuple-element.51.s_ref, f32[16,72,256]{2,1,0:T(8,128)S(1)} %get-tuple-element.52.d_ref, f32[16,2,128,128]{3,2,1,0:T(8,128)S(1)} %get-tuple-element.53.g_ref, ...), custom_call_target="tpu_custom_call" | custom-call | flops 4000000000 | bytes 8000000 | tf_op jit(solution)/shard_map/backward_narrow/pallas_call | solution.py:514
  109.8 1.7 %fusion.2 = f32[16,150]{1,0:T(8,128)} fusion(f32[16,4096]{1,0:T(8,128)S(1)} %backward_narrow.1, f32[150,4096]{1,0:T(8,128)S(1)} %copy-done), kind=kOutput, calls=%fused_computation.12 | convolution fusion | flops 58982400 | bytes 2729344 | tf_op jit(solution)/shard_map/dot_general | solution.py:612
  (82 shorter events, 15.3 us)
Async XLA Ops:
  0.6 4.0 %copy-start.26 = (s32[16,1]{0,1:T(1,128)S(1)}, s32[16,1]{0,1:T(1,128)}, u32[]{:S(2)}) copy-start(s32[16,1]{0,1:T(1,128)} %param.30) | copy-start | bytes 196
  14.7 7.4 %copy-start.2 = (f32[16,2,128,128]{3,2,1,0:T(8,128)S(1)}, f32[16,2,128,128]{3,2,1,0:T(8,128)}, u32[]{:S(2)}) copy-start(f32[16,2,128,128]{3,2,1,0:T(8,128)} %rest_2_.1) | copy-start | bytes 6291460
  14.7 7.4 %copy-start.8 = (bf16[256,256]{1,0:T(8,128)(2,1)S(1)}, bf16[256,256]{1,0:T(8,128)(2,1)}, u32[]{:S(2)}) copy-start(bf16[256,256]{1,0:T(8,128)(2,1)} %constant.95.clone.rest_3_) | copy-start | bytes 393220
  14.7 7.4 %copy-start.20 = (bf16[128,256]{1,0:T(8,128)(2,1)S(1)}, bf16[128,256]{1,0:T(8,128)(2,1)}, u32[]{:S(2)}) copy-start(bf16[128,256]{1,0:T(8,128)(2,1)} %constant.96.clone.rest_4_) | copy-start | bytes 196612
  18.8 14.2 %collective-permute-start.1 = (f32[824,128]{1,0:T(8,128)S(1)}, f32[824,128]{1,0:T(8,128)S(1)}, u32[]{:S(2)}, u32[]{:S(2)}) collective-permute-start(f32[824,128]{1,0:T(8,128)S(1)} %get-tuple-element.58), channel_id=1, source_target_pairs={{0,16},{1,17},{2,18},{3,19},{4,20},{5,21},{6,22},{7,23},{8,24},{9,... | collective-permute-start | bytes 1265672 | tf_op jit(solution)/shard_map/ppermute | solution.py:546
  25.9 16.3 %collective-permute-start.2 = (f32[880,128]{1,0:T(8,128)S(1)}, f32[880,128]{1,0:T(8,128)S(1)}, u32[]{:S(2)}, u32[]{:S(2)}) collective-permute-start(f32[880,128]{1,0:T(8,128)S(1)} %get-tuple-element.59), channel_id=1, source_target_pairs={{0,24},{1,25},{2,26},{3,27},{4,28},{5,29},{6,30},{7,31},{8,0},{9,1... | collective-permute-start | bytes 1351688 | tf_op jit(solution)/shard_map/ppermute | solution.py:546
  27.1 15.2 %collective-permute-start = (f32[880,128]{1,0:T(8,128)S(1)}, f32[880,128]{1,0:T(8,128)S(1)}, u32[]{:S(2)}, u32[]{:S(2)}) collective-permute-start(f32[880,128]{1,0:T(8,128)S(1)} %get-tuple-element.57), channel_id=1, source_target_pairs={{0,8},{1,9},{2,10},{3,11},{4,12},{5,13},{6,14},{7,15},{8,16},{9,17... | collective-permute-start | bytes 1351688 | tf_op jit(solution)/shard_map/ppermute | solution.py:546
  28.1 14.1 %collective-permute-start.3 = (f32[56,128]{1,0:T(8,128)S(1)}, f32[56,128]{1,0:T(8,128)S(1)}, u32[]{:S(2)}, u32[]{:S(2)}) collective-permute-start(f32[56,128]{1,0:T(8,128)S(1)} %get-tuple-element.63), channel_id=1, source_target_pairs={{0,16},{1,17},{2,18},{3,19},{4,20},{5,21},{6,22},{7,23},{8,24},{9,... | collective-permute-start | bytes 86024 | tf_op jit(solution)/shard_map/ppermute | solution.py:546
  42.2 54.7 %copy-start.5 = (bf16[256,256]{1,0:T(8,128)(2,1)S(1)}, bf16[256,256]{1,0:T(8,128)(2,1)}, u32[]{:S(2)}) copy-start(bf16[256,256]{1,0:T(8,128)(2,1)} %constant.103.clone.refs_5_.refs_6_) | copy-start | bytes 393220
  42.2 54.7 %copy-start.6 = (bf16[256,256]{1,0:T(8,128)(2,1)S(1)}, bf16[256,256]{1,0:T(8,128)(2,1)}, u32[]{:S(2)}) copy-start(bf16[256,256]{1,0:T(8,128)(2,1)} %constant.104.clone.refs_6_.refs_7_) | copy-start | bytes 393220
  42.2 54.7 %copy-start.13 = (bf16[128,144]{1,0:T(8,128)(2,1)S(1)}, bf16[128,144]{1,0:T(8,128)(2,1)}, u32[]{:S(2)}) copy-start(bf16[128,144]{1,0:T(8,128)(2,1)} %constant.105.clone.refs_7_.refs_8_) | copy-start | bytes 110596
  42.2 54.7 %copy-start.14 = (bf16[128,144]{1,0:T(8,128)(2,1)S(1)}, bf16[128,144]{1,0:T(8,128)(2,1)}, u32[]{:S(2)}) copy-start(bf16[128,144]{1,0:T(8,128)(2,1)} %constant.106.clone.refs_8_.refs_9_) | copy-start | bytes 110596
  42.3 54.7 %copy-start.15 = (bf16[128,256]{1,0:T(8,128)(2,1)S(1)}, bf16[128,256]{1,0:T(8,128)(2,1)}, u32[]{:S(2)}) copy-start(bf16[128,256]{1,0:T(8,128)(2,1)} %constant.107.clone.refs_9_.refs_10_) | copy-start | bytes 196612
  42.3 54.7 %copy-start.16 = (bf16[128,256]{1,0:T(8,128)(2,1)S(1)}, bf16[128,256]{1,0:T(8,128)(2,1)}, u32[]{:S(2)}) copy-start(bf16[128,256]{1,0:T(8,128)(2,1)} %constant.108.clone.refs_10_.refs_11_) | copy-start | bytes 196612
  42.3 54.7 %copy-start.17 = (bf16[256,128]{1,0:T(8,128)(2,1)S(1)}, bf16[256,128]{1,0:T(8,128)(2,1)}, u32[]{:S(2)}) copy-start(bf16[256,128]{1,0:T(8,128)(2,1)} %constant.109.clone.refs_11_.refs_12_) | copy-start | bytes 196612
  42.3 54.7 %copy-start.18 = (bf16[256,128]{1,0:T(8,128)(2,1)S(1)}, bf16[256,128]{1,0:T(8,128)(2,1)}, u32[]{:S(2)}) copy-start(bf16[256,128]{1,0:T(8,128)(2,1)} %constant.110.clone.refs_12_.refs_13_) | copy-start | bytes 196612
  42.3 54.7 %copy-start.23 = (bf16[128,128]{1,0:T(8,128)(2,1)S(1)}, bf16[128,128]{1,0:T(8,128)(2,1)}, u32[]{:S(2)}) copy-start(bf16[128,128]{1,0:T(8,128)(2,1)} %constant.111.clone.refs_13_.refs_14_) | copy-start | bytes 98308
  42.3 54.7 %copy-start.24 = (bf16[128,128]{1,0:T(8,128)(2,1)S(1)}, bf16[128,128]{1,0:T(8,128)(2,1)}, u32[]{:S(2)}) copy-start(bf16[128,128]{1,0:T(8,128)(2,1)} %constant.112.clone.refs_14_.refs_15_) | copy-start | bytes 98308
  43.8 11.8 %collective-permute-start.4 = (f32[544,128]{1,0:T(8,128)S(1)}, f32[544,128]{1,0:T(8,128)S(1)}, u32[]{:S(2)}, u32[]{:S(2)}) collective-permute-start(f32[544,128]{1,0:T(8,128)S(1)} %get-tuple-element.65), channel_id=1, source_target_pairs={{0,1},{1,2},{2,3},{3,4},{4,5},{5,6},{6,7},{7,0},{8,9},{9,10},{10,1... | collective-permute-start | bytes 835592 | tf_op jit(solution)/shard_map/ppermute | solution.py:546
  45.8 9.3 %collective-permute-start.5 = (f32[536,128]{1,0:T(8,128)S(1)}, f32[536,128]{1,0:T(8,128)S(1)}, u32[]{:S(2)}, u32[]{:S(2)}) collective-permute-start(f32[536,128]{1,0:T(8,128)S(1)} %get-tuple-element.66), channel_id=1, source_target_pairs={{0,7},{1,0},{2,1},{3,2},{4,3},{5,4},{6,5},{7,6},{8,15},{9,8},{10,9... | collective-permute-start | bytes 823304 | tf_op jit(solution)/shard_map/ppermute | solution.py:546
  55.7 10.6 %collective-permute-start.6 = (f32[216,128]{1,0:T(8,128)S(1)}, f32[216,128]{1,0:T(8,128)S(1)}, u32[]{:S(2)}, u32[]{:S(2)}) collective-permute-start(f32[216,128]{1,0:T(8,128)S(1)} %get-tuple-element.67), channel_id=1, source_target_pairs={{0,3},{1,4},{2,5},{3,6},{4,7},{5,0},{6,1},{7,2},{8,11},{9,12},{10,... | collective-permute-start | bytes 331784 | tf_op jit(solution)/shard_map/ppermute | solution.py:546
  60.3 10.8 %collective-permute-start.7 = (f32[216,128]{1,0:T(8,128)S(1)}, f32[216,128]{1,0:T(8,128)S(1)}, u32[]{:S(2)}, u32[]{:S(2)}) collective-permute-start(f32[216,128]{1,0:T(8,128)S(1)} %get-tuple-element.68), channel_id=1, source_target_pairs={{0,5},{1,6},{2,7},{3,0},{4,1},{5,2},{6,3},{7,4},{8,13},{9,14},{10,... | collective-permute-start | bytes 331784 | tf_op jit(solution)/shard_map/ppermute | solution.py:546
  71.1 7.0 %collective-permute-start.8 = (f32[144,128]{1,0:T(8,128)S(1)}, f32[144,128]{1,0:T(8,128)S(1)}, u32[]{:S(2)}, u32[]{:S(2)}) collective-permute-start(f32[144,128]{1,0:T(8,128)S(1)} %objects.1.own), channel_id=1, source_target_pairs={{0,5},{1,6},{2,7},{3,0},{4,1},{5,2},{6,3},{7,4},{8,13},{9,14},{10,... | collective-permute-start | bytes 221192 | tf_op jit(solution)/shard_map/ppermute | solution.py:546
  71.2 8.1 %collective-permute-start.9 = (f32[144,128]{1,0:T(8,128)S(1)}, f32[144,128]{1,0:T(8,128)S(1)}, u32[]{:S(2)}, u32[]{:S(2)}) collective-permute-start(f32[144,128]{1,0:T(8,128)S(1)} %objects.1.own), channel_id=1, source_target_pairs={{0,3},{1,4},{2,5},{3,6},{4,7},{5,0},{6,1},{7,2},{8,11},{9,12},{10,... | collective-permute-start | bytes 221192 | tf_op jit(solution)/shard_map/ppermute | solution.py:546
  79.4 6.8 %collective-permute-start.10 = (f32[360,128]{1,0:T(8,128)S(1)}, f32[360,128]{1,0:T(8,128)S(1)}, u32[]{:S(2)}, u32[]{:S(2)}) collective-permute-start(f32[360,128]{1,0:T(8,128)S(1)} %get-tuple-element.86), channel_id=1, source_target_pairs={{0,1},{1,2},{2,3},{3,4},{4,5},{5,6},{6,7},{7,0},{8,9},{9,10},{10,1... | collective-permute-start | bytes 552968 | tf_op jit(solution)/shard_map/ppermute | solution.py:546
  81.0 5.5 %collective-permute-start.11 = (f32[360,128]{1,0:T(8,128)S(1)}, f32[360,128]{1,0:T(8,128)S(1)}, u32[]{:S(2)}, u32[]{:S(2)}) collective-permute-start(f32[360,128]{1,0:T(8,128)S(1)} %get-tuple-element.85), channel_id=1, source_target_pairs={{0,7},{1,0},{2,1},{3,2},{4,3},{5,4},{6,5},{7,6},{8,15},{9,8},{10,9... | collective-permute-start | bytes 552968 | tf_op jit(solution)/shard_map/ppermute | solution.py:546
  87.3 7.8 %collective-permute-start.15 = (f32[64,128]{1,0:T(8,128)S(1)}, f32[64,128]{1,0:T(8,128)S(1)}, u32[]{:S(2)}, u32[]{:S(2)}) collective-permute-start(f32[64,128]{1,0:T(8,128)S(1)} %get-tuple-element.78), channel_id=1, source_target_pairs={{0,8},{1,9},{2,10},{3,11},{4,12},{5,13},{6,14},{7,15},{8,16},{9,17... | collective-permute-start | bytes 98312 | tf_op jit(solution)/shard_map/ppermute | solution.py:546
  89.3 7.6 %collective-permute-start.16 = (f32[64,128]{1,0:T(8,128)S(1)}, f32[64,128]{1,0:T(8,128)S(1)}, u32[]{:S(2)}, u32[]{:S(2)}) collective-permute-start(f32[64,128]{1,0:T(8,128)S(1)} %get-tuple-element.79), channel_id=1, source_target_pairs={{0,16},{1,17},{2,18},{3,19},{4,20},{5,21},{6,22},{7,23},{8,24},{9,... | collective-permute-start | bytes 98312 | tf_op jit(solution)/shard_map/ppermute | solution.py:546
  92.2 4.7 %collective-permute-start.17 = (f32[64,128]{1,0:T(8,128)S(1)}, f32[64,128]{1,0:T(8,128)S(1)}, u32[]{:S(2)}, u32[]{:S(2)}) collective-permute-start(f32[64,128]{1,0:T(8,128)S(1)} %get-tuple-element.80), channel_id=1, source_target_pairs={{0,24},{1,25},{2,26},{3,27},{4,28},{5,29},{6,30},{7,31},{8,0},{9,1... | collective-permute-start | bytes 98312 | tf_op jit(solution)/shard_map/ppermute | solution.py:546
  93.6 10.6 %collective-permute-start.12 = (f32[512,128]{1,0:T(8,128)S(1)}, f32[512,128]{1,0:T(8,128)S(1)}, u32[]{:S(2)}, u32[]{:S(2)}) collective-permute-start(f32[512,128]{1,0:T(8,128)S(1)} %get-tuple-element.70), channel_id=1, source_target_pairs={{0,8},{1,9},{2,10},{3,11},{4,12},{5,13},{6,14},{7,15},{8,16},{9,17... | collective-permute-start | bytes 786440 | tf_op jit(solution)/shard_map/ppermute | solution.py:546
  94.3 9.8 %collective-permute-start.13 = (f32[512,128]{1,0:T(8,128)S(1)}, f32[512,128]{1,0:T(8,128)S(1)}, u32[]{:S(2)}, u32[]{:S(2)}) collective-permute-start(f32[512,128]{1,0:T(8,128)S(1)} %get-tuple-element.71), channel_id=1, source_target_pairs={{0,16},{1,17},{2,18},{3,19},{4,20},{5,21},{6,22},{7,23},{8,24},{9,... | collective-permute-start | bytes 786440 | tf_op jit(solution)/shard_map/ppermute | solution.py:546
  95.0 9.8 %collective-permute-start.14 = (f32[512,128]{1,0:T(8,128)S(1)}, f32[512,128]{1,0:T(8,128)S(1)}, u32[]{:S(2)}, u32[]{:S(2)}) collective-permute-start(f32[512,128]{1,0:T(8,128)S(1)} %get-tuple-element.72), channel_id=1, source_target_pairs={{0,24},{1,25},{2,26},{3,27},{4,28},{5,29},{6,30},{7,31},{8,0},{9,1... | collective-permute-start | bytes 786440 | tf_op jit(solution)/shard_map/ppermute | solution.py:546
  (13 other events, 16.9 us)
